TPU v7x, 32 devices: a whole 2x2x4 slice. The times are simulated.
32 devices in a mesh: fsdp: 4 (over y, core), seq: 8 (over z, x).
Axes of the slice: x: 2, y: 2, z: 4, core: 2. Of those that a mesh axis runs over, the one named last changes fastest.
Arguments:
- tokens: bfloat16 [3, 4, 1024, 1024], P(None, 'fsdp', 'seq'), may hold values from -6 to 6
- scene_ids: int32 [3, 4, 1024], P(None, 'fsdp'), may hold values from 0 to 4, as said below
- valid_mask: int32 [3, 4, 1024], P(None, 'fsdp'), may hold values 0 or 1
- norm_gain: bfloat16 [1024], P(('fsdp', 'seq')), may hold values from 0.099609375 to 1.8984375
- w_in: bfloat16 [1024, 4384], P(('fsdp', 'seq')), may hold values from -0.1875 to 0.1875
- conv_w: bfloat16 [4, 2304], P(None, ('fsdp', 'seq')), may hold values from -3 to 3
- conv_b: bfloat16 [2304], P(('fsdp', 'seq')), may hold values from -0.5 to 0.5
- dt_bias: float32 [32], P('seq'), may hold values from -5 to -1
- a_log: float32 [32], P('seq'), may hold values from -7 to 1
- d_skip: float32 [32], P('seq'), may hold values from 0.5 to 1.5
- gate_gain: bfloat16 [2048], P(('fsdp', 'seq')), may hold values from 0.099609375 to 1.8984375
- w_out: bfloat16 [2048, 1024], P(('fsdp', 'seq')), may hold values from -0.125 to 0.125
- d_out: bfloat16 [3, 4, 1024, 1024], P(None, 'fsdp', 'seq'), may hold values from -6 to 6
Outputs:
- block_out: bfloat16 [3, 4, 1024, 1024], P(None, 'fsdp', 'seq')
- grad_in: bfloat16 [3, 4, 1024, 1024], P(None, 'fsdp', 'seq')
- grad_norm_gain: float32 [1024], P(('fsdp', 'seq'))
- grad_w_in: float32 [1024, 4384], P(('fsdp', 'seq'))
- grad_conv_w: float32 [4, 2304], P(None, ('fsdp', 'seq'))
- grad_conv_b: float32 [2304], P(('fsdp', 'seq'))
- grad_dt_bias: float32 [32], P('seq')
- grad_a_log: float32 [32], P('seq')
- grad_d_skip: float32 [32], P('seq')
- grad_gate_gain: float32 [2048], P(('fsdp', 'seq'))
- grad_w_out: float32 [2048, 1024], P(('fsdp', 'seq'))
Inputs may be any that keep to these rules, and one draw needn't show every extreme that they name: `scene_ids`: in each packed sequence scene numbers start at 0 and rise by one at each of four scene starts. Counting positions from 0: scene 1 starts at a position of 1 or more, before scene 2; scene 2 starts at a position from 2 to 64; scene 3 starts at a position from 960 to 1022; scene 4 starts after scene 3, at 1023 at the latest.
All inputs are finite; a program needn't handle non-finite values. No bound on the sum of `valid_mask` on one device may be relied on, other than what follows from the above.
Results may differ from a plain program's by a relative error of at most 0.013.
Values may be sent and summed in bfloat16 or wider, within the bound.
No kernel may reach another device: no remote copies, remote signals or barrier semaphores. Data moves between devices by JAX's collectives and lax.ppermute only.
A program may use at most 192 MiB of HBM per device.

v0:
```python
import jax
import jax.numpy as jnp
from jax import lax
from jax.sharding import PartitionSpec as P

H = 32
P_SIZE = 64
N = 128
KERNEL = 4
SPAN = 256
MB = 3


epsilon = 1e-05


def shifted(block, axis, distance):
    devices = range(lax.axis_size(axis))
    route = [(i - distance, i) for i in devices if i - distance in devices]
    return lax.ppermute(block, axis, route)


def causal_conv(extended, ext_ids, conv_kernel, conv_bias):
    length = extended.shape[0] - KERNEL + 1
    own_ids = ext_ids[KERNEL - 1 :]
    summed = jnp.zeros((length, extended.shape[1]), jnp.float32) + conv_bias
    for offset in range(KERNEL):
        same_scene = (ext_ids[offset : offset + length] == own_ids).astype(jnp.float32)
        summed = (
            summed + conv_kernel[offset] * extended[offset : offset + length] * same_scene[:, None]
        )
    return summed


def state_scan(values, b_part, c_part, step_size, a_log, d_skip, scene_row):
    length, head_count, head_dim = values.shape
    state_dim = b_part.shape[1]
    blocks = length // SPAN
    decay_rate = jnp.exp(a_log)
    block_ids = scene_row.reshape(blocks, SPAN)
    before = jnp.concatenate([jnp.full((1,), -1, jnp.int32), block_ids[:-1, -1]])
    lower_mask = lax.broadcasted_iota(jnp.int32, (SPAN, SPAN), 0) >= lax.broadcasted_iota(
        jnp.int32, (SPAN, SPAN), 1
    )
    three_pass = lax.Precision.HIGH

    def span_step(carried, span_item):
        span_x, span_b, span_c, span_dt, span_ids, prior_id = span_item
        log_decay = -span_dt * decay_rate
        cumulative = jnp.cumsum(log_decay, axis=0).T
        same_scene = lower_mask & (span_ids[:, None] == span_ids[None, :])
        log_ratio = cumulative[:, :, None] - cumulative[:, None, :]
        decay_in = jnp.exp(jnp.where(same_scene[None], log_ratio, -jnp.inf))
        intersection = jnp.dot(span_c, span_b.T, precision=three_pass)
        scaled = span_x * span_dt[:, :, None]
        inside = jnp.einsum(
            "hts,shp->thp", decay_in * intersection[None], scaled, precision=three_pass
        )
        carry_in = (span_ids == prior_id).astype(jnp.float32)
        reach_in = jnp.exp(cumulative) * carry_in[None, :]
        from_state = (
            jnp.einsum("tn,hpn->thp", span_c, carried, precision=three_pass)
            * reach_in.T[:, :, None]
        )
        tail_mask = span_ids == span_ids[-1]
        weight_end = jnp.exp(
            jnp.where(tail_mask[None, :], cumulative[:, -1:] - cumulative, -jnp.inf)
        )
        fresh_state = jnp.einsum("hs,shp,sn->hpn", weight_end, scaled, span_b, precision=three_pass)
        carried = carried * (jnp.exp(cumulative[:, -1]) * carry_in[-1])[:, None, None] + fresh_state
        block_out = inside + from_state + d_skip[None, :, None] * span_x
        return (carried, block_out)

    initial = jnp.zeros((head_count, head_dim, state_dim), jnp.float32)
    _, outputs = lax.scan(
        jax.checkpoint(span_step),
        initial,
        (
            values.reshape(blocks, SPAN, head_count, head_dim),
            b_part.reshape(blocks, SPAN, state_dim),
            c_part.reshape(blocks, SPAN, state_dim),
            step_size.reshape(blocks, SPAN, head_count),
            block_ids,
            before,
        ),
    )
    return outputs.reshape(length, head_count, head_dim)


def body(
    tokens,
    scene_ids,
    valid_mask,
    norm_gain,
    w_in,
    conv_w,
    conv_b,
    dt_bias,
    a_log,
    d_skip,
    gate_gain,
    w_out,
    d_out,
):
    tok_rows = tokens.shape[2]
    seq_rank = lax.axis_index("seq")
    inner_width = H * P_SIZE
    rim_rows = KERNEL - 1
    conv_width = inner_width + 2 * N
    results = []
    input_grads = []
    sum_shift = jnp.zeros_like(dt_bias)
    sum_logrates = jnp.zeros_like(a_log)
    sum_skips = jnp.zeros_like(d_skip)
    for micro_index in range(MB):
        gathered = (
            lax.all_gather(w_in, ("fsdp", "seq"), axis=0, tiled=True),
            lax.all_gather(w_out, ("fsdp", "seq"), axis=0, tiled=True),
            lax.all_gather(conv_w, ("fsdp", "seq"), axis=1, tiled=True),
            lax.all_gather(conv_b, ("fsdp", "seq"), axis=0, tiled=True),
            lax.all_gather(norm_gain, ("fsdp", "seq"), axis=0, tiled=True),
            lax.all_gather(gate_gain, ("fsdp", "seq"), axis=0, tiled=True),
        )
        win_full, wout_full, kernel_full, bias_full, gain_first, gain_second = gathered
        conv_kernel = kernel_full.astype(jnp.float32)
        conv_bias = bias_full.astype(jnp.float32)
        gain_in = gain_first.astype(jnp.float32)
        gain_out = gain_second.astype(jnp.float32)
        inputs = tokens[micro_index, 0].astype(jnp.float32)
        in_scale = lax.rsqrt(jnp.mean(inputs * inputs, axis=-1, keepdims=True) + epsilon)
        unit_in = inputs * in_scale
        normed = (unit_in * gain_in).astype(jnp.bfloat16)
        projected = jnp.dot(normed, win_full, preferred_element_type=jnp.float32)
        gate_in = projected[:, :inner_width]
        conv_in = projected[:, inner_width : 2 * inner_width + 2 * N]
        step_raw = projected[:, 2 * inner_width + 2 * N :]
        scene_row = scene_ids[micro_index, 0]
        valid_row = valid_mask[micro_index, 0].astype(jnp.float32)
        padded_ids = jnp.concatenate([jnp.full((rim_rows,), -1, jnp.int32), scene_row])
        ext_ids = lax.dynamic_slice_in_dim(padded_ids, seq_rank * tok_rows, tok_rows + rim_rows)
        rim_block = shifted(conv_in[tok_rows - rim_rows :], "seq", 1)
        extended = jnp.concatenate([rim_block, conv_in], axis=0)
        conv_pre = causal_conv(extended, ext_ids, conv_kernel, conv_bias)
        activated = jax.nn.silu(conv_pre)
        x_low = activated[:, :inner_width].astype(jnp.bfloat16)
        bc_low = activated[:, inner_width:].astype(jnp.bfloat16)
        step_low = step_raw.astype(jnp.bfloat16)
        x_heads, step_heads = (
            lax.all_to_all(
                x_low.reshape(tok_rows, H, P_SIZE), "seq", split_axis=1, concat_axis=0, tiled=True
            ),
            lax.all_to_all(step_low, "seq", split_axis=1, concat_axis=0, tiled=True),
        )
        bc_all = lax.all_gather(bc_low, "seq", axis=0, tiled=True)

        def local_scan(values, bc_vals, step_vals, dt_shift, logrates, skip_gain):
            step_size = jax.nn.softplus(step_vals + dt_shift) * valid_row[:, None]
            return state_scan(
                values, bc_vals[:, :N], bc_vals[:, N:], step_size, logrates, skip_gain, scene_row
            )

        scanned, pullback = jax.vjp(
            local_scan,
            x_heads.astype(jnp.float32),
            bc_all.astype(jnp.float32),
            step_heads.astype(jnp.float32),
            dt_bias,
            a_log,
            d_skip,
        )
        mixed_heads = lax.all_to_all(
            scanned.astype(jnp.bfloat16), "seq", split_axis=0, concat_axis=1, tiled=True
        )
        mixed_out = mixed_heads.reshape(tok_rows, inner_width).astype(jnp.float32)
        gate_act = jax.nn.silu(gate_in)
        gated_out = mixed_out * gate_act
        out_scale = lax.rsqrt(jnp.mean(gated_out * gated_out, axis=-1, keepdims=True) + epsilon)
        unit_out = gated_out * out_scale
        normed_out = (unit_out * gain_out).astype(jnp.bfloat16)
        result = inputs + jnp.dot(normed_out, wout_full, preferred_element_type=jnp.float32)
        results.append(result.astype(jnp.bfloat16))
        upstream = d_out[micro_index, 0]
        grad_wout = jnp.dot(normed_out.T, upstream, preferred_element_type=jnp.float32)
        grad_normed_out = jnp.dot(upstream, wout_full.T, preferred_element_type=jnp.float32)
        grad_gain_out = jnp.sum(grad_normed_out * unit_out, axis=0)
        grad_unit_out = grad_normed_out * gain_out
        grad_gated = out_scale * (
            grad_unit_out - unit_out * jnp.mean(grad_unit_out * unit_out, axis=-1, keepdims=True)
        )
        grad_mixed = grad_gated * gate_act
        sigmoid_gate = jax.nn.sigmoid(gate_in)
        grad_gate_in = (
            grad_gated * mixed_out * sigmoid_gate * (1.0 + gate_in * (1.0 - sigmoid_gate))
        )
        grad_heads = lax.all_to_all(
            grad_mixed.astype(jnp.bfloat16).reshape(tok_rows, H, P_SIZE),
            "seq",
            split_axis=1,
            concat_axis=0,
            tiled=True,
        )
        grad_values, grad_bc, grad_steps, grad_shift, grad_logrates, grad_skips = pullback(
            grad_heads.astype(jnp.float32)
        )
        sum_shift = sum_shift + grad_shift
        sum_logrates = sum_logrates + grad_logrates
        sum_skips = sum_skips + grad_skips
        back_x, back_steps = (
            lax.all_to_all(
                grad_values.astype(jnp.bfloat16), "seq", split_axis=0, concat_axis=1, tiled=True
            ),
            lax.all_to_all(
                grad_steps.astype(jnp.bfloat16), "seq", split_axis=0, concat_axis=1, tiled=True
            ),
        )
        back_bc = lax.psum_scatter(
            grad_bc.astype(jnp.bfloat16), "seq", scatter_dimension=0, tiled=True
        ).astype(jnp.float32)
        grad_act = jnp.concatenate(
            [back_x.reshape(tok_rows, inner_width).astype(jnp.float32), back_bc], axis=1
        )
        sigmoid_conv = jax.nn.sigmoid(conv_pre)
        grad_pre = grad_act * sigmoid_conv * (1.0 + conv_pre * (1.0 - sigmoid_conv))
        grad_bias = jnp.sum(grad_pre, axis=0)
        own_ids = ext_ids[rim_rows:]
        grad_ext = jnp.zeros((tok_rows + rim_rows, conv_width), jnp.float32)
        kernel_rows = []
        for offset in range(KERNEL):
            same_scene = (ext_ids[offset : offset + tok_rows] == own_ids).astype(jnp.float32)[
                :, None
            ]
            masked = grad_pre * same_scene
            kernel_rows.append(jnp.sum(masked * extended[offset : offset + tok_rows], axis=0))
            grad_ext = grad_ext.at[offset : offset + tok_rows].add(masked * conv_kernel[offset])
        grad_kernel = jnp.stack(kernel_rows)
        rim_back = shifted(grad_ext[:rim_rows], "seq", -1)
        grad_conv_in = grad_ext[rim_rows:] + jnp.concatenate(
            [jnp.zeros((tok_rows - rim_rows, conv_width), jnp.float32), rim_back], axis=0
        )
        grad_projected = jnp.concatenate(
            [grad_gate_in, grad_conv_in, back_steps.astype(jnp.float32)], axis=1
        ).astype(jnp.bfloat16)
        grad_win = jnp.dot(normed.T, grad_projected, preferred_element_type=jnp.float32)
        grad_normed = jnp.dot(grad_projected, win_full.T, preferred_element_type=jnp.float32)
        grad_gain_in = jnp.sum(grad_normed * unit_in, axis=0)
        grad_unit_in = grad_normed * gain_in
        grad_inputs = upstream.astype(jnp.float32) + in_scale * (
            grad_unit_in - unit_in * jnp.mean(grad_unit_in * unit_in, axis=-1, keepdims=True)
        )
        input_grads.append(grad_inputs.astype(jnp.bfloat16))
        local_grads = (grad_win, grad_wout, grad_kernel, grad_bias, grad_gain_in, grad_gain_out)
        if micro_index == 0:
            full_totals = local_grads
        else:
            full_totals = tuple((first + second for first, second in zip(full_totals, local_grads)))
    total_win, total_wout, total_kernel, total_bias, total_gain_in, total_gain_out = full_totals
    shard_totals = (
        lax.psum_scatter(total_win, ("fsdp", "seq"), scatter_dimension=0, tiled=True),
        lax.psum_scatter(total_wout, ("fsdp", "seq"), scatter_dimension=0, tiled=True),
        lax.psum_scatter(total_kernel, ("fsdp", "seq"), scatter_dimension=1, tiled=True),
        lax.psum_scatter(total_bias, ("fsdp", "seq"), scatter_dimension=0, tiled=True),
        lax.psum_scatter(total_gain_in, ("fsdp", "seq"), scatter_dimension=0, tiled=True),
        lax.psum_scatter(total_gain_out, ("fsdp", "seq"), scatter_dimension=0, tiled=True),
    )
    shard_win, shard_wout, shard_kernel, shard_bias, shard_gain_in, shard_gain_out = shard_totals
    head_shift, head_logrates, head_skips = lax.psum((sum_shift, sum_logrates, sum_skips), "fsdp")
    block_out = jnp.stack(results)[:, None]
    grad_in = jnp.stack(input_grads)[:, None]
    return (
        block_out,
        grad_in,
        shard_gain_in,
        shard_win,
        shard_kernel,
        shard_bias,
        head_shift,
        head_logrates,
        head_skips,
        shard_gain_out,
        shard_wout,
    )


def solution(mesh):
    placed = (
        P(None, "fsdp", "seq", None),
        P(None, "fsdp", None),
        P(None, "fsdp", None),
        P(("fsdp", "seq")),
        P(("fsdp", "seq"), None),
        P(None, ("fsdp", "seq")),
        P(("fsdp", "seq")),
        P("seq"),
        P("seq"),
        P("seq"),
        P(("fsdp", "seq")),
        P(("fsdp", "seq"), None),
        P(None, "fsdp", "seq", None),
    )
    return jax.shard_map(
        body,
        mesh=mesh,
        in_specs=placed,
        out_specs=(
            P(None, "fsdp", "seq", None),
            P(None, "fsdp", "seq", None),
            P(("fsdp", "seq")),
            P(("fsdp", "seq"), None),
            P(None, ("fsdp", "seq")),
            P(("fsdp", "seq")),
            P("seq"),
            P("seq"),
            P("seq"),
            P(("fsdp", "seq")),
            P(("fsdp", "seq"), None),
        ),
        check_vma=False,
    )
```

profile of v0, /device:TPU:0, one launch (start us, length us, event | category | flops | bytes accessed | tf_op | source)
XLA Modules:
  0.0 1941.1 jit_solution(16383021504470873206)
XLA Ops:
  10.9 42.9 %all-reduce.30 = (bf16[1024]{0:T(1024)(128)(2,1)S(1)}, bf16[2304]{0:T(1024)(128)(2,1)}, bf16[2048]{0:T(1024)(128)(2,1)}) all-reduce(bf16[1024]{0:T(1024)(128)(2,1)S(1)} %dynamic-update-slice.36, bf16[2304]{0:T(1024)(128)(2,1)S(1)} %dynamic-update-slice.37, ...), channel_id=1, replica_groups=mesh['fsdp'=4,'seq'=8] {'fsdp','seq'}, use_global_device_ids=true, to_apply=%add.21 | all-reduce | flops 5376 | bytes 21504
  57.7 66.4 %all-gather = bf16[32,72,4]{1,2,0:T(4,128)(2,1)S(1)} all-gather(bf16[1,72,4]{1,2,0:T(4,128)(2,1)S(1)} %bitcast.1436), channel_id=1, replica_groups=mesh['fsdp'=4,'seq'=8] {'fsdp','seq'}, dimensions={0}, use_global_device_ids=true | all-gather | bytes 19008 | tf_op jit(solution)/shard_map/all_gather | solution.py:119
  183.5 30.6 %all_gather.43 = bf16[1024,256]{0,1:T(8,128)(2,1)S(1)} all-gather(bf16[128,256]{0,1:T(8,128)(2,1)S(1)} %slice.898), channel_id=1, replica_groups=mesh['fsdp'=4,'seq'=8] {'seq'}, dimensions={0}, use_global_device_ids=true | all-gather | bytes 589824 | tf_op jit(solution)/shard_map/all_gather | solution.py:154
  218.6 57.2 %while.141 = (s32[]{:T(128)}, f32[4,64,128]{2,1,0:T(8,128)S(1)}, bf16[4,256,4,64]{1,3,2,0:T(8,128)(2,1)S(1)}, f32[4,4,64,128]{3,2,1,0:T(8,128)}, f32[4,256,4]{1,...) while((s32[]{:T(128)}, f32[4,64,128]{2,1,0:T(8,128)S(1)}, ...), condition=%wide.region_4.6_spmd.clone, body=%wide.region_1.5_spmd.clone.sunk | while | flops 253401104 | bytes 3503594 | solution.py:75
  281.5 10.2 all-to-all-done.2
  306.6 9.8 all-to-all-done.9
  321.9 152.2 %while.144 = (s32[]{:T(128)}, f32[4]{0:T(128)}, f32[4]{0:T(128)}, f32[4,64,128]{2,1,0:T(8,128)}, bf16[4,256,4,64]{1,3,2,0:T(8,128)(2,1)}, /*index=5*/f32[4,256,1...) while((s32[]{:T(128)}, f32[4]{0:T(128)}, f32[4]{0:T(128)}, ...), condition=%wide.region_33.35_spmd.clone, body=%wide.region_19.34_spmd.clone.sunk | while | flops 609016576 | bytes 14558553 | solution.py:75
  498.6 38.9 %reduce-scatter.17.cloned.1.call-done = bf16[128,256]{1,0:T(8,128)(2,1)} async-done(((bf16[1024,256]{1,0:T(8,128)(2,1)}), bf16[128,256]{1,0:T(8,128)(2,1)}) %reduce-scatter.17.cloned.1.call-update) | async-done | bytes 65552
  550.5 8.3 scatter-add.31
  558.9 8.6 multiply_convert_fusion
  575.4 31.1 %all_gather.47 = bf16[1024,256]{0,1:T(8,128)(2,1)S(1)} all-gather(bf16[128,256]{0,1:T(8,128)(2,1)S(1)} %slice.924), channel_id=1, replica_groups=mesh['fsdp'=4,'seq'=8] {'seq'}, dimensions={0}, use_global_device_ids=true | all-gather | bytes 589824 | tf_op jit(solution)/shard_map/all_gather | solution.py:154
  615.0 57.2 %while.143 = (s32[]{:T(128)}, f32[4,64,128]{2,1,0:T(8,128)S(1)}, bf16[4,256,4,64]{1,3,2,0:T(8,128)(2,1)S(1)}, f32[4,4,64,128]{3,2,1,0:T(8,128)}, f32[4,256,4]{1,...) while((s32[]{:T(128)}, f32[4,64,128]{2,1,0:T(8,128)S(1)}, ...), condition=%wide.region_16.18_spmd.clone, body=%wide.region_13.17_spmd.clone.sunk | while | flops 253401104 | bytes 3503594 | solution.py:75
  676.0 14.7 all_to_all.186
  707.1 10.2 all-to-all-done.15
  722.7 151.7 %while.146 = (s32[]{:T(128)}, f32[4]{0:T(128)}, f32[4]{0:T(128)}, f32[4,64,128]{2,1,0:T(8,128)}, bf16[4,256,4,64]{1,3,2,0:T(8,128)(2,1)}, /*index=5*/f32[4,256,1...) while((s32[]{:T(128)}, f32[4]{0:T(128)}, f32[4]{0:T(128)}, ...), condition=%wide.region_69.71_spmd.clone, body=%wide.region_55.70_spmd.clone.sunk | while | flops 609016576 | bytes 14558553 | solution.py:75
  891.6 8.2 scatter-add.34
  912.8 25.9 %reduce-scatter.21.cloned.1.call-done = bf16[128,256]{1,0:T(8,128)(2,1)} async-done(((bf16[1024,256]{1,0:T(8,128)(2,1)}), bf16[128,256]{1,0:T(8,128)(2,1)}) %reduce-scatter.21.cloned.1.call-update) | async-done | bytes 65552
  951.4 8.3 scatter-add.41
  959.8 10.6 multiply_convert_fusion.1
  974.7 34.7 %all_gather.46 = bf16[1024,256]{0,1:T(8,128)(2,1)S(1)} all-gather(bf16[128,256]{0,1:T(8,128)(2,1)S(1)} %slice.911), channel_id=1, replica_groups=mesh['fsdp'=4,'seq'=8] {'seq'}, dimensions={0}, use_global_device_ids=true | all-gather | bytes 589824 | tf_op jit(solution)/shard_map/all_gather | solution.py:154
  1018.7 59.8 %while.142 = (s32[]{:T(128)}, f32[4,64,128]{2,1,0:T(8,128)S(1)}, bf16[4,256,4,64]{1,3,2,0:T(8,128)(2,1)}, f32[4,4,64,128]{3,2,1,0:T(8,128)}, f32[4,256,4]{1,2,0:...) while((s32[]{:T(128)}, f32[4,64,128]{2,1,0:T(8,128)S(1)}, ...), condition=%wide.region_10.12_spmd.clone, body=%wide.region_7.11_spmd.clone.sunk | while | flops 253401104 | bytes 3503594 | solution.py:75
  1081.8 14.5 all_to_all.187
  1127.5 155.2 %while.145 = (s32[]{:T(128)}, f32[4]{0:T(128)}, f32[4]{0:T(128)}, f32[4,64,128]{2,1,0:T(8,128)}, bf16[4,256,4,64]{1,3,2,0:T(8,128)(2,1)}, /*index=5*/f32[4,256,1...) while((s32[]{:T(128)}, f32[4]{0:T(128)}, f32[4]{0:T(128)}, ...), condition=%wide.region_51.53_spmd.clone, body=%wide.region_37.52_spmd.clone.sunk | while | flops 609016576 | bytes 14558553 | solution.py:75
  1307.1 8.3 scatter-add.44
  1340.5 11.4 reduce-scatter.19.cloned.1.call-done
  1364.1 8.3 scatter-add.36
  1376.1 8.3 scatter-add.39
  1395.7 10.3 fusion.333
  1420.0 10.3 fusion.331
  1430.3 21.1 %add_add_fusion = f32[1024,4384]{1,0:T(8,128)} fusion(f32[1024,4384]{1,0:T(8,128)} %fusion.333, f32[1024,4384]{1,0:T(8,128)} %fusion.331, bf16[128,32]{0,1:T(8,128)(2,1)S(1)} %bitcast.1431, bf16[128,2304]{0,1:T(8,128)(2,1)} %get-tuple-element.2985, bf16[128,2048]{0,1:T(8,128)(2,1)} %get-tuple-element.2970, f32[128]{0:T(128)S(1)} %copy-done.149, ...), kind=kOutput, calls=%fused_computation.441 | convolution fusion | flops 1162108928 | bytes 56046080 | tf_op jit(solution)/shard_map/dot_general | solution.py:243
  1485.6 47.2 %all-reduce.28 = (f32[1024]{0:T(1024)S(1)}, f32[4,2304]{1,0:T(4,128)S(1)}, f32[2304]{0:T(1024)S(1)}, f32[2048]{0:T(1024)S(1)}) all-reduce(f32[1024]{0:T(1024)S(1)} %add_add_fusion.4, f32[4,2304]{1,0:T(4,128)S(1)} %fusion.364, f32[2304]{0:T(1024)S(1)} %add_add_fusion.2, ...), channel_id=5, replica_groups=mesh['fsdp'=4,'seq'=8] {'fsdp','seq'}, use_global_device_ids=true, to_apply=%region_75.77.clone | all-reduce | flops 14592 | bytes 116736
  1539.8 394.2 %reduce-scatter.13.cloned.1.call-done = f32[32,4384]{1,0:T(8,128)} async-done(((f32[1024,4384]{1,0:T(8,128)}), f32[32,4384]{1,0:T(8,128)}) %reduce-scatter.13.cloned.1.call-update) | async-done | bytes 561168 | tf_op jit(solution)/shard_map/reduce_scatter | solution.py:258
  (1654 shorter events, 1021.1 us)
Async XLA Ops:
  7.2 117.8 %copy-start.15 = (bf16[3,1,128,1024]{3,2,1,0:T(8,128)(2,1)S(1)}, bf16[3,1,128,1024]{3,2,1,0:T(8,128)(2,1)}, u32[]{:S(2)}) copy-start(bf16[3,1,128,1024]{3,2,1,0:T(8,128)(2,1)} %param.50) | copy-start | bytes 2359300
  7.3 117.8 %all-gather.4.cloned.1.call-start = ((), (), s32[]{:S(2)}) async-start(), calls=%async_computation.23 | async-start | bytes 9461760 | tf_op jit(solution)/shard_map/all_gather | solution.py:117
  8.0 287.2 %all-gather.6.cloned.1.call-start = ((), (), s32[]{:S(2)}) async-start(), calls=%async_computation.24 | async-start | bytes 4325376 | tf_op jit(solution)/shard_map/all_gather | solution.py:118
  10.1 135.8 %copy-start.112 = (f32[128]{0:T(128)}, f32[128]{0:T(128)S(1)}, u32[]{:S(2)}) copy-start(f32[128]{0:T(128)S(1)} %add_rsqrt_fusion.5) | copy-start | bytes 1540
  53.8 92.1 %copy-start.43 = (f32[1024]{0:T(1024)}, f32[1024]{0:T(1024)S(1)}, u32[]{:S(2)}) copy-start(f32[1024]{0:T(1024)S(1)} %convert_element_type.487) | copy-start | bytes 12292
  134.3 21.8 %all-to-all-start.6 = ((bf16[128,8,4]{0,2,1:T(4,128)(2,1)}), bf16[128,8,4]{0,2,1:T(4,128)(2,1)S(1)}, u32[]{:S(2)}, u32[]{:S(2)}) async-start(bf16[128,8,4]{0,2,1:T(4,128)(2,1)} %bitcast.43), calls=%async_computation.6 | async-start | bytes 16384 | tf_op jit(solution)/shard_map/all_to_all | solution.py:152
  151.7 11.1 collective-permute-start
  156.1 10.5 all-to-all-start.3
  166.6 10.3 all-to-all-start
  176.9 39.4 %all-to-all-start.1 = ((bf16[128,32,64]{0,2,1:T(8,128)(2,1)}), bf16[128,32,64]{0,2,1:T(8,128)(2,1)S(1)}, u32[]{:S(2)}, u32[]{:S(2)}) async-start(bf16[128,32,64]{0,2,1:T(8,128)(2,1)} %bitcast.18), calls=%async_computation.1 | async-start | bytes 1048576 | tf_op jit(solution)/shard_map/all_to_all | solution.py:149
  278.0 13.7 all-to-all-start.2
  302.5 13.9 all-to-all-start.9
  306.2 231.4 %reduce-scatter.17.cloned.1.call-start = ((), (), s32[]{:S(2)}) async-start(), calls=%async_computation.27 | async-start | bytes 589824
  478.9 15.8 all-to-all-start.10
  485.7 6.5 collective-permute-start.2
  568.3 42.1 %all-to-all-start.7 = ((bf16[128,32,64]{0,2,1:T(8,128)(2,1)}), bf16[128,32,64]{0,2,1:T(8,128)(2,1)S(1)}, u32[]{:S(2)}, u32[]{:S(2)}) async-start(bf16[128,32,64]{0,2,1:T(8,128)(2,1)} %bitcast.49), calls=%async_computation.7 | async-start | bytes 1048576 | tf_op jit(solution)/shard_map/all_to_all | solution.py:149
  703.5 13.9 all-to-all-start.15
  707.1 231.6 %reduce-scatter.21.cloned.1.call-start = ((), (), s32[]{:S(2)}) async-start(), calls=%async_computation.29 | async-start | bytes 589824
  879.2 29.7 %all-to-all-start.16 = ((bf16[8,2,16384]{2,1,0:T(2,128)(2,1)}), bf16[8,2,16384]{2,1,0:T(2,128)(2,1)}, u32[]{:S(2)}, u32[]{:S(2)}) async-start(bf16[8,2,16384]{2,1,0:T(2,128)(2,1)} %reshape.1591), calls=%async_computation.16 | async-start | bytes 1048576 | tf_op jit(solution)/shard_map/all_to_all | solution.py:209
  887.8 17.9 collective-permute-start.1
  901.5 5.9 collective-permute-start.3
  971.1 42.2 %all-to-all-start.4 = ((bf16[128,32,64]{0,2,1:T(8,128)(2,1)}), bf16[128,32,64]{0,2,1:T(8,128)(2,1)S(1)}, u32[]{:S(2)}, u32[]{:S(2)}) async-start(bf16[128,32,64]{0,2,1:T(8,128)(2,1)} %bitcast.34), calls=%async_computation.4 | async-start | bytes 1048576 | tf_op jit(solution)/shard_map/all_to_all | solution.py:149
  1106.7 14.5 all-to-all-start.12
  1110.8 241.1 %reduce-scatter.19.cloned.1.call-start = ((), (), s32[]{:S(2)}) async-start(), calls=%async_computation.28 | async-start | bytes 589824
  1288.2 251.6 %reduce-scatter.15.cloned.1.call-start = ((), (), s32[]{:S(2)}) async-start(), calls=%async_computation.26 | async-start | bytes 8650752 | tf_op jit(solution)/shard_map/reduce_scatter | solution.py:259
  1303.0 26.0 %all-to-all-start.13 = ((bf16[8,2,16384]{2,1,0:T(2,128)(2,1)}), bf16[8,2,16384]{2,1,0:T(2,128)(2,1)}, u32[]{:S(2)}, u32[]{:S(2)}) async-start(bf16[8,2,16384]{2,1,0:T(2,128)(2,1)} %reshape.1593), calls=%async_computation.13 | async-start | bytes 1048576 | tf_op jit(solution)/shard_map/all_to_all | solution.py:209
  1319.5 5.9 collective-permute-start.5
  1329.0 60.8 %all-to-all-start.11 = ((bf16[8,128,4]{1,2,0:T(4,128)(2,1)}), bf16[8,128,4]{1,2,0:T(4,128)(2,1)S(1)}, u32[]{:S(2)}, u32[]{:S(2)}) async-start(bf16[8,128,4]{1,2,0:T(4,128)(2,1)} %bitcast.846), calls=%async_computation.11 | async-start | bytes 16384 | tf_op jit(solution)/shard_map/all_to_all | solution.py:212
  1388.5 17.5 collective-permute-start.4
  1389.8 24.1 %all-to-all-start.14 = ((bf16[8,128,4]{1,2,0:T(4,128)(2,1)}), bf16[8,128,4]{1,2,0:T(4,128)(2,1)S(1)}, u32[]{:S(2)}, u32[]{:S(2)}) async-start(bf16[8,128,4]{1,2,0:T(4,128)(2,1)} %bitcast.845), calls=%async_computation.14 | async-start | bytes 16384 | tf_op jit(solution)/shard_map/all_to_all | solution.py:212
  1413.9 16.3 all-to-all-start.17
  1419.9 514.1 %reduce-scatter.13.cloned.1.call-start = ((), (), s32[]{:S(2)}) async-start(), calls=%async_computation.25 | async-start | bytes 18923520 | tf_op jit(solution)/shard_map/reduce_scatter | solution.py:258
  (199 other events, 1803.9 us)
Sparse Core Ops, SparseCore 0:
  10.9 84.2 all-gather.3
  98.3 60.8 all-gather.5
  476.8 60.6 reduce-scatter.16
  877.1 61.5 reduce-scatter.20
  1288.3 63.6 reduce-scatter.18
  1354.8 184.9 reduce-scatter.14
  1542.8 391.1 reduce-scatter.12
where the time goes:
time: 1960 us; the launch traced here: 1940 us
  waiting for transfers between devices  519 us (26%)
  other arithmetic  378 us (19%)
  local copies, waits for them, and re-layouts  359 us (18%)
  blocking collectives  289 us (15%)
  matrix products  283 us (14%)
  starting transfers between devices  86 us (4%)
    reduce_scatter x1, waiting for transfers between devices, body(): lax.psum_scatter(total_win, ('fsdp', 'seq'), scatter_dimension=0, tiled=T...  394 us
    another operation x103, other arithmetic  151 us
    all_gather x3, blocking collectives, body(): bc_all = lax.all_gather(bc_low, 'seq', axis=0, tiled=True)  96.4 us
    unnamed x2, blocking collectives  90.1 us
    unnamed x10, waiting for transfers between devices  77.6 us
    all_gather x1, blocking collectives, body(): lax.all_gather(conv_w, ('fsdp', 'seq'), axis=1, tiled=True)  66.4 us
    dot_general x36, matrix products, span_step(): jnp.einsum('hts,shp->thp', decay_in * intersection[None], scaled, precisi...  58.8 us
    unnamed x348, local copies, waits for them, and re-layouts  56.3 us
  transfers between devices with their start and end apart: 29, of which 14 were waited for; matrix products, arithmetic and copies ran while one was open for 16% of the time, Pallas kernels for 0%

commit v1 on v0

v1 whole, which is shorter than its diff:
```python
import functools

import numpy as np
import jax
import jax.numpy as jnp
from jax import lax
from jax.experimental import pallas as pl
from jax.experimental.pallas import tpu as pltpu
from jax.sharding import PartitionSpec as P

D = 1024
H = 32
P_SIZE = 64
N = 128
KERNEL = 4
MB = 3
INNER = H * P_SIZE
CONV = INNER + 2 * N
HALO = 16
FRONT = 384
TILE = 256
P_TILES = 3
P_COLS = FRONT + P_TILES * TILE
W1_COLS = FRONT + INNER
Q_COLS = W1_COLS - P_COLS
GROUP = 8
EPS = 1e-05
F32 = jnp.float32
BF16 = jnp.bfloat16
BOTH = ("fsdp", "seq")
VMEM = pl.BlockSpec(memory_space=pltpu.VMEM)
SMEM = pl.BlockSpec(memory_space=pltpu.SMEM)
ANY = pl.BlockSpec(memory_space=pl.ANY)
HBM = pl.BlockSpec(memory_space=pltpu.HBM)
SMALL = pl.CostEstimate(flops=1, bytes_accessed=1, transcendentals=0)


def shape(dims, dtype=F32):
    return jax.ShapeDtypeStruct(dims, dtype)


def params(mib=48):
    return pltpu.CompilerParams(vmem_limit_bytes=mib * 2**20)


def permute(block, mask):
    size = lax.axis_size("fsdp") * lax.axis_size("seq")
    return lax.ppermute(block, BOTH, [(i, i ^ mask) for i in range(size)])


def tied(*values):
    return lax.optimization_barrier(values)


def combos(masks):
    found = [0]
    for mask in masks:
        found += [c | mask for c in found]
    return found[1:]


def spread(held, stage):
    return jnp.concatenate([held] + [permute(held, m) for m in stage], axis=0)


def cut(total, stage):
    width = total.shape[0] // (len(stage) + 1)
    return [total[i * width : (i + 1) * width] for i in range(len(stage) + 1)]


def fold(pieces, stage, dtype=BF16):
    total = pieces[0].astype(F32)
    for part, m in zip(pieces[1:], stage):
        total = total + permute(part, m).astype(F32)
    return total.astype(dtype)


def order_of(stages):
    masks = [0]
    for stage in stages:
        held = list(masks)
        for m in stage:
            masks += [k ^ m for k in held]
    return np.array(masks, np.int32)


def split3(v):
    high = lax.reduce_precision(v, 8, 7)
    mid = lax.reduce_precision(v - high, 8, 7)
    return [p.astype(BF16) for p in (high, mid, v - high - mid)]


def nn(a, b):
    return jnp.dot(a, b, preferred_element_type=F32)


def nt(a, b):
    return lax.dot_general(a, b, (((1,), (1,)), ((), ())), preferred_element_type=F32)


def tn(a, b):
    return lax.dot_general(a, b, (((0,), (0,)), ((), ())), preferred_element_type=F32)


def split(v, count=3):
    parts = []
    for _ in range(count):
        part = v.astype(BF16)
        parts.append(part)
        v = v - part.astype(F32)
    return parts


def one_hot(tile):
    row = lax.broadcasted_iota(jnp.int32, (N, TILE), 0)
    col = lax.broadcasted_iota(jnp.int32, (N, TILE), 1)
    return ((row % H == tile * (TILE // P_SIZE) + col // P_SIZE) & (row < 3 * H)).astype(F32).astype(BF16)


def packed(v):
    lane = lax.broadcasted_iota(jnp.int32, v.shape, 1)
    v = jnp.where(lane < H, v, 0.0)
    high, mid, low = [p.astype(F32) for p in split(v)]
    return (high + pltpu.roll(mid, H, 1) + pltpu.roll(low, 2 * H, 1)).astype(BF16)


def wide(parts, hot):
    return nn(parts, hot)


def head_sum(v, hot):
    return sum(nt(p, hot) for p in split(v, 2))


def sigmoid(v):
    return 1.0 / (1.0 + jnp.exp(-v))


def exact_sum(matrix, v):
    return sum(nn(matrix, p) for p in split(v))


def turned(v):
    return v.astype(F32).T


def block_copies(lin, masks, sources, place, sems):
    copies = []
    half = len(masks) // 2
    for r, mask in enumerate(masks):
        where = lin ^ int(mask)
        source = sources[r // half].at[r % half]
        for src, dst in place(source, where):
            copy = pltpu.make_async_copy(src, dst, sems.at[len(copies)])
            copy.start()
            copies.append(copy)
    return copies


def rows_at(ref, where, height, cols):
    return ref.at[pl.ds(pl.multiple_of(where * height, height), height), cols]


def put(out_ref, piece, offset, width, rows):
    first, shift = offset // 128, offset % 128
    lane = lax.broadcasted_iota(jnp.int32, piece.shape, 1)
    moved = pltpu.roll(jnp.where(lane < width, piece, 0.0), shift, 1) if shift else jnp.where(lane < width, piece, 0.0)
    if shift + width > 128:
        out_ref[rows, first * 128 : first * 128 + 128] += jnp.where(lane >= shift, moved, 0.0)
        out_ref[rows, first * 128 + 128 : first * 128 + 256] += jnp.where(lane < shift, moved, 0.0)
    else:
        out_ref[rows, first * 128 : first * 128 + 128] += moved


def get(in_ref, offset, width, rows):
    first, shift = offset // 128, offset % 128
    piece = in_ref[rows, first * 128 : first * 128 + 128]
    lane = lax.broadcasted_iota(jnp.int32, piece.shape, 1)
    if shift + width > 128:
        piece = jnp.where(lane >= shift, piece, in_ref[rows, first * 128 + 128 : first * 128 + 256])
    piece = pltpu.roll(piece, 128 - shift, 1) if shift else piece
    return jnp.where(lane < width, piece, 0.0)


def small_kernel(n_dev, n_s, total, part, tab, small_ref, line_ref, taps_ref, gin_ref, gout_ref, hp_ref, skip_ref, meta_ref, col_ref, row_ref, conv_s):
    conv_s[...] = jnp.zeros_like(conv_s)
    gin_ref[...] = jnp.zeros_like(gin_ref)
    gout_ref[...] = jnp.zeros_like(gout_ref)
    hp_ref[...] = jnp.zeros_like(hp_ref)
    channels, features, wider, heads = CONV // n_dev, D // n_dev, INNER // n_dev, H // n_s
    everything = slice(0, 8)
    for d in range(n_dev):
        block = small_ref[tab[d]]
        if part:
            block = block.astype(F32)
            block = pltpu.roll(block[:8] + block[8:16] + block[16:24], 128 - H, 1)
        put(conv_s, block, d * channels, channels, everything)
        put(gin_ref, block[5:6], d * features, features, slice(0, 1))
        put(gout_ref, block[6:7], d * wider, wider, slice(0, 1))
        if d < n_s:
            for k in range(3):
                head = block[7:8] if k == 0 else pltpu.roll(block[7:8], 128 - k * heads, 1)
                put(hp_ref, head, d * heads, heads, slice(k, k + 1))
    taps_ref[:, : 2 * N] = conv_s[:, INNER:]
    taps_ref[:, 2 * N :] = conv_s[:, :INNER]
    lane = lax.broadcasted_iota(jnp.int32, (1, N), 1)
    hp_ref[1:2, :] = jnp.where(lane < H, jnp.exp(hp_ref[1:2, :]), 0.0)
    parts = packed(jnp.broadcast_to(hp_ref[2:3, :], (16, N)))
    for j in range(INNER // TILE):
        skip_ref[:, j * TILE : (j + 1) * TILE] = wide(parts, one_hot(j))[:1]
    line = line_ref[...]
    wide_line = line.shape[1]
    moved = lambda v, k: pltpu.roll(v, wide_line - k, 1)[:, :total]
    ids = line[0:1]
    own = moved(ids, HALO)
    keep = lambda test: jnp.where(test, 1.0, 0.0)
    same = [keep(moved(ids, HALO - 3 + k) == own) for k in range(3)]
    before = jnp.sum(jnp.where(lax.broadcasted_iota(jnp.int32, ids.shape, 1) == HALO - 1, ids, 0.0), axis=1, keepdims=True)
    final = jnp.sum(jnp.where(lax.broadcasted_iota(jnp.int32, ids.shape, 1) == HALO + total - 1, ids, 0.0), axis=1, keepdims=True)
    rows = same + [moved(line[1:2], HALO), keep(own == before), keep(own == final), own, own]
    turned_rows = jnp.concatenate(rows, axis=0).T
    meta_ref[...] = turned_rows
    col_ref[...] = turned_rows[:, 6:7]
    row_ref[...] = own


def small_stage(tab, small, line, n_dev, n_s, total):
    return pl.pallas_call(
        functools.partial(small_kernel, n_dev, n_s, total, small.dtype == BF16),
        out_shape=(
            shape((8, CONV)), shape((1, D)), shape((1, INNER)), shape((8, N)), shape((1, INNER)), shape((total, 8)), shape((total, 1)), shape((1, total)),
        ),
        in_specs=[SMEM, VMEM, VMEM],
        out_specs=tuple([VMEM] * 8),
        scratch_shapes=[pltpu.VMEM((8, CONV), F32)],
        compiler_params=params(),
        cost_estimate=SMALL,
        name="small_stage",
    )(tab, small, line)


def grad_small(n_dev, n_s, tab, gp_ref, gq_ref, gout_ref, few_ref, out_ref, conv_s):
    split_at = P_TILES * TILE
    conv_s[:, :split_at] = gp_ref[:, FRONT:]
    conv_s[:, split_at:INNER] = gq_ref[...]
    conv_s[:, INNER:] = gp_ref[:, 128:FRONT]
    channels, wider, heads = CONV // n_dev, INNER // n_dev, H // n_s
    for d in range(n_dev):
        where = (d % n_s) * heads
        head = jnp.zeros((1, 128), F32)
        for k in range(3):
            piece = get(few_ref.at[k], where, heads, slice(0, 1))
            head = head + (pltpu.roll(piece, k * heads, 1) if k else piece)
        rows = [get(conv_s, d * channels, channels, slice(0, 8))[:5], jnp.zeros((1, 128), F32)]
        rows += [get(gout_ref, d * wider, wider, slice(0, 1)), head]
        out_ref[tab[d]] = jnp.concatenate(rows, axis=0)


def grad_small_stage(tab, gp, gq, gout, few, n_dev, n_s):
    return pl.pallas_call(
        functools.partial(grad_small, n_dev, n_s),
        out_shape=shape((n_dev, 8, 128)),
        in_specs=[SMEM] + [VMEM] * 4,
        out_specs=VMEM,
        scratch_shapes=[pltpu.VMEM((8, CONV), F32)],
        compiler_params=params(),
        cost_estimate=SMALL,
        name="grad_small_stage",
    )(tab, gp, gq, gout, few)


def first_kernel(masks_p, masks_q, total, lin_ref, halo_ref, t0_ref, t1_ref, t2_ref, gain_ref, meta_ref, taps_ref, hp_ref, po, px, qo, qx,
                 w1_ref, normed_ref, cin_ref, pre_ref, bc_ref, x_ref, dtx_ref, hd_ref, cumt_ref, pay_ref, cin_s, w1_s, cin_b, pre_b, sem_p, sem_q, sem_out):
    lin = lin_ref[0]
    rows = D // len(masks_p)
    place = lambda cols: lambda src, where: [(src, rows_at(w1_s, where, rows, cols))]
    first = block_copies(lin, masks_p, (po, px), place(pl.ds(0, P_COLS)), sem_p)
    second = block_copies(lin, masks_q, (qo, qx), place(pl.ds(P_COLS, Q_COLS)), sem_q)
    start = 0
    for ref in (halo_ref, t0_ref, t1_ref, t2_ref):
        u = ref[...].astype(F32)
        scale = lax.rsqrt(jnp.mean(u * u, axis=-1, keepdims=True) + EPS)
        normed_ref[start : start + u.shape[0], :] = (u * scale * gain_ref[...]).astype(BF16)
        start += u.shape[0]
    written = []

    def write(source, target):
        copy = pltpu.make_async_copy(source, target, sem_out.at[len(written)])
        copy.start()
        written.append(copy)

    for copy in first:
        copy.wait()
    meta = meta_ref[...]
    same = [meta[:, k : k + 1] for k in range(3)]
    valid, carry, tail = meta[:, 3:4], meta[:, 4:5], meta[:, 5:6]

    def conv(made, cols):
        cin_s[...] = made
        cin_b[:, cols] = made.astype(BF16)
        acc = taps_ref[4:5, cols] + taps_ref[3:4, cols] * made[HALO:]
        for k in range(3):
            acc = acc + taps_ref[k : k + 1, cols] * (cin_s[HALO - 3 + k : HALO - 3 + k + total, :] * same[k])
        pre_b[:, cols] = acc.astype(BF16)
        write(cin_b.at[:, cols], cin_ref.at[:, cols])
        write(pre_b.at[:, cols], pre_ref.at[:, cols])
        return (acc * sigmoid(acc)).astype(BF16)

    front = nn(normed_ref[...], w1_s[:, :FRONT])
    lane = lax.broadcasted_iota(jnp.int32, (total, 128), 1)
    shifted = jnp.where(lane < H, front[HALO:, :128], 0.0).astype(BF16).astype(F32) + hp_ref[0:1, :]
    dt = (jnp.maximum(shifted, 0.0) + jnp.log1p(jnp.exp(-jnp.abs(shifted)))) * valid
    row = lax.broadcasted_iota(jnp.int32, (total, total), 0)
    col = lax.broadcasted_iota(jnp.int32, (total, total), 1)
    lower = (row >= col).astype(F32).astype(BF16)
    cum = exact_sum(lower, -dt * hp_ref[1:2, :])
    reach = jnp.exp(cum) * carry
    w_end = jnp.exp(cum[total - 1 : total] - cum) * tail
    hd_ref[0], hd_ref[1], hd_ref[2], hd_ref[3], hd_ref[4] = dt, cum, reach, w_end, shifted
    cumt_ref[...] = cum.T[:H]
    bc = conv(front[:, 128:], pl.ds(0, 2 * N))
    bc_ref[...] = bc
    b_turned = turned(bc[:, :N]).astype(BF16)
    through = jnp.broadcast_to(reach[total - 1 : total], (8, N))
    dt_parts, both_parts = packed(dt), packed(dt * w_end)
    through_parts = [packed(p.astype(F32)) for p in split(through)]
    for j in range(INNER // TILE):
        if j == P_TILES:
            for copy in second:
                copy.wait()
            write(w1_s, w1_ref)
        cols = pl.ds(2 * N + j * TILE, TILE)
        own = slice(j * TILE, (j + 1) * TILE)
        x = conv(nn(normed_ref[...], w1_s[:, FRONT + j * TILE : FRONT + (j + 1) * TILE]), cols)
        x_ref[:, own] = x
        xf = x.astype(F32)
        hot = one_hot(j)
        dtx_ref[:, own] = (xf * wide(dt_parts, hot)).astype(BF16)
        pay_ref[:N, own] = nn(b_turned, (xf * wide(both_parts, hot)).astype(BF16)).astype(BF16)
        extra = [nn(p, hot)[:1] for p in through_parts]
        pay_ref[N:, own] = jnp.concatenate(extra + [jnp.zeros((HALO - 3, TILE), F32)], axis=0).astype(BF16)
    for copy in written:
        copy.wait()


def first_stage(tok, gain_in, meta, taps, hp, p, q, total):
    (po, px, masks_p, lin_p), (qo, qx, masks_q, _) = p, q
    ext = total + HALO
    return pl.pallas_call(
        functools.partial(first_kernel, masks_p, masks_q, total),
        out_shape=(
            shape((D, W1_COLS), BF16), shape((ext, D), BF16), shape((ext, CONV), BF16), shape((total, CONV), BF16), shape((total, 2 * N), BF16),
            shape((total, INNER), BF16), shape((total, INNER), BF16), shape((5, total, N)), shape((H, total)), shape((N + HALO, INNER), BF16),
        ),
        in_specs=[SMEM] + [VMEM] * 8 + [ANY] * 4,
        out_specs=(HBM, VMEM, HBM, HBM) + tuple([VMEM] * 6),
        scratch_shapes=[pltpu.VMEM((ext, TILE), F32), pltpu.VMEM((D, W1_COLS), BF16), pltpu.VMEM((ext, CONV), BF16), pltpu.VMEM((total, CONV), BF16), pltpu.SemaphoreType.DMA((len(masks_p),)), pltpu.SemaphoreType.DMA((len(masks_q),)), pltpu.SemaphoreType.DMA((2 * (INNER // TILE + 1) + 1,))],
        compiler_params=params(),
        cost_estimate=SMALL,
        name="first_stage",
    )(lin_p, *tok, gain_in, meta, taps, hp, po, px, qo, qx)


def late_copies(count, blocks, wg_s, wo_s, sem_g, sem_o):
    rows = D // count
    first, second = [], []
    for r in range(count):
        copy = pltpu.make_async_copy(blocks.at[r, 0], wg_s.at[pl.ds(r * rows, rows)], sem_g.at[r])
        copy.start()
        first.append(copy)
    for r in range(count):
        for i in range(2):
            target = wo_s.at[pl.ds((2 * r + i) * rows, rows)]
            copy = pltpu.make_async_copy(blocks.at[r, 1, :, pl.ds(i * D, D)], target, sem_o.at[2 * r + i])
            copy.start()
            second.append(copy)
    return first, second


def late_scratch(count):
    return [pltpu.VMEM((D, INNER), BF16), pltpu.VMEM((INNER, D), BF16), pltpu.SemaphoreType.DMA((count,)), pltpu.SemaphoreType.DMA((2 * count,))]


def gate_kernel(count, normed_ref, g_ref, blocks, ga_ref, dga_ref, gno_ref, wg_s, wo_s, sem_g, sem_o):
    first, second = late_copies(count, blocks, wg_s, wo_s, sem_g, sem_o)
    for copy in first:
        copy.wait()
    for j in range(INNER // TILE):
        own = slice(j * TILE, (j + 1) * TILE)
        gate = nn(normed_ref[HALO:], wg_s[:, own])
        sig = sigmoid(gate)
        ga_ref[:, own] = (gate * sig).astype(BF16)
        dga_ref[:, own] = (sig * (1.0 + gate * (1.0 - sig))).astype(BF16)
    for copy in second:
        copy.wait()
    for j in range(INNER // TILE):
        own = slice(j * TILE, (j + 1) * TILE)
        gno_ref[:, own] = nt(g_ref[...], wo_s[own, :]).astype(BF16)


def gate_stage(normed, g, blocks, total):
    count = blocks.shape[0]
    return pl.pallas_call(
        functools.partial(gate_kernel, count),
        out_shape=(shape((total, INNER), BF16),) * 3,
        in_specs=[VMEM] * 2 + [HBM],
        out_specs=tuple([VMEM] * 3),
        scratch_shapes=late_scratch(count),
        compiler_params=params(),
        cost_estimate=SMALL,
        name="gate_stage",
    )(normed, g, blocks)


def left_lanes():
    return lax.broadcasted_iota(jnp.int32, (1, 2 * P_SIZE), 1) < P_SIZE


def pairs_kernel(total, bc_ref, dtx_ref, cumt_ref, id_col, id_row, out_ref, cb_ref, mask_ref):
    @pl.when(pl.program_id(0) == 0)
    def _():
        cb_ref[...] = nt(bc_ref[:, N:], bc_ref[:, :N])
        row = lax.broadcasted_iota(jnp.int32, (total, total), 0)
        col = lax.broadcasted_iota(jnp.int32, (total, total), 1)
        mask_ref[...] = jnp.where((row >= col) & (id_col[...] == id_row[...]), 0.0, -1e30)

    cum_cols = cumt_ref[...].T
    left = left_lanes()
    for pair in range(GROUP // 2):
        lanes = slice(pair * 2 * P_SIZE, (pair + 1) * 2 * P_SIZE)
        for a in range(total // N):
            rows, width = slice(a * N, (a + 1) * N), (a + 1) * N
            made = []
            for i in (2 * pair, 2 * pair + 1):
                decay = jnp.exp(cum_cols[rows, i : i + 1] - cumt_ref[i : i + 1, :width] + mask_ref[rows, :width])
                made.append(nn((decay * cb_ref[rows, :width]).astype(BF16), dtx_ref[:width, lanes]))
            out_ref[rows, lanes] = jnp.where(left, made[0], made[1])


def pairs_stage(bc, dtx, cumt, id_col, id_row, total):
    block = pl.BlockSpec((total, GROUP * P_SIZE), lambda g: (0, g))
    return pl.pallas_call(
        functools.partial(pairs_kernel, total),
        grid=(H // GROUP,),
        out_shape=shape((total, INNER)),
        in_specs=[VMEM, block, pl.BlockSpec((GROUP, total), lambda g: (g, 0)), VMEM, VMEM],
        out_specs=block,
        scratch_shapes=[pltpu.VMEM((total, total), F32)] * 2,
        compiler_params=params(),
        cost_estimate=SMALL,
        name="pairs_stage",
    )(bc, dtx, cumt, id_col, id_row)


def pairs_back_kernel(total, bc_ref, dtx_ref, e_ref, cumt_ref, id_col, id_row, gdtx_ref, gb_ref, gc_ref, cb_ref, mask_ref, acc_ref):
    @pl.when(pl.program_id(0) == 0)
    def _():
        cb_ref[...] = nt(bc_ref[:, :N], bc_ref[:, N:])
        row = lax.broadcasted_iota(jnp.int32, (total, total), 0)
        col = lax.broadcasted_iota(jnp.int32, (total, total), 1)
        mask_ref[...] = jnp.where((row <= col) & (id_col[...] == id_row[...]), 0.0, -1e30)
        acc_ref[...] = jnp.zeros_like(acc_ref)

    cum_cols = cumt_ref[...].T
    left = left_lanes()
    for pair in range(GROUP // 2):
        lanes = slice(pair * 2 * P_SIZE, (pair + 1) * 2 * P_SIZE)
        for a in range(total // N):
            rows, after = slice(a * N, (a + 1) * N), slice(a * N, total)
            made, added = [], None
            for side, i in enumerate((2 * pair, 2 * pair + 1)):
                decay = jnp.exp(cumt_ref[i : i + 1, after] - cum_cols[rows, i : i + 1] + mask_ref[rows, after])
                made.append(nn((decay * cb_ref[rows, after]).astype(BF16), e_ref[after, lanes]))
                mine = dtx_ref[rows, lanes].astype(F32)
                mine = jnp.where(left, mine, 0.0) if side == 0 else jnp.where(left, 0.0, mine)
                term = nt(mine.astype(BF16), e_ref[after, lanes]) * decay
                added = term if added is None else added + term
            gdtx_ref[rows, lanes] = jnp.where(left, made[0], made[1])
            acc_ref[rows, after] += added

    @pl.when(pl.program_id(0) == H // GROUP - 1)
    def _():
        gb_ref[...] = nn(acc_ref[...].astype(BF16), bc_ref[:, N:])
        gc_ref[...] = nn(acc_ref[...].T.astype(BF16), bc_ref[:, :N])


def pairs_back_stage(bc, dtx, e, cumt, id_col, id_row, total):
    block = pl.BlockSpec((total, GROUP * P_SIZE), lambda g: (0, g))
    flat = pl.BlockSpec((total, N), lambda g: (0, 0))
    return pl.pallas_call(
        functools.partial(pairs_back_kernel, total),
        grid=(H // GROUP,),
        out_shape=(shape((total, INNER)), shape((total, N)), shape((total, N))),
        in_specs=[VMEM, block, block, pl.BlockSpec((GROUP, total), lambda g: (g, 0)), VMEM, VMEM],
        out_specs=(block, flat, flat),
        scratch_shapes=[pltpu.VMEM((total, total), F32)] * 3,
        compiler_params=params(),
        cost_estimate=SMALL,
        name="pairs_back_stage",
    )(bc, dtx, e, cumt, id_col, id_row)


def combined(refs, cols):
    states = refs[0][:N, cols].astype(F32)
    factor = None
    for near, ref in zip(refs, refs[1:]):
        step = jnp.sum(near[N:, cols].astype(F32), axis=0, keepdims=True)
        factor = step if factor is None else factor * step
        states = states + factor * ref[:N, cols].astype(F32)
    return states


def output_kernel(count, total, *refs):
    got = refs[:count]
    (inside_ref, bc_ref, x_ref, hd_ref, ga_ref, dga_ref, gno_ref, gain_ref, skip_ref, own_ref,
     state_ref, no_ref, e_ref, gg_ref, pay_ref, gc_ref, rows_ref, ggain_ref, scan_s, gated_s) = refs[count:]
    c_part = bc_ref[:, N:]
    reach = packed(hd_ref[2])
    squares = jnp.zeros((total, 1), F32)
    crossed = jnp.zeros((total, 1), F32)
    for j in range(INNER // TILE):
        own = slice(j * TILE, (j + 1) * TILE)
        state = combined(got, own).astype(BF16)
        state_ref[:, own] = state
        scan = inside_ref[:, own] + nn(c_part, state) * wide(reach, one_hot(j))
        scan_s[:, own] = scan
        mixed = (scan + skip_ref[:, own] * x_ref[:, own].astype(F32)).astype(BF16)
        gg_ref[:, own] = mixed
        gated = mixed.astype(F32) * ga_ref[:, own].astype(F32)
        gated_s[:, own] = gated
        squares = squares + jnp.sum(gated * gated, axis=-1, keepdims=True)
        crossed = crossed + jnp.sum(gno_ref[:, own].astype(F32) * gain_ref[:, own] * gated, axis=-1, keepdims=True)
    scale = lax.rsqrt(squares / INNER + EPS)
    mean = crossed * scale / INNER
    c_turned = turned(c_part).astype(BF16)
    grad_c = jnp.zeros((total, N), F32)
    row_sum = jnp.zeros((total, N), F32)
    for j in range(INNER // TILE):
        own = slice(j * TILE, (j + 1) * TILE)
        hot = one_hot(j)
        unit = gated_s[:, own] * scale
        gno = gno_ref[:, own].astype(F32)
        no_ref[:, own] = (unit * gain_ref[:, own]).astype(BF16)
        ggain_ref[:, own] = jnp.sum(gno * unit, axis=0, keepdims=True)
        grad = scale * (gno * gain_ref[:, own] - unit * mean)
        e = (grad * ga_ref[:, own].astype(F32)).astype(BF16)
        e_ref[:, own] = e
        gg_ref[:, own] = (grad * gg_ref[:, own].astype(F32) * dga_ref[:, own].astype(F32)).astype(BF16)
        ef = e.astype(F32)
        e_reach = (ef * wide(reach, hot)).astype(BF16)
        pay_ref[:N, own] = nn(c_turned, e_reach).astype(BF16)
        grad_c = grad_c + nt(e_reach, state_ref[:, own])
        row_sum = row_sum + head_sum(ef * scan_s[:, own], hot)
    pay_ref[N:, :] = own_ref[N:, :]
    gc_ref[...] = grad_c
    rows_ref[...] = row_sum


def output_stage(got, inside, bc, x, hd, ga, dga, gno, gain_out, skip_wide, pay, total):
    count = len(got)
    big = lambda t: shape((total, INNER), t)
    return pl.pallas_call(
        functools.partial(output_kernel, count, total),
        out_shape=(shape((N, INNER), BF16), big(BF16), big(BF16), big(BF16), shape((N + HALO, INNER), BF16), shape((total, N)), shape((total, N)), shape((1, INNER))),
        in_specs=[VMEM] * (count + 10),
        out_specs=tuple([VMEM] * 8),
        scratch_shapes=[pltpu.VMEM((total, INNER), F32)] * 2,
        compiler_params=params(),
        cost_estimate=SMALL,
        name="output_stage",
    )(*got, inside, bc, x, hd, ga, dga, gno, gain_out, skip_wide, pay)


def turn_kernel(count, tab_p, tab_q, normed_ref, p_ref, q_ref):
    rows = D // count
    for j in range(D // TILE):
        made = normed_ref[:, j * TILE : (j + 1) * TILE].astype(F32).T.astype(BF16)
        for i in range(TILE // rows):
            block = made[i * rows : (i + 1) * rows]
            a = j * (TILE // rows) + i
            p_ref[pl.ds(pl.multiple_of(tab_p[a] * rows, rows), rows), :] = block
            q_ref[pl.ds(pl.multiple_of(tab_q[a] * rows, rows), rows), :] = block


def turn_stage(tab_p, tab_q, normed):
    out = shape((D, normed.shape[0]), BF16)
    return pl.pallas_call(
        functools.partial(turn_kernel, tab_p.shape[0]),
        out_shape=(out, out),
        in_specs=[SMEM, SMEM, VMEM],
        out_specs=(VMEM, VMEM),
        compiler_params=params(),
        cost_estimate=SMALL,
        name="turn_stage",
    )(tab_p, tab_q, normed)


def weights_kernel(count, tab_q, turned_ref, gg_ref, no_ref, g_ref, keep_g, send_g, keep_o, send_o, turned_s):
    for j in range(INNER // TILE):
        own = slice(j * TILE, (j + 1) * TILE)
        weight_grad(turned_ref[:, HALO:], gg_ref[:, own], own, keep_g, send_g)
    rows = INNER // count
    for j in range(INNER // TILE):
        made = no_ref[:, j * TILE : (j + 1) * TILE].astype(F32).T.astype(BF16)
        for i in range(TILE // rows):
            place = pl.ds(pl.multiple_of(tab_q[j * (TILE // rows) + i] * rows, rows), rows)
            turned_s[place, :] = made[i * rows : (i + 1) * rows]
    for j in range(D // TILE):
        own = slice(j * TILE, (j + 1) * TILE)
        weight_grad(turned_s[...], g_ref[:, own], own, keep_o, send_o)


def weights_stage(tab_q, turned_rows, grad_gate, normed_out, g, total):
    return pl.pallas_call(
        functools.partial(weights_kernel, tab_q.shape[0]),
        out_shape=(shape((D // 2, INNER), BF16),) * 2 + (shape((D, D), BF16),) * 2,
        in_specs=[SMEM] + [VMEM] * 4,
        out_specs=tuple([VMEM] * 4),
        scratch_shapes=[pltpu.VMEM((INNER, total), BF16)],
        compiler_params=params(),
        cost_estimate=SMALL,
        name="weights_stage",
    )(tab_q, turned_rows, grad_gate, normed_out, g)


def rest_kernel(count, no_ref, gg_ref, tok_ref, blocks, out_ref, part_ref, wg_s, wo_s, sem_g, sem_o):
    first, second = late_copies(count, blocks, wg_s, wo_s, sem_g, sem_o)
    for copy in first:
        copy.wait()
    half = D // 4
    for j in range(4):
        own = slice(j * half, (j + 1) * half)
        part_ref[:, own] = nt(gg_ref[...], wg_s[own, :])
    for copy in second:
        copy.wait()
    for j in range(4):
        own = slice(j * half, (j + 1) * half)
        out_ref[:, own] = (tok_ref[HALO:, own].astype(F32) + nn(no_ref[...], wo_s[:, own])).astype(BF16)


def rest_stage(normed_out, grad_gate, ext_tok, blocks, total):
    count = blocks.shape[0]
    return pl.pallas_call(
        functools.partial(rest_kernel, count),
        out_shape=(shape((total, D), BF16), shape((total, D))),
        in_specs=[VMEM] * 3 + [HBM],
        out_specs=(VMEM, VMEM),
        scratch_shapes=late_scratch(count),
        compiler_params=params(),
        cost_estimate=SMALL,
        name="rest_stage",
    )(normed_out, grad_gate, ext_tok, blocks)


def heads_back(count, total, tiles, got, refs, sums, emit):
    gdtx_ref, e_ref, x_ref, dtx_ref, bc_ref, state_ref, hd_ref, skip_ref = refs
    gb, q_sum, back_sum, xg, both, gskip = sums
    b_part = bc_ref[:, :N]
    dt_parts, end_parts = packed(hd_ref[0]), packed(hd_ref[3])
    for n, j in enumerate(tiles):
        own = slice(j * TILE, (j + 1) * TILE)
        hot = one_hot(j)
        later = combined(got, own)
        later_low = later.astype(BF16)
        w_end, dt = wide(end_parts, hot), wide(dt_parts, hot)
        from_later = nn(b_part, later_low) * w_end
        inner = gdtx_ref[:, own]
        dtx = dtx_ref[:, own].astype(F32)
        x, e = x_ref[:, own].astype(F32), e_ref[:, own].astype(F32)
        q_sum = q_sum + head_sum(dtx * from_later, hot)
        back_sum = back_sum + head_sum(dtx * inner, hot)
        grad = inner + from_later
        xg = xg + head_sum(x * grad, hot)
        crossing = jnp.sum(state_ref[:, own].astype(F32) * later, axis=0, keepdims=True)
        skipped = jnp.sum(x * e, axis=0, keepdims=True)
        both = both + head_sum(jnp.broadcast_to(crossing, (8, TILE)), hot)
        gskip = gskip + head_sum(jnp.broadcast_to(skipped, (8, TILE)), hot)
        gb = gb + nt((dtx * w_end).astype(BF16), later_low)
        emit(n, j, (dt * grad + skip_ref[:, own] * e).astype(BF16).astype(F32))
    return gb, q_sum, back_sum, xg, both, gskip


def conv_back(total, grad_act, cols, place, conv_refs, ext_s, cin_s):
    pre_ref, cin_ref, taps_ref, meta_ref, gt_ref = conv_refs
    pre = pre_ref[:, cols].astype(F32)
    sig = sigmoid(pre)
    cin_s[...] = cin_ref[:, cols].astype(F32)
    grad = grad_act * sig * (1.0 + pre * (1.0 - sig))
    gt_ref[KERNEL : KERNEL + 1, place] = jnp.sum(grad, axis=0, keepdims=True)
    ext_s[...] = jnp.zeros_like(ext_s)
    for k in range(KERNEL):
        masked = grad if k == 3 else grad * meta_ref[:, k : k + 1]
        rows = slice(HALO - 3 + k, HALO - 3 + k + total)
        gt_ref[k : k + 1, place] = jnp.sum(masked * cin_s[rows, :], axis=0, keepdims=True)
        ext_s[rows, :] += masked * taps_ref[k : k + 1, cols]
    return ext_s[...].astype(BF16)


def weight_grad(turned, grads, place, keep_ref, send_ref):
    made = nn(turned, grads)
    half = made.shape[0] // 2
    keep_ref[:, place] = made[:half].astype(BF16)
    send_ref[:, place] = made[half:].astype(BF16)


def back_kernel(count, total, last, small, *refs):
    got, refs = refs[:count], refs[count:]
    heads, refs = refs[:8], refs[8:]
    pre_ref, cin_ref, taps_ref, meta_ref, turned_ref = refs[:5]
    refs = refs[5:]
    if last:
        acc_in, few_in, gcs_ref, gcp_ref, gbp_ref, rows_ref, hp_ref = refs[:7]
        refs = refs[7:]
        if small:
            gt_first, gout_ref, tab = refs[:3]
            refs = refs[3:]
    keep_ref, send_ref, proj_ref, gt_ref, acc_ref, few_ref, ext_s, cin_s = refs[:8]
    conv_refs = (pre_ref, cin_ref, taps_ref, meta_ref, gt_ref)
    gt_ref[...] = jnp.zeros_like(gt_ref)
    base = FRONT if last else 0

    def emit(n, j, grad_x):
        place = slice(base + n * TILE, base + (n + 1) * TILE)
        grads = conv_back(total, grad_x, slice(2 * N + j * TILE, 2 * N + (j + 1) * TILE), place, conv_refs, ext_s, cin_s)
        proj_ref[:, place] = grads
        weight_grad(turned_ref[...], grads, place, keep_ref, send_ref)

    tiles = range(P_TILES) if last else range(P_TILES, INNER // TILE)
    if last:
        sums = tuple(acc_in[i] for i in range(4)) + (few_in[0], few_in[1])
    else:
        zero = jnp.zeros((total, N), F32)
        sums = (zero,) * 4 + (jnp.zeros((8, N), F32),) * 2
    gb, q_sum, back_sum, xg, both, gskip = heads_back(count, total, tiles, got, heads, sums, emit)
    if not last:
        acc_ref[0], acc_ref[1], acc_ref[2], acc_ref[3] = gb, q_sum, back_sum, xg
        few_ref[0], few_ref[1] = both, gskip
        return
    hd_ref = heads[6]
    grad_bc = jnp.concatenate([gb + gbp_ref[...], gcs_ref[...] + gcp_ref[...]], axis=1)
    place = slice(128, FRONT)
    proj_ref[:, place] = conv_back(total, grad_bc, slice(0, 2 * N), place, conv_refs, ext_s, cin_s)
    row = lax.broadcasted_iota(jnp.int32, (total, total), 0)
    col = lax.broadcasted_iota(jnp.int32, (total, total), 1)
    upper = (row <= col).astype(F32).astype(BF16)
    below = (row > col).astype(F32).astype(BF16)
    dt, reach, shifted, rate = hd_ref[0], hd_ref[2], hd_ref[4], hp_ref[1:2, :]
    grad_ld = exact_sum(upper, rows_ref[...] - back_sum) + exact_sum(below, q_sum) + both[0:1] * reach[total - 1 : total]
    grad_step = (xg - grad_ld * rate) * meta_ref[:, 3:4] * sigmoid(shifted)
    grad_step = jnp.where(lax.broadcasted_iota(jnp.int32, grad_step.shape, 1) < H, grad_step, 0.0)
    proj_ref[:HALO, :128] = jnp.zeros((HALO, 128), BF16)
    proj_ref[HALO:, :128] = grad_step.astype(BF16)
    few_ref[0] = jnp.broadcast_to(jnp.sum(grad_step, axis=0, keepdims=True), (8, N))
    few_ref[1] = jnp.broadcast_to(jnp.sum(grad_ld * (-dt * rate), axis=0, keepdims=True), (8, N))
    few_ref[2] = gskip
    acc_ref[...] = jnp.zeros_like(acc_ref)
    if not small:
        weight_grad(turned_ref[...], proj_ref[:, :FRONT], slice(0, FRONT), keep_ref, send_ref)
        return
    small_s, front_s, conv_s = refs[8:]
    grad_small(*small, tab, gt_ref, gt_first, gout_ref, few_ref, small_s, conv_s)
    made = nn(turned_ref[...], proj_ref[:, :FRONT])
    front_s[...] = made[:, :128]
    rows = D // small[0]
    for r in range(small[0]):
        front_s[r * rows : r * rows + 8, :] += pltpu.roll(small_s[r], H, 1)
    half = D // 2
    keep_ref[:, :128], send_ref[:, :128] = front_s[:half].astype(BF16), front_s[half:].astype(BF16)
    keep_ref[:, 128:FRONT], send_ref[:, 128:FRONT] = made[:half, 128:].astype(BF16), made[half:, 128:].astype(BF16)


def back_stage(got, heads, conv_refs, turned_rows, more, total, small=()):
    last = bool(more)
    width = P_COLS if last else Q_COLS
    ext = total + HALO
    acc = shape((1, 8, N)) if last else shape((4, total, N))
    scratch = [pltpu.VMEM((ext, TILE), F32)] * 2
    if small:
        scratch += [pltpu.VMEM((small[0], 8, 128), F32), pltpu.VMEM((D, 128), F32), pltpu.VMEM((8, CONV), F32)]
    return pl.pallas_call(
        functools.partial(back_kernel, len(got), total, last, small),
        out_shape=(shape((D // 2, width), BF16), shape((D // 2, width), BF16), shape((ext, width), BF16), shape((8, width)), acc, shape((3 if last else 2, 8, N))),
        in_specs=[VMEM] * (len(got) + 13 + len(more) - bool(small)) + [SMEM] * bool(small),
        out_specs=tuple([VMEM] * 6),
        scratch_shapes=scratch,
        compiler_params=params(),
        cost_estimate=SMALL,
        name="back_last" if last else "back_first",
    )(*got, *heads, *conv_refs, turned_rows, *more)


def normed_kernel(pp_ref, pq_ref, w1_ref, part_ref, out_ref):
    out_ref[...] = nt(pp_ref[:, 128:], w1_ref[:, 128:P_COLS]) + nt(pq_ref[...], w1_ref[:, P_COLS:])
    out_ref[...] += nt(pp_ref[:, :H], w1_ref[:, :H])
    out_ref[HALO:, :] += part_ref[...]


def normed_stage(proj_p, proj_q, w1, part):
    return pl.pallas_call(
        normed_kernel,
        out_shape=shape((proj_p.shape[0], D)),
        in_specs=[VMEM] * 4,
        out_specs=VMEM,
        compiler_params=params(),
        cost_estimate=SMALL,
        name="normed_stage",
    )(proj_p, proj_q, w1, part)


def body(tokens, scene_ids, valid_mask, norm_gain, w_in, conv_w, conv_b, dt_bias, a_log, d_skip, gate_gain, w_out, d_out):
    n_f, n_s = lax.axis_size("fsdp"), lax.axis_size("seq")
    n_dev = n_f * n_s
    s_rank = lax.axis_index("seq")
    lin = lax.axis_index("fsdp") * n_s + s_rank
    rows = tokens.shape[2]
    total, length = MB * rows, n_s * rows
    r_in, r_out = w_in.shape[0], w_out.shape[0]
    f_bits = [n_s << b for b in range(n_f.bit_length() - 1)]
    s_bits = [1 << b for b in range(n_s.bit_length() - 1)]
    n_x = len(f_bits) - 1
    z, x, y = combos(s_bits[n_x:]), combos(s_bits[:n_x]), combos(f_bits[1:])
    xy, core = combos(s_bits[:n_x] + f_bits[1:]), [n_s]
    orders = [order_of([z, x, y, core]), order_of([z, y, x, core]), order_of([z, xy, core])]
    aligned = r_in % 16 == 0
    tables = jnp.asarray(np.stack([np.argsort(o) for o in orders]), jnp.int32)[:, jnp.arange(n_dev) ^ lin]

    inverse3 = pow(3, -1, n_s)
    source = lambda i: [((3 * d + i) % n_s, d) for d in range(n_s)]

    def chosen(arr, i):
        d = (inverse3 * (s_rank - i + n_s)) % n_s
        return lax.select_n((3 * d + i + MB * n_s) // n_s % MB, arr[0, 0], arr[1, 0], arr[2, 0])

    def home(parts):
        return [lax.ppermute(part, "seq", [(d, k) for k, d in source(i)]) for i, part in enumerate(parts)]

    def placed(blocks):
        return jnp.stack([lax.select_n((m * n_s + s_rank) % MB, *blocks) for m in range(MB)])[:, None]

    late = jnp.concatenate([w_in[:, :INNER], jnp.concatenate([w_out[: r_out // 2], w_out[r_out // 2 :]], axis=1)])
    spare = 128 - H
    line = lambda v: jnp.pad(v.astype(F32), ((0, 0), (0, (spare if aligned else 128) - v.shape[1])))
    heads = jnp.concatenate([dt_bias, a_log, d_skip])[None]
    small = jnp.concatenate([line(conv_w), line(conv_b[None]), line(norm_gain[None]), line(gate_gain[None]), line(heads)])
    if aligned:
        pad = jnp.pad(jnp.concatenate(split3(small)), ((0, r_in - 24), (0, 0)))
    else:
        pad = jnp.zeros((r_in, spare), BF16)
    w1 = jnp.concatenate([w_in[:, INNER + CONV :], pad, w_in[:, 2 * INNER : INNER + CONV], w_in[:, INNER : 2 * INNER]], axis=1)

    first = spread(w1[None], z)
    halo = lax.ppermute(chosen(tokens, -1)[rows - HALO :], "seq", source(-1))
    first, halo, tokens, d_out, tables, late = tied(first, halo, tokens, d_out, tables, late)
    tab_small = tables[2]
    tab_p, tab_q = (tables[0], tables[1]) if aligned else (jnp.arange(32, dtype=jnp.int32),) * 2
    p, q = first[..., :P_COLS], first[..., P_COLS:]
    got = [lax.ppermute(chosen(tokens, i), "seq", source(i)) for i in range(MB)]
    picked = [chosen(d_out, i) for i in range(MB)]
    p, q, picked, *got = tied(spread(p, x), spread(q, y), picked, *got)
    g = [lax.ppermute(picked[i], "seq", source(i)) for i in range(MB)]
    ids = (scene_ids[:, 0] + 8 * jnp.arange(MB, dtype=jnp.int32)[:, None]).reshape(1, -1)
    lines = jnp.concatenate([jnp.pad(ids, ((0, 0), (HALO, 0)), constant_values=-1), jnp.pad(valid_mask[:, 0].reshape(1, -1), ((0, 0), (HALO, 0)))])
    lines = lax.dynamic_slice_in_dim(lines, s_rank * total, total + HALO, axis=1)
    lines = jnp.pad(lines.astype(F32), ((0, 6), (0, -(total + HALO) % 128)))
    p, q, lines, *g = tied(spread(p, y), spread(q, x), lines, *g)
    p_other, q_other = permute(p, n_s), permute(q, n_s)
    if aligned:
        small = jnp.concatenate([p[:, :, :128], p_other[:, :, :128]])
        tab_small = tab_p
    else:
        small = jnp.pad(small, ((0, 8 - small.shape[0]), (0, 0)))[None]
        for stage in (z, xy, core):
            small = spread(small, stage)
    taps, gain_in, gain_out, hp, skip_wide, meta, id_col, id_row = small_stage(tab_small, small, lines, n_dev, n_s, total)

    late = lax.all_gather(late, BOTH, axis=0, tiled=True).reshape(n_dev, 2, r_in, INNER)
    if not aligned:
        wg = late[:, 0].reshape(32, D // 32, INNER)
        wo = late[:, 1].reshape(n_dev, r_in, 2, D).transpose(0, 2, 1, 3).reshape(32, 2, D // 32, D)
        late = jnp.stack([wg, wo.transpose(0, 2, 1, 3).reshape(32, D // 32, INNER)], axis=1)

    def pieces(own, other, which):
        if aligned:
            return own, other, orders[which], lin[None]
        both = jnp.concatenate([own, other])[tables[which]]
        both = both.reshape(32, D // 32, both.shape[2])
        return both[:16], both[16:], np.arange(32), jnp.zeros((1,), jnp.int32)

    w1_full, normed, conv_in, conv_pre, bc, x_part, dtx, hd, cumt, pay = first_stage(
        (halo, *got), gain_in, meta, taps, hp, pieces(p, p_other, 0), pieces(q, q_other, 1), total
    )

    def spans(k):
        return [d for d in range(n_s - k) if ((d + 1) * total - 1) // length == (d + k) * total // length]

    far = max(k for k in range(1, n_s) if spans(k))
    pay, normed, dtx, cumt = tied(pay, normed, dtx, cumt)
    before = [lax.ppermute(pay, "seq", [(d, d + k) for d in spans(k)]) for k in range(1, far + 1)]
    normed_p, normed_q = turn_stage(tab_p, tab_q, normed)
    inside = pairs_stage(bc, dtx, cumt, id_col, id_row, total)
    g = jnp.concatenate(g)
    ga, dga, gno = gate_stage(normed, g, late, total)
    inside, normed_p, normed_q, gno, *before = tied(inside, normed_p, normed_q, gno, *before)
    state_in, normed_out, e, grad_gate, pay_back, gc_state, row_sum, grad_gain_out = output_stage(
        before, inside, bc, x_part, hd, ga, dga, gno, gain_out, skip_wide, pay, total
    )

    adjoints = [None if k == 2 else lax.ppermute(pay_back, "seq", [(d + k, d) for d in spans(k)]) for k in range(1, far + 1)]

    def sent(keep, send, which):
        if aligned:
            return keep, send
        both = jnp.concatenate([keep, send])
        both = both.reshape(n_dev, -1, both.shape[1])[jnp.asarray(orders[which]) ^ lin].reshape(both.shape)
        return both[: keep.shape[0]], both[keep.shape[0] :]

    ext_tok = jnp.concatenate([halo] + got)
    blocks = lambda v: v.reshape(n_dev // 2, -1, v.shape[1])
    keep_g, send_g, keep_o, send_o = weights_stage(tab_q, normed_p, grad_gate, normed_out, g, total)
    gdtx, gb_pairs, gc_pairs = pairs_back_stage(bc, dtx, e, cumt, id_col, id_row, total)
    rg, ro = sent(keep_g, send_g, 0), sent(keep_o, send_o, 1)
    (rg, ro), gdtx, gb_pairs, gc_pairs, normed_out, pay_back, near, *more = tied(
        (rg, ro), gdtx, gb_pairs, gc_pairs, normed_out, pay_back, adjoints[0], *adjoints[2:]
    )
    adjoints = [near] + [lax.ppermute(pay_back, "seq", [(d + 2, d) for d in spans(2)])] + more
    block_out, part = rest_stage(normed_out, grad_gate, ext_tok, late, total)
    rg, ro = cut(blocks(fold(rg, core)), y), cut(blocks(fold(ro, core)), x)
    (rg, ro), gdtx, block_out, part, *adjoints = tied((rg, ro), gdtx, block_out, part, *adjoints)

    conv_refs = (conv_pre, conv_in, taps, meta)
    head_refs = (gdtx, e, x_part, dtx, bc, state_in, hd, skip_wide)
    keep_q, send_q, proj_q, gt_q, acc, few = back_stage(adjoints, head_refs, conv_refs, normed_q, (), total)
    rg, ro = cut(fold(rg, y), x), cut(fold(ro, x), y)
    thirds = lambda v: [v[i * rows : (i + 1) * rows] for i in range(MB)]
    block_out = home(thirds(block_out))
    rq = sent(keep_q, send_q, 1)
    (rg, ro, rq), proj_q, gt_q, acc, few, block_out = tied((rg, ro, rq), proj_q, gt_q, acc, few, block_out)

    more = (acc, few, gc_state, gc_pairs, gb_pairs, row_sum, hp) + ((gt_q, grad_gain_out, tab_p) if aligned else ())
    keep_p, send_p, proj_p, gt_p, _, few = back_stage(
        adjoints, head_refs, conv_refs, normed_p, more, total, (n_dev, n_s) if aligned else ()
    )
    rg, ro = fold(rg, x), fold(ro, y)
    ro = jnp.concatenate([ro[:, : r_out // 2], ro[:, r_out // 2 :]], axis=2)
    both = cut(jnp.stack([rg, ro], axis=1), z)
    rp = sent(keep_p, send_p, 0)
    (both, rq, rp), proj_p, gt_p, few, block_out = tied((both, rq, rp), proj_p, gt_p, few, block_out)

    grad_normed = normed_stage(proj_p, proj_q, w1_full, part)
    both = fold(both, z, F32)[0]
    rp, rq = cut(blocks(fold(rp, core)), y), cut(blocks(fold(rq, core)), x)
    (rp, rq), both, grad_normed = tied((rp, rq), both, grad_normed)
    rim = lax.ppermute(grad_normed[:HALO], "seq", [(d + 1, d) for d in range(n_s - 1)])
    rp, rq = cut(fold(rp, y), x), cut(fold(rq, x), y)
    (rp, rq), rim, grad_normed = tied((rp, rq), rim, grad_normed)
    own = grad_normed[HALO:]
    own = jnp.concatenate([own[: total - HALO], own[total - HALO :] + rim])
    u = ext_tok[HALO:].astype(F32)
    in_scale = lax.rsqrt(jnp.mean(u * u, axis=-1, keepdims=True) + EPS)
    unit, q_in = u * in_scale, own * gain_in
    grad_in = (g.astype(F32) + in_scale * (q_in - unit * jnp.mean(q_in * unit, axis=-1, keepdims=True))).astype(BF16)
    grad_in = home(thirds(grad_in))
    w1_grad = cut(jnp.concatenate([fold(rp, x), fold(rq, y)], axis=2), z)
    w1_grad, grad_in, block_out = tied(w1_grad, grad_in, block_out)
    w1_grad = fold(w1_grad, z, F32)[0]
    if aligned:
        small = w1_grad[:8, H:128]
    else:
        small = grad_small_stage(tab_small, gt_p, gt_q, grad_gain_out, few, n_dev, n_s)
        for stage in (core, xy, z):
            small = fold(cut(small, stage), stage, F32)
        small = small[0]
    block_out, grad_in = placed(block_out), placed(grad_in)
    out_wo = jnp.concatenate([both[1, :, :D], both[1, :, D:]], axis=0)
    out_win = jnp.concatenate([both[0], w1_grad[:, FRONT:], w1_grad[:, 128:FRONT], w1_grad[:, :H]], axis=1)
    grad_gain = jnp.sum(out_win * w_in.astype(F32), axis=1) / norm_gain.astype(F32)
    count = dt_bias.shape[0]
    head = lambda k: small[7, k * count : (k + 1) * count]
    return (
        block_out, grad_in, grad_gain, out_win, small[:KERNEL, : conv_b.shape[0]], small[KERNEL, : conv_b.shape[0]],
        head(0), head(1), head(2), small[6, :r_out], out_wo,
    )


def solution(mesh):
    tok = P(None, "fsdp", "seq", None)
    row = P(None, "fsdp", None)
    specs = (tok, row, row, P(BOTH), P(BOTH, None), P(None, BOTH), P(BOTH), P("seq"), P("seq"), P("seq"), P(BOTH), P(BOTH, None), tok)
    outs = (tok, tok, P(BOTH), P(BOTH, None), P(None, BOTH), P(BOTH), P("seq"), P("seq"), P("seq"), P(BOTH), P(BOTH, None))
    return jax.shard_map(body, mesh=mesh, in_specs=specs, out_specs=outs, check_vma=False)
```

time: 1960 us -> 359 us (0.18)
  waiting for transfers between devices: 519 us -> 97.8 us
  other arithmetic: 378 us -> 21 us
  local copies, waits for them, and re-layouts: 359 us -> 24.7 us
  blocking collectives: 289 us -> 0 us
  matrix products: 283 us -> 0 us
  Pallas kernels: 0 us -> 100 us
    reduce_scatter x2 -> x0, waiting for transfers between devices: 396 us -> none  [the longest x1 394 us: body(): lax.psum_scatter(total_win, ('fsdp', 'seq'), scatter_dimension=0, tiled=T...]
    dot_general x186 -> x0, matrix products: 283 us -> none  [the longest x36 58.8 us: span_step(): jnp.einsum('hts,shp->thp', decay_in * intersection[None], scaled, precisi...]
    all_gather x4 -> x0, blocking collectives: 163 us -> none  [the longest x3 96.4 us: body(): bc_all = lax.all_gather(bc_low, 'seq', axis=0, tiled=True)]
    another operation x116 -> x5, other arithmetic: 161 us -> 1.34 us  [the longest x3 1.17 us: body(): both = cut(jnp.stack([rg, ro], axis=1), z)]
    pallas_call x0 -> x12, Pallas kernels: none -> 100 us  [the longest x2 26.8 us: back_stage(): pl.pallas_call(functools.partial(back_kernel, len(got), total, last, smal...]
    ppermute x6 -> x47, waiting for transfers between devices: 4.9 us -> 97.8 us  [the longest x27 70.6 us: permute(): return lax.ppermute(block, BOTH, [(i, i ^ mask) for i in range(size)])]
    unnamed x2 -> x0, blocking collectives: 90.1 us -> none
    ppermute x6 -> x47, starting transfers between devices: 16.5 us -> 96.1 us  [the longest x27 37.3 us: permute(): return lax.ppermute(block, BOTH, [(i, i ^ mask) for i in range(size)])]
  transfers between devices with their start and end apart: 29 -> 48, of which waited for: 14 -> 17; matrix products, arithmetic and copies ran while one was open for 16% -> 5% of each run, Pallas kernels for 0% -> 25%
where the time goes in v1:
time: 359 us; the launch traced here: 356 us
  Pallas kernels  100 us (28%)
  waiting for transfers between devices  97.8 us (27%)
  starting transfers between devices  96.2 us (27%)
  local copies, waits for them, and re-layouts  24.7 us (7%)
  other arithmetic  21 us (6%)
  between operations  15.9 us (4%)
    ppermute x27, waiting for transfers between devices, permute(): return lax.ppermute(block, BOTH, [(i, i ^ mask) for i in range(size)])  70.6 us
    ppermute x27, starting transfers between devices, permute(): return lax.ppermute(block, BOTH, [(i, i ^ mask) for i in range(size)])  37.3 us
    pallas_call x2, Pallas kernels, back_stage(): pl.pallas_call(functools.partial(back_kernel, len(got), total, last, smal...  26.8 us
    ppermute x6, starting transfers between devices, home(): lax.ppermute(part, 'seq', [(d, k) for k, d in source(i)])  20.1 us
    ppermute x3, waiting for transfers between devices, body(): got = [lax.ppermute(chosen(tokens, i), 'seq', source(i)) for i in range(MB)]  16.6 us
    unnamed x132, local copies, waits for them, and re-layouts  15.5 us
    pallas_call x1, Pallas kernels, first_stage(): pl.pallas_call(functools.partial(first_kernel, masks_p, masks_q, total),...  13.5 us
    pallas_call x1, Pallas kernels, output_stage(): pl.pallas_call(functools.partial(output_kernel, count, total), out_shape=...  11.6 us
  transfers between devices with their start and end apart: 48, of which 17 were waited for; matrix products, arithmetic and copies ran while one was open for 5% of the time, Pallas kernels for 25%

profile of v1, /device:TPU:0, one launch (start us, length us, event | category | flops | bytes accessed | tf_op | source)
XLA Modules:
  0.0 356.0 jit_solution(17447418646787750581)
XLA Ops:
  12.6 5.1 %collective-permute-start.2 = (bf16[1,32,2432]{2,1,0:T(8,128)(2,1)S(1)}, bf16[1,32,2432]{2,1,0:T(8,128)(2,1)S(1)}, u32[]{:S(2)}, u32[]{:S(2)}) collective-permute-start(bf16[1,32,2432]{2,1,0:T(8,128)(2,1)S(1)} %bitcast.95), channel_id=1, source_target_pairs={{0,6},{1,7},{2,4},{3,5},{4,2},{5,3},{6,0},{7,1},{8,14},{9,15},{10,... | collective-permute-start | bytes 466952 | tf_op jit(solution)/shard_map/ppermute | solution.py:48
  23.3 7.6 %collective-permute-done.1 = bf16[1,32,2432]{2,1,0:T(8,128)(2,1)S(1)} collective-permute-done((bf16[1,32,2432]{2,1,0:T(8,128)(2,1)S(1)}, bf16[1,32,2432]{2,1,0:T(8,128)(2,1)S(1)}, u32[]{:S(2)}, u32[]{:S(2)}) %collective-permute-start.1) | collective-permute-done | bytes 155680 | tf_op jit(solution)/shard_map/ppermute | solution.py:48
  37.1 4.0 %collective-permute-start.7 = (bf16[128,1024]{1,0:T(8,128)(2,1)S(1)}, bf16[128,1024]{1,0:T(8,128)(2,1)S(1)}, u32[]{:S(2)}, u32[]{:S(2)}) collective-permute-start(bf16[128,1024]{1,0:T(8,128)(2,1)S(1)} %get-tuple-element.363), channel_id=1, source_target_pairs={{1,0},{4,1},{7,2},{2,3},{5,4},{0,5},{3,6},{6,7},{9,8},{12,9},{15,1... | collective-permute-start | bytes 786440 | tf_op jit(solution)/shard_map/ppermute | solution.py:857
  43.5 7.9 %collective-permute-done.7.t1_ref = bf16[128,1024]{1,0:T(8,128)(2,1)S(1)} collective-permute-done((bf16[128,1024]{1,0:T(8,128)(2,1)S(1)}, bf16[128,1024]{1,0:T(8,128)(2,1)S(1)}, u32[]{:S(2)}, u32[]{:S(2)}) %collective-permute-start.7) | collective-permute-done | bytes 262176 | tf_op jit(solution)/shard_map/ppermute | solution.py:857
  51.4 8.7 %collective-permute-done.8.t2_ref = bf16[128,1024]{1,0:T(8,128)(2,1)S(1)} collective-permute-done((bf16[128,1024]{1,0:T(8,128)(2,1)S(1)}, bf16[128,1024]{1,0:T(8,128)(2,1)S(1)}, u32[]{:S(2)}, u32[]{:S(2)}) %collective-permute-start.8) | collective-permute-done | bytes 262176 | tf_op jit(solution)/shard_map/ppermute | solution.py:857
  65.4 3.6 %collective-permute-start.13 = (bf16[128,1024]{1,0:T(8,128)(2,1)}, bf16[128,1024]{1,0:T(8,128)(2,1)S(1)}, u32[]{:S(2)}, u32[]{:S(2)}) collective-permute-start(bf16[128,1024]{1,0:T(8,128)(2,1)} %get-tuple-element.171), channel_id=1, source_target_pairs={{2,0},{5,1},{0,2},{3,3},{6,4},{1,5},{4,6},{7,7},{10,8},{13,9},{8,1... | collective-permute-start | bytes 786440 | tf_op jit(solution)/shard_map/ppermute | solution.py:860
  69.0 8.8 %collective-permute-done.9 = bf16[8,32,1152]{2,1,0:T(8,128)(2,1)S(1)} collective-permute-done((bf16[8,32,1152]{2,1,0:T(8,128)(2,1)S(1)}, bf16[8,32,1152]{2,1,0:T(8,128)(2,1)S(1)}, u32[]{:S(2)}, u32[]{:S(2)}) %collective-permute-start.9) | collective-permute-done | bytes 589856 | tf_op jit(solution)/shard_map/ppermute | solution.py:48
  77.9 9.0 %collective-permute-done.10 = bf16[8,32,1280]{2,1,0:T(8,128)(2,1)S(1)} collective-permute-done((bf16[8,32,1280]{2,1,0:T(8,128)(2,1)S(1)}, bf16[8,32,1280]{2,1,0:T(8,128)(2,1)S(1)}, u32[]{:S(2)}, u32[]{:S(2)}) %collective-permute-start.10) | collective-permute-done | bytes 655392 | tf_op jit(solution)/shard_map/ppermute | solution.py:48
  89.2 4.0 %collective-permute-done.14.px = bf16[16,32,1152]{2,1,0:T(8,128)(2,1)S(1)} collective-permute-done((bf16[16,32,1152]{2,1,0:T(8,128)(2,1)S(1)}, bf16[16,32,1152]{2,1,0:T(8,128)(2,1)S(1)}, u32[]{:S(2)}, u32[]{:S(2)}) %collective-permute-start.14) | collective-permute-done | bytes 1179680 | tf_op jit(solution)/shard_map/ppermute | solution.py:48
  96.4 13.5 %first_stage.1 = (bf16[1024,2432]{1,0:T(8,128)(2,1)}, bf16[400,1024]{1,0:T(8,128)(2,1)S(1)}, bf16[400,2304]{1,0:T(8,128)(2,1)}, bf16[384,2304]{1,0:T(8,128)(2,1)...) custom-call(s32[1]{0:T(128)} %bitcast.8.lin_ref, ...), custom_call_target="tpu_custom_call" | custom-call | flops 1 | bytes 1 | tf_op jit(solution)/shard_map/first_stage/pallas_call | solution.py:349
  110.6 4.2 %collective-permute-start.16 = (bf16[144,2048]{1,0:T(8,128)(2,1)}, bf16[144,2048]{1,0:T(8,128)(2,1)}, u32[]{:S(2)}, u32[]{:S(2)}) collective-permute-start(bf16[144,2048]{1,0:T(8,128)(2,1)} %get-tuple-element.196.refs_12_), channel_id=1, source_target_pairs={{0,1},{1,2},{2,3},{3,4},{4,5},{5,6},{6,7},{8,9},{9,10},{10,11},{11... | collective-permute-start | bytes 1769480 | tf_op jit(solution)/shard_map/ppermute | solution.py:898
  121.8 4.9 %pairs_stage.1.refs_3_ = f32[384,2048]{1,0:T(8,128)S(1)} custom-call(bf16[384,256]{1,0:T(8,128)(2,1)S(1)} %get-tuple-element.179.bc_ref.refs_4_.refs_7_, bf16[384,2048]{1,0:T(8,128)(2,1)S(1)} %copy-done, f32[32,384]{1,0:T(8,128)S(1)} %get-tuple-element.185.cumt_ref, f32[384,1]{1,0:T(8,128)S(1)} %get-tuple-element.186.id_col, ...), custom_call_target="tpu_custom_call" | custom-call | flops 1 | bytes 1 | tf_op jit(solution)/shard_map/pairs_stage/pallas_call | solution.py:442
  129.5 10.1 %gate_stage.1 = (bf16[384,2048]{1,0:T(8,128)(2,1)S(1)}, bf16[384,2048]{1,0:T(8,128)(2,1)S(1)}, bf16[384,2048]{1,0:T(8,128)(2,1)}) custom-call(bf16[400,1024]{1,0:T(8,128)(2,1)S(1)} %copy-done.15, bf16[384,1024]{1,0:T(8,128)(2,1)S(1)} %constant_dynamic-update-slice_fusion.g_ref, bf16[32,2,32,2048]{3,2,1,0:T(8,128)(2,1)} %bitcast.87), custom_call_target="tpu_custom_call" | custom-call | flops 1 | bytes 1 | tf_op jit(solution)/shard_map/gate_stage/pallas_call | solution.py:403
  142.1 11.6 %output_stage.1 = (bf16[128,2048]{1,0:T(8,128)(2,1)S(1)}, bf16[384,2048]{1,0:T(8,128)(2,1)}, bf16[384,2048]{1,0:T(8,128)(2,1)}, bf16[384,2048]{1,0:T(8,128)(2,1)...) custom-call(bf16[144,2048]{1,0:T(8,128)(2,1)} %collective-permute-don, ...), custom_call_target="tpu_custom_call" | custom-call | flops 1 | bytes 1 | tf_op jit(solution)/shard_map/output_stage/pallas_call | solution.py:562
  155.0 10.0 %collective-permute-start.20 = (bf16[144,2048]{1,0:T(8,128)(2,1)S(1)}, bf16[144,2048]{1,0:T(8,128)(2,1)S(1)}, u32[]{:S(2)}, u32[]{:S(2)}) collective-permute-start(bf16[144,2048]{1,0:T(8,128)(2,1)S(1)} %get-tuple-element.229), channel_id=1, source_target_pairs={{5,2},{13,10},{21,18},{29,26}} | collective-permute-start | bytes 1769480 | tf_op jit(solution)/shard_map/ppermute | solution.py:908
  166.5 8.7 %pairs_back_stage.1 = (f32[384,2048]{1,0:T(8,128)}, f32[384,128]{1,0:T(8,128)S(1)}, f32[384,128]{1,0:T(8,128)S(1)}) custom-call(bf16[384,256]{1,0:T(8,128)(2,1)S(1)} %get-tuple-element.179.bc_ref.refs_4_.refs_7_, bf16[384,2048]{1,0:T(8,128)(2,1)S(1)} %copy-done, bf16[384,2048]{1,0:T(8,128)(2,1)S(1)} %copy-done.1, f32[32,384]{1,0:T(8,128)S(1)} %copy-done.32, ...), custom_call_target="tpu_custom_call" | custom-call | flops 1 | bytes 1 | tf_op jit(solution)/shard_map/pairs_back_stage/pallas_call | solution.py:490
  175.2 7.7 %weights_stage.1 = (bf16[512,2048]{1,0:T(8,128)(2,1)}, bf16[512,2048]{1,0:T(8,128)(2,1)}, bf16[1024,1024]{1,0:T(8,128)(2,1)}, bf16[1024,1024]{1,0:T(8,128)(2,1)}) custom-call(s32[32]{0:T(128)S(1)} %copy-done.42, bf16[1024,400]{1,0:T(8,128)(2,1)S(1)} %copy-done.13, bf16[384,2048]{1,0:T(8,128)(2,1)S(1)} %copy-done.11, bf16[384,2048]{1,0:T(8,128)(2,1)S(1)} %copy-done.10, ...), custom_call_target="tpu_custom_call" | custom-call | flops 1 | bytes 1 | tf_op jit(solution)/shard_map/weights_stage/pallas_call | solution.py:614
  184.9 9.5 %rest_stage.1 = (bf16[384,1024]{1,0:T(8,128)(2,1)S(1)}, f32[384,1024]{1,0:T(8,128)S(1)}) custom-call(bf16[384,2048]{1,0:T(8,128)(2,1)S(1)} %copy-done.10, bf16[384,2048]{1,0:T(8,128)(2,1)} %get-tuple-element.209.gg_ref, bf16[400,1024]{1,0:T(8,128)(2,1)S(1)} %pad_maximum_fusion.2.tok_ref, bf16[32,2,32,2048]{3,2,1,0:T(8,128)(2,1)} %bitcast.88), custom_call_target="tpu_custom_call" | custom-call | flops 1 | bytes 1 | tf_op jit(solution)/shard_map/rest_stage/pallas_call | solution.py:643
  201.5 5.0 %collective-permute-done.23.refs_1_ = bf16[144,2048]{1,0:T(8,128)(2,1)S(1)} collective-permute-done((bf16[144,2048]{1,0:T(8,128)(2,1)S(1)}, bf16[144,2048]{1,0:T(8,128)(2,1)S(1)}, u32[]{:S(2)}, u32[]{:S(2)}) %collective-permute-start.23) | collective-permute-done | bytes 589856 | tf_op jit(solution)/shard_map/ppermute | solution.py:925
  208.7 6.3 %collective-permute-start.27 = (bf16[128,1024]{1,0:T(8,128)(2,1)S(1)}, bf16[128,1024]{1,0:T(8,128)(2,1)S(1)}, u32[]{:S(2)}, u32[]{:S(2)}) collective-permute-start(bf16[128,1024]{1,0:T(8,128)(2,1)S(1)} %get-tuple-element.359), channel_id=1, source_target_pairs={{0,1},{1,4},{2,7},{3,2},{4,5},{5,0},{6,3},{7,6},{8,9},{9,12},{10,1... | collective-permute-start | bytes 786440 | tf_op jit(solution)/shard_map/ppermute | solution.py:835
  215.0 5.7 %collective-permute-start.28 = (bf16[128,1024]{1,0:T(8,128)(2,1)S(1)}, bf16[128,1024]{1,0:T(8,128)(2,1)S(1)}, u32[]{:S(2)}, u32[]{:S(2)}) collective-permute-start(bf16[128,1024]{1,0:T(8,128)(2,1)S(1)} %get-tuple-element.358), channel_id=1, source_target_pairs={{0,2},{1,5},{2,0},{3,3},{4,6},{5,1},{6,4},{7,7},{8,10},{9,13},{10,... | collective-permute-start | bytes 786440 | tf_op jit(solution)/shard_map/ppermute | solution.py:835
  220.8 14.0 %back_first.1 = (bf16[512,1280]{1,0:T(8,128)(2,1)}, bf16[512,1280]{1,0:T(8,128)(2,1)}, bf16[400,1280]{1,0:T(8,128)(2,1)S(1)}, f32[8,1280]{1,0:T(8,128)S(1)}, f32...) custom-call(bf16[144,2048]{1,0:T(8,128)(2,1)S(1)} %collective-permute-done.19.refs_0_, ...), custom_call_target="tpu_custom_call" | custom-call | flops 1 | bytes 1 | tf_op jit(solution)/shard_map/back_first/pallas_call | solution.py:780
  239.5 12.8 %back_last.1 = (bf16[512,1152]{1,0:T(8,128)(2,1)}, bf16[512,1152]{1,0:T(8,128)(2,1)}, bf16[400,1152]{1,0:T(8,128)(2,1)S(1)}, f32[8,1152]{1,0:T(8,128)}, f32[1,8,128]{2,1,0:T(8,128)}, /*index=5*/f32[3,8,128]{2,1,0:T(8,128)}) custom-call(bf16[144,2048]{1,0:T(8,128)(2,1)S(1)} %collective-permute-done.19.refs_0_, ...), custom_call_target="tpu_custom_call" | custom-call | flops 1 | bytes 1 | tf_op jit(solution)/shard_map/back_last/pallas_call | solution.py:780
  254.4 8.2 %collective-permute-start.35 = (bf16[1,2,32,2048]{3,2,1,0:T(8,128)(2,1)}, bf16[1,2,32,2048]{3,2,1,0:T(8,128)(2,1)S(1)}, u32[]{:S(2)}, u32[]{:S(2)}) collective-permute-start(bf16[1,2,32,2048]{3,2,1,0:T(8,128)(2,1)} %get-tuple-element.277), channel_id=1, source_target_pairs={{0,6},{1,7},{2,4},{3,5},{4,2},{5,3},{6,0},{7,1},{8,14},{9,15},{10,... | collective-permute-start | bytes 786440 | tf_op jit(solution)/shard_map/ppermute | solution.py:48
  265.9 4.8 %normed_stage.1 = f32[400,1024]{1,0:T(8,128)S(1)} custom-call(bf16[400,1152]{1,0:T(8,128)(2,1)S(1)} %copy-done.26, bf16[400,1280]{1,0:T(8,128)(2,1)S(1)} %copy-done.24, bf16[1024,2432]{1,0:T(8,128)(2,1)} %get-tuple-element.280.w1_ref, f32[384,1024]{1,0:T(8,128)S(1)} %copy-done.21), custom_call_target="tpu_custom_call" | custom-call | flops 1 | bytes 1 | tf_op jit(solution)/shard_map/normed_stage/pallas_call | solution.py:799
  270.7 14.2 %collective-permute-done.34 = bf16[1,2,32,2048]{3,2,1,0:T(8,128)(2,1)S(1)} collective-permute-done((bf16[1,2,32,2048]{3,2,1,0:T(8,128)(2,1)}, bf16[1,2,32,2048]{3,2,1,0:T(8,128)(2,1)S(1)}, u32[]{:S(2)}, u32[]{:S(2)}) %collective-permute-start.34) | collective-permute-done | bytes 262176 | tf_op jit(solution)/shard_map/ppermute | solution.py:48
  292.8 10.8 %collective-permute-done.36 = bf16[8,32,1152]{2,1,0:T(8,128)(2,1)S(1)} collective-permute-done((bf16[8,32,1152]{2,1,0:T(8,128)(2,1)S(1)}, bf16[8,32,1152]{2,1,0:T(8,128)(2,1)S(1)}, u32[]{:S(2)}, u32[]{:S(2)}) %collective-permute-start.36) | collective-permute-done | bytes 589856 | tf_op jit(solution)/shard_map/ppermute | solution.py:48
  303.8 3.1 collective-permute-done.37
  313.4 4.3 %collective-permute-start.43 = (bf16[128,1024]{1,0:T(8,128)(2,1)S(1)}, bf16[128,1024]{1,0:T(8,128)(2,1)S(1)}, u32[]{:S(2)}, u32[]{:S(2)}) collective-permute-start(bf16[128,1024]{1,0:T(8,128)(2,1)S(1)} %get-tuple-element.355), channel_id=1, source_target_pairs={{0,2},{1,5},{2,0},{3,3},{4,6},{5,1},{6,4},{7,7},{8,10},{9,13},{10,... | collective-permute-start | bytes 786440 | tf_op jit(solution)/shard_map/ppermute | solution.py:835
  319.3 3.7 %collective-permute-done.42 = bf16[128,1024]{1,0:T(8,128)(2,1)S(1)} collective-permute-done((bf16[128,1024]{1,0:T(8,128)(2,1)S(1)}, bf16[128,1024]{1,0:T(8,128)(2,1)S(1)}, u32[]{:S(2)}, u32[]{:S(2)}) %collective-permute-start.42) | collective-permute-done | bytes 262176 | tf_op jit(solution)/shard_map/ppermute | solution.py:835
  322.9 9.4 %collective-permute-start.46 = (bf16[1,32,2432]{2,1,0:T(8,128)(2,1)S(1)}, bf16[1,32,2432]{2,1,0:T(8,128)(2,1)S(1)}, u32[]{:S(2)}, u32[]{:S(2)}) collective-permute-start(bf16[1,32,2432]{2,1,0:T(8,128)(2,1)S(1)} %get-tuple-element.306), channel_id=1, source_target_pairs={{0,6},{1,7},{2,4},{3,5},{4,2},{5,3},{6,0},{7,1},{8,14},{9,15},{10,... | collective-permute-start | bytes 466952 | tf_op jit(solution)/shard_map/ppermute | solution.py:48
  337.3 7.4 %collective-permute-done.45 = bf16[1,32,2432]{2,1,0:T(8,128)(2,1)S(1)} collective-permute-done((bf16[1,32,2432]{2,1,0:T(8,128)(2,1)S(1)}, bf16[1,32,2432]{2,1,0:T(8,128)(2,1)S(1)}, u32[]{:S(2)}, u32[]{:S(2)}) %collective-permute-start.45) | collective-permute-done | bytes 155680 | tf_op jit(solution)/shard_map/ppermute | solution.py:48
  (300 shorter events, 91.5 us)
Async XLA Ops:
  7.2 121.2 %all-gather.2.cloned.1.call-start = ((), (), s32[]{:S(2)}) async-start(), calls=%async_computation | async-start | bytes 8650752 | tf_op jit(solution)/shard_map/all_gather | solution.py:876
  17.7 13.2 %collective-permute-start.1 = (bf16[1,32,2432]{2,1,0:T(8,128)(2,1)S(1)}, bf16[1,32,2432]{2,1,0:T(8,128)(2,1)S(1)}, u32[]{:S(2)}, u32[]{:S(2)}) collective-permute-start(bf16[1,32,2432]{2,1,0:T(8,128)(2,1)S(1)} %bitcast.96), channel_id=1, source_target_pairs={{0,4},{1,5},{2,6},{3,7},{4,0},{5,1},{6,2},{7,3},{8,12},{9,13},{10,... | collective-permute-start | bytes 466952 | tf_op jit(solution)/shard_map/ppermute | solution.py:48
  37.1 14.4 %collective-permute-start.7 = (bf16[128,1024]{1,0:T(8,128)(2,1)S(1)}, bf16[128,1024]{1,0:T(8,128)(2,1)S(1)}, u32[]{:S(2)}, u32[]{:S(2)}) collective-permute-start(bf16[128,1024]{1,0:T(8,128)(2,1)S(1)} %get-tuple-element.363), channel_id=1, source_target_pairs={{1,0},{4,1},{7,2},{2,3},{5,4},{0,5},{3,6},{6,7},{9,8},{12,9},{15,1... | collective-permute-start | bytes 786440 | tf_op jit(solution)/shard_map/ppermute | solution.py:857
  41.1 19.0 %collective-permute-start.8 = (bf16[128,1024]{1,0:T(8,128)(2,1)S(1)}, bf16[128,1024]{1,0:T(8,128)(2,1)S(1)}, u32[]{:S(2)}, u32[]{:S(2)}) collective-permute-start(bf16[128,1024]{1,0:T(8,128)(2,1)S(1)} %get-tuple-element.361), channel_id=1, source_target_pairs={{2,0},{5,1},{0,2},{3,3},{6,4},{1,5},{4,6},{7,7},{10,8},{13,9},{8,1... | collective-permute-start | bytes 786440 | tf_op jit(solution)/shard_map/ppermute | solution.py:857
  60.1 17.7 %collective-permute-start.9 = (bf16[8,32,1152]{2,1,0:T(8,128)(2,1)S(1)}, bf16[8,32,1152]{2,1,0:T(8,128)(2,1)S(1)}, u32[]{:S(2)}, u32[]{:S(2)}) collective-permute-start(bf16[8,32,1152]{2,1,0:T(8,128)(2,1)S(1)} %pad_maximum_fusion.6), channel_id=1, source_target_pairs={{0,16},{1,17},{2,18},{3,19},{4,20},{5,21},{6,22},{7,23},{8,24},{9,... | collective-permute-start | bytes 1769480 | tf_op jit(solution)/shard_map/ppermute | solution.py:48
  60.6 26.3 %collective-permute-start.10 = (bf16[8,32,1280]{2,1,0:T(8,128)(2,1)S(1)}, bf16[8,32,1280]{2,1,0:T(8,128)(2,1)S(1)}, u32[]{:S(2)}, u32[]{:S(2)}) collective-permute-start(bf16[8,32,1280]{2,1,0:T(8,128)(2,1)S(1)} %pad_maximum_fusion.4), channel_id=1, source_target_pairs={{0,1},{1,0},{2,3},{3,2},{4,5},{5,4},{6,7},{7,6},{8,9},{9,8},{10,11... | collective-permute-start | bytes 1966088 | tf_op jit(solution)/shard_map/ppermute | solution.py:48
  61.6 25.5 %collective-permute-start.11 = (bf16[128,1024]{1,0:T(8,128)(2,1)}, bf16[128,1024]{1,0:T(8,128)(2,1)S(1)}, u32[]{:S(2)}, u32[]{:S(2)}) collective-permute-start(bf16[128,1024]{1,0:T(8,128)(2,1)} %get-tuple-element.169), channel_id=1, source_target_pairs={{0,0},{3,1},{6,2},{1,3},{4,4},{7,5},{2,6},{5,7},{8,8},{11,9},{14,1... | collective-permute-start | bytes 786440 | tf_op jit(solution)/shard_map/ppermute | solution.py:860
  63.3 25.2 %collective-permute-start.12 = (bf16[128,1024]{1,0:T(8,128)(2,1)}, bf16[128,1024]{1,0:T(8,128)(2,1)S(1)}, u32[]{:S(2)}, u32[]{:S(2)}) collective-permute-start(bf16[128,1024]{1,0:T(8,128)(2,1)} %get-tuple-element.170), channel_id=1, source_target_pairs={{1,0},{4,1},{7,2},{2,3},{5,4},{0,5},{3,6},{6,7},{9,8},{12,9},{15,1... | collective-permute-start | bytes 786440 | tf_op jit(solution)/shard_map/ppermute | solution.py:860
  65.4 23.1 %collective-permute-start.13 = (bf16[128,1024]{1,0:T(8,128)(2,1)}, bf16[128,1024]{1,0:T(8,128)(2,1)S(1)}, u32[]{:S(2)}, u32[]{:S(2)}) collective-permute-start(bf16[128,1024]{1,0:T(8,128)(2,1)} %get-tuple-element.171), channel_id=1, source_target_pairs={{2,0},{5,1},{0,2},{3,3},{6,4},{1,5},{4,6},{7,7},{10,8},{13,9},{8,1... | collective-permute-start | bytes 786440 | tf_op jit(solution)/shard_map/ppermute | solution.py:860
  110.6 31.4 %collective-permute-start.16 = (bf16[144,2048]{1,0:T(8,128)(2,1)}, bf16[144,2048]{1,0:T(8,128)(2,1)}, u32[]{:S(2)}, u32[]{:S(2)}) collective-permute-start(bf16[144,2048]{1,0:T(8,128)(2,1)} %get-tuple-element.196.refs_12_), channel_id=1, source_target_pairs={{0,1},{1,2},{2,3},{3,4},{4,5},{5,6},{6,7},{8,9},{9,10},{10,11},{11... | collective-permute-start | bytes 1769480 | tf_op jit(solution)/shard_map/ppermute | solution.py:898
  114.8 27.2 %collective-permute-start.17 = (bf16[144,2048]{1,0:T(8,128)(2,1)}, bf16[144,2048]{1,0:T(8,128)(2,1)}, u32[]{:S(2)}, u32[]{:S(2)}) collective-permute-start(bf16[144,2048]{1,0:T(8,128)(2,1)} %get-tuple-element.196.refs_12_), channel_id=1, source_target_pairs={{0,2},{2,4},{3,5},{5,7},{8,10},{10,12},{11,13},{13,15},{16,18},{18... | collective-permute-start | bytes 1769480 | tf_op jit(solution)/shard_map/ppermute | solution.py:898
  117.0 25.0 %collective-permute-start.18 = (bf16[144,2048]{1,0:T(8,128)(2,1)}, bf16[144,2048]{1,0:T(8,128)(2,1)}, u32[]{:S(2)}, u32[]{:S(2)}) collective-permute-start(bf16[144,2048]{1,0:T(8,128)(2,1)} %get-tuple-element.196.refs_12_), channel_id=1, source_target_pairs={{2,5},{10,13},{18,21},{26,29}} | collective-permute-start | bytes 1769480 | tf_op jit(solution)/shard_map/ppermute | solution.py:898
  153.7 29.1 %collective-permute-start.19 = (bf16[144,2048]{1,0:T(8,128)(2,1)S(1)}, bf16[144,2048]{1,0:T(8,128)(2,1)S(1)}, u32[]{:S(2)}, u32[]{:S(2)}) collective-permute-start(bf16[144,2048]{1,0:T(8,128)(2,1)S(1)} %get-tuple-element.229), channel_id=1, source_target_pairs={{1,0},{2,1},{3,2},{4,3},{5,4},{6,5},{7,6},{9,8},{10,9},{11,10},{12... | collective-permute-start | bytes 1769480 | tf_op jit(solution)/shard_map/ppermute | solution.py:908
  155.0 27.8 %collective-permute-start.20 = (bf16[144,2048]{1,0:T(8,128)(2,1)S(1)}, bf16[144,2048]{1,0:T(8,128)(2,1)S(1)}, u32[]{:S(2)}, u32[]{:S(2)}) collective-permute-start(bf16[144,2048]{1,0:T(8,128)(2,1)S(1)} %get-tuple-element.229), channel_id=1, source_target_pairs={{5,2},{13,10},{21,18},{29,26}} | collective-permute-start | bytes 1769480 | tf_op jit(solution)/shard_map/ppermute | solution.py:908
  182.9 14.5 %collective-permute-start.22 = (bf16[1024,1024]{1,0:T(8,128)(2,1)}, bf16[1024,1024]{1,0:T(8,128)(2,1)}, u32[]{:S(2)}, u32[]{:S(2)}) collective-permute-start(bf16[1024,1024]{1,0:T(8,128)(2,1)} %get-tuple-element.223), channel_id=1, source_target_pairs={{0,8},{1,9},{2,10},{3,11},{4,12},{5,13},{6,14},{7,15},{8,0},{9,1},... | collective-permute-start | bytes 6291464 | tf_op jit(solution)/shard_map/ppermute | solution.py:48
  183.5 23.0 %collective-permute-start.23 = (bf16[144,2048]{1,0:T(8,128)(2,1)S(1)}, bf16[144,2048]{1,0:T(8,128)(2,1)S(1)}, u32[]{:S(2)}, u32[]{:S(2)}) collective-permute-start(bf16[144,2048]{1,0:T(8,128)(2,1)S(1)} %get-tuple-element.229), channel_id=1, source_target_pairs={{2,0},{4,2},{5,3},{7,5},{10,8},{12,10},{13,11},{15,13},{18,16},{20... | collective-permute-start | bytes 1769480 | tf_op jit(solution)/shard_map/ppermute | solution.py:925
  206.5 28.3 %collective-permute-start.24 = (bf16[8,32,2048]{2,1,0:T(8,128)(2,1)S(1)}, bf16[8,32,2048]{2,1,0:T(8,128)(2,1)S(1)}, u32[]{:S(2)}, u32[]{:S(2)}) collective-permute-start(bf16[8,32,2048]{2,1,0:T(8,128)(2,1)S(1)} %bitcast.93), channel_id=1, source_target_pairs={{0,16},{1,17},{2,18},{3,19},{4,20},{5,21},{6,22},{7,23},{8,24},{9,... | collective-permute-start | bytes 3145736 | tf_op jit(solution)/shard_map/ppermute | solution.py:48
  207.9 30.2 %collective-permute-start.25 = (bf16[8,64,1024]{2,1,0:T(8,128)(2,1)}, bf16[8,64,1024]{2,1,0:T(8,128)(2,1)S(1)}, u32[]{:S(2)}, u32[]{:S(2)}) collective-permute-start(bf16[8,64,1024]{2,1,0:T(8,128)(2,1)} %bitcast.21), channel_id=1, source_target_pairs={{0,1},{1,0},{2,3},{3,2},{4,5},{5,4},{6,7},{7,6},{8,9},{9,8},{10,11... | collective-permute-start | bytes 3145736 | tf_op jit(solution)/shard_map/ppermute | solution.py:48
  208.0 30.6 %collective-permute-start.26 = (bf16[128,1024]{1,0:T(8,128)(2,1)S(1)}, bf16[128,1024]{1,0:T(8,128)(2,1)S(1)}, u32[]{:S(2)}, u32[]{:S(2)}) collective-permute-start(bf16[128,1024]{1,0:T(8,128)(2,1)S(1)} %get-tuple-element.360), channel_id=1, source_target_pairs={{0,0},{1,3},{2,6},{3,1},{4,4},{5,7},{6,2},{7,5},{8,8},{9,11},{10,1... | collective-permute-start | bytes 786440 | tf_op jit(solution)/shard_map/ppermute | solution.py:835
  208.7 30.0 %collective-permute-start.27 = (bf16[128,1024]{1,0:T(8,128)(2,1)S(1)}, bf16[128,1024]{1,0:T(8,128)(2,1)S(1)}, u32[]{:S(2)}, u32[]{:S(2)}) collective-permute-start(bf16[128,1024]{1,0:T(8,128)(2,1)S(1)} %get-tuple-element.359), channel_id=1, source_target_pairs={{0,1},{1,4},{2,7},{3,2},{4,5},{5,0},{6,3},{7,6},{8,9},{9,12},{10,1... | collective-permute-start | bytes 786440 | tf_op jit(solution)/shard_map/ppermute | solution.py:835
  215.0 23.6 %collective-permute-start.28 = (bf16[128,1024]{1,0:T(8,128)(2,1)S(1)}, bf16[128,1024]{1,0:T(8,128)(2,1)S(1)}, u32[]{:S(2)}, u32[]{:S(2)}) collective-permute-start(bf16[128,1024]{1,0:T(8,128)(2,1)S(1)} %get-tuple-element.358), channel_id=1, source_target_pairs={{0,2},{1,5},{2,0},{3,3},{4,6},{5,1},{6,4},{7,7},{8,10},{9,13},{10,... | collective-permute-start | bytes 786440 | tf_op jit(solution)/shard_map/ppermute | solution.py:835
  238.7 13.6 %collective-permute-start.30 = (bf16[4,64,1024]{2,1,0:T(8,128)(2,1)S(1)}, bf16[4,64,1024]{2,1,0:T(8,128)(2,1)S(1)}, u32[]{:S(2)}, u32[]{:S(2)}) collective-permute-start(bf16[4,64,1024]{2,1,0:T(8,128)(2,1)S(1)} %get-tuple-element.253), channel_id=1, source_target_pairs={{0,16},{1,17},{2,18},{3,19},{4,20},{5,21},{6,22},{7,23},{8,24},{9,... | collective-permute-start | bytes 1572872 | tf_op jit(solution)/shard_map/ppermute | solution.py:48
  239.4 13.8 %collective-permute-start.29 = (bf16[4,32,2048]{2,1,0:T(8,128)(2,1)S(1)}, bf16[4,32,2048]{2,1,0:T(8,128)(2,1)S(1)}, u32[]{:S(2)}, u32[]{:S(2)}) collective-permute-start(bf16[4,32,2048]{2,1,0:T(8,128)(2,1)S(1)} %get-tuple-element.251), channel_id=1, source_target_pairs={{0,1},{1,0},{2,3},{3,2},{4,5},{5,4},{6,7},{7,6},{8,9},{9,8},{10,11... | collective-permute-start | bytes 1572872 | tf_op jit(solution)/shard_map/ppermute | solution.py:48
  254.3 30.6 %collective-permute-start.31 = (bf16[512,1152]{1,0:T(8,128)(2,1)}, bf16[512,1152]{1,0:T(8,128)(2,1)}, u32[]{:S(2)}, u32[]{:S(2)}) collective-permute-start(bf16[512,1152]{1,0:T(8,128)(2,1)} %get-tuple-element.271), channel_id=1, source_target_pairs={{0,8},{1,9},{2,10},{3,11},{4,12},{5,13},{6,14},{7,15},{8,0},{9,1},... | collective-permute-start | bytes 3538952 | tf_op jit(solution)/shard_map/ppermute | solution.py:48
  254.4 16.3 %collective-permute-start.35 = (bf16[1,2,32,2048]{3,2,1,0:T(8,128)(2,1)}, bf16[1,2,32,2048]{3,2,1,0:T(8,128)(2,1)S(1)}, u32[]{:S(2)}, u32[]{:S(2)}) collective-permute-start(bf16[1,2,32,2048]{3,2,1,0:T(8,128)(2,1)} %get-tuple-element.277), channel_id=1, source_target_pairs={{0,6},{1,7},{2,4},{3,5},{4,2},{5,3},{6,0},{7,1},{8,14},{9,15},{10,... | collective-permute-start | bytes 786440 | tf_op jit(solution)/shard_map/ppermute | solution.py:48
  262.6 22.3 %collective-permute-start.34 = (bf16[1,2,32,2048]{3,2,1,0:T(8,128)(2,1)}, bf16[1,2,32,2048]{3,2,1,0:T(8,128)(2,1)S(1)}, u32[]{:S(2)}, u32[]{:S(2)}) collective-permute-start(bf16[1,2,32,2048]{3,2,1,0:T(8,128)(2,1)} %get-tuple-element.276), channel_id=1, source_target_pairs={{0,4},{1,5},{2,6},{3,7},{4,0},{5,1},{6,2},{7,3},{8,12},{9,13},{10,... | collective-permute-start | bytes 786440 | tf_op jit(solution)/shard_map/ppermute | solution.py:48
  262.6 22.3 %collective-permute-start.33 = (bf16[1,2,32,2048]{3,2,1,0:T(8,128)(2,1)}, bf16[1,2,32,2048]{3,2,1,0:T(8,128)(2,1)S(1)}, u32[]{:S(2)}, u32[]{:S(2)}) collective-permute-start(bf16[1,2,32,2048]{3,2,1,0:T(8,128)(2,1)} %get-tuple-element.275), channel_id=1, source_target_pairs={{0,2},{1,3},{2,0},{3,1},{4,6},{5,7},{6,4},{7,5},{8,10},{9,11},{10,... | collective-permute-start | bytes 786440 | tf_op jit(solution)/shard_map/ppermute | solution.py:48
  263.4 23.3 %collective-permute-start.32 = (bf16[512,1280]{1,0:T(8,128)(2,1)}, bf16[512,1280]{1,0:T(8,128)(2,1)S(1)}, u32[]{:S(2)}, u32[]{:S(2)}) collective-permute-start(bf16[512,1280]{1,0:T(8,128)(2,1)} %get-tuple-element.273), channel_id=1, source_target_pairs={{0,8},{1,9},{2,10},{3,11},{4,12},{5,13},{6,14},{7,15},{8,0},{9,1},... | collective-permute-start | bytes 3932168 | tf_op jit(solution)/shard_map/ppermute | solution.py:48
  288.3 15.2 %collective-permute-start.36 = (bf16[8,32,1152]{2,1,0:T(8,128)(2,1)S(1)}, bf16[8,32,1152]{2,1,0:T(8,128)(2,1)S(1)}, u32[]{:S(2)}, u32[]{:S(2)}) collective-permute-start(bf16[8,32,1152]{2,1,0:T(8,128)(2,1)S(1)} %bitcast.99), channel_id=1, source_target_pairs={{0,16},{1,17},{2,18},{3,19},{4,20},{5,21},{6,22},{7,23},{8,24},{9,... | collective-permute-start | bytes 1769480 | tf_op jit(solution)/shard_map/ppermute | solution.py:48
  289.8 17.0 %collective-permute-start.37 = (bf16[8,32,1280]{2,1,0:T(8,128)(2,1)S(1)}, bf16[8,32,1280]{2,1,0:T(8,128)(2,1)S(1)}, u32[]{:S(2)}, u32[]{:S(2)}) collective-permute-start(bf16[8,32,1280]{2,1,0:T(8,128)(2,1)S(1)} %bitcast.94), channel_id=1, source_target_pairs={{0,1},{1,0},{2,3},{3,2},{4,5},{5,4},{6,7},{7,6},{8,9},{9,8},{10,11... | collective-permute-start | bytes 1966088 | tf_op jit(solution)/shard_map/ppermute | solution.py:48
  290.7 16.8 %collective-permute-start.38 = (f32[16,1024]{1,0:T(8,128)S(1)}, f32[16,1024]{1,0:T(8,128)S(1)}, u32[]{:S(2)}, u32[]{:S(2)}) collective-permute-start(f32[16,1024]{1,0:T(8,128)S(1)} %slice.314), channel_id=1, source_target_pairs={{1,0},{2,1},{3,2},{4,3},{5,4},{6,5},{7,6},{9,8},{10,9},{11,10},{12... | collective-permute-start | bytes 196616 | tf_op jit(solution)/shard_map/ppermute | solution.py:953
  322.9 14.3 %collective-permute-start.46 = (bf16[1,32,2432]{2,1,0:T(8,128)(2,1)S(1)}, bf16[1,32,2432]{2,1,0:T(8,128)(2,1)S(1)}, u32[]{:S(2)}, u32[]{:S(2)}) collective-permute-start(bf16[1,32,2432]{2,1,0:T(8,128)(2,1)S(1)} %get-tuple-element.306), channel_id=1, source_target_pairs={{0,6},{1,7},{2,4},{3,5},{4,2},{5,3},{6,0},{7,1},{8,14},{9,15},{10,... | collective-permute-start | bytes 466952 | tf_op jit(solution)/shard_map/ppermute | solution.py:48
  (80 other events, 1161.8 us)
Sparse Core Ops, SparseCore 0:
  31.2 95.5 all-gather.1

commit v2 on v1

--- a/solution.py
+++ b/solution.py
@@ -39,7 +39,7 @@
     return jax.ShapeDtypeStruct(dims, dtype)
 
 
-def params(mib=48):
+def params(mib=27):
     return pltpu.CompilerParams(vmem_limit_bytes=mib * 2**20)
 
 
@@ -73,6 +73,17 @@
     for part, m in zip(pieces[1:], stage):
         total = total + permute(part, m).astype(F32)
     return total.astype(dtype)
+
+
+def fold_cut(pieces, stage, after):
+    parts = [permute(part, m) for part, m in zip(pieces[1:], stage)]
+    made = []
+    for cuts in zip(*[cut(v, after) for v in [pieces[0]] + parts]):
+        total = cuts[0].astype(F32)
+        for part in cuts[1:]:
+            total = total + part.astype(F32)
+        made.append(total.astype(BF16))
+    return made
 
 
 def order_of(stages):
@@ -269,13 +280,17 @@
     )(tab, gp, gq, gout, few)
 
 
-def first_kernel(masks_p, masks_q, total, lin_ref, halo_ref, t0_ref, t1_ref, t2_ref, gain_ref, meta_ref, taps_ref, hp_ref, po, px, qo, qx,
-                 w1_ref, normed_ref, cin_ref, pre_ref, bc_ref, x_ref, dtx_ref, hd_ref, cumt_ref, pay_ref, cin_s, w1_s, cin_b, pre_b, sem_p, sem_q, sem_out):
-    lin = lin_ref[0]
+def weight_copies(lin, masks_p, masks_q, po, px, qo, qx, w1_s, sem_p, sem_q):
     rows = D // len(masks_p)
     place = lambda cols: lambda src, where: [(src, rows_at(w1_s, where, rows, cols))]
     first = block_copies(lin, masks_p, (po, px), place(pl.ds(0, P_COLS)), sem_p)
     second = block_copies(lin, masks_q, (qo, qx), place(pl.ds(P_COLS, Q_COLS)), sem_q)
+    return first, second
+
+
+def first_kernel(masks_p, masks_q, total, lin_ref, halo_ref, t0_ref, t1_ref, t2_ref, gain_ref, meta_ref, taps_ref, hp_ref, po, px, qo, qx,
+                 normed_ref, cin_ref, pre_ref, bc_ref, x_ref, dtx_ref, hd_ref, cumt_ref, pay_ref, cin_s, w1_s, cin_b, pre_b, sem_p, sem_q, sem_out):
+    first, second = weight_copies(lin_ref[0], masks_p, masks_q, po, px, qo, qx, w1_s, sem_p, sem_q)
     start = 0
     for ref in (halo_ref, t0_ref, t1_ref, t2_ref):
         u = ref[...].astype(F32)
@@ -328,7 +343,6 @@
         if j == P_TILES:
             for copy in second:
                 copy.wait()
-            write(w1_s, w1_ref)
         cols = pl.ds(2 * N + j * TILE, TILE)
         own = slice(j * TILE, (j + 1) * TILE)
         x = conv(nn(normed_ref[...], w1_s[:, FRONT + j * TILE : FRONT + (j + 1) * TILE]), cols)
@@ -349,12 +363,12 @@
     return pl.pallas_call(
         functools.partial(first_kernel, masks_p, masks_q, total),
         out_shape=(
-            shape((D, W1_COLS), BF16), shape((ext, D), BF16), shape((ext, CONV), BF16), shape((total, CONV), BF16), shape((total, 2 * N), BF16),
+            shape((ext, D), BF16), shape((ext, CONV), BF16), shape((total, CONV), BF16), shape((total, 2 * N), BF16),
             shape((total, INNER), BF16), shape((total, INNER), BF16), shape((5, total, N)), shape((H, total)), shape((N + HALO, INNER), BF16),
         ),
         in_specs=[SMEM] + [VMEM] * 8 + [ANY] * 4,
-        out_specs=(HBM, VMEM, HBM, HBM) + tuple([VMEM] * 6),
-        scratch_shapes=[pltpu.VMEM((ext, TILE), F32), pltpu.VMEM((D, W1_COLS), BF16), pltpu.VMEM((ext, CONV), BF16), pltpu.VMEM((total, CONV), BF16), pltpu.SemaphoreType.DMA((len(masks_p),)), pltpu.SemaphoreType.DMA((len(masks_q),)), pltpu.SemaphoreType.DMA((2 * (INNER // TILE + 1) + 1,))],
+        out_specs=(VMEM, HBM, HBM) + tuple([VMEM] * 6),
+        scratch_shapes=[pltpu.VMEM((ext, TILE), F32), pltpu.VMEM((D, W1_COLS), BF16), pltpu.VMEM((ext, CONV), BF16), pltpu.VMEM((total, CONV), BF16), pltpu.SemaphoreType.DMA((len(masks_p),)), pltpu.SemaphoreType.DMA((len(masks_q),)), pltpu.SemaphoreType.DMA((2 * (INNER // TILE + 1),))],
         compiler_params=params(),
         cost_estimate=SMALL,
         name="first_stage",
@@ -406,7 +420,7 @@
         in_specs=[VMEM] * 2 + [HBM],
         out_specs=tuple([VMEM] * 3),
         scratch_shapes=late_scratch(count),
-        compiler_params=params(),
+        compiler_params=params(40),
         cost_estimate=SMALL,
         name="gate_stage",
     )(normed, g, blocks)
@@ -508,6 +522,28 @@
         factor = step if factor is None else factor * step
         states = states + factor * ref[:N, cols].astype(F32)
     return states
+
+
+def double_kernel(own_ref, next_ref, out_ref):
+    for j in range(INNER // TILE):
+        cols = slice(j * TILE, (j + 1) * TILE)
+        factor = jnp.sum(own_ref[N:, cols].astype(F32), axis=0, keepdims=True)
+        further = jnp.sum(next_ref[N:, cols].astype(F32), axis=0, keepdims=True)
+        out_ref[:N, cols] = (own_ref[:N, cols].astype(F32) + factor * next_ref[:N, cols].astype(F32)).astype(BF16)
+        parts = [p.astype(F32) for p in split(factor * further)]
+        out_ref[N:, cols] = jnp.concatenate(parts + [jnp.zeros((HALO - 3, TILE), F32)], axis=0).astype(BF16)
+
+
+def double_stage(own, following):
+    return pl.pallas_call(
+        double_kernel,
+        out_shape=shape(own.shape, BF16),
+        in_specs=[VMEM] * 2,
+        out_specs=VMEM,
+        compiler_params=params(),
+        cost_estimate=SMALL,
+        name="double_stage",
+    )(own, following)
 
 
 def output_kernel(count, total, *refs):
@@ -646,7 +682,7 @@
         in_specs=[VMEM] * 3 + [HBM],
         out_specs=(VMEM, VMEM),
         scratch_shapes=late_scratch(count),
-        compiler_params=params(),
+        compiler_params=params(40),
         cost_estimate=SMALL,
         name="rest_stage",
     )(normed_out, grad_gate, ext_tok, blocks)
@@ -789,22 +825,52 @@
     )(*got, *heads, *conv_refs, turned_rows, *more)
 
 
-def normed_kernel(pp_ref, pq_ref, w1_ref, part_ref, out_ref):
-    out_ref[...] = nt(pp_ref[:, 128:], w1_ref[:, 128:P_COLS]) + nt(pq_ref[...], w1_ref[:, P_COLS:])
-    out_ref[...] += nt(pp_ref[:, :H], w1_ref[:, :H])
+def normed_kernel(masks_p, masks_q, lin_ref, pp_ref, pq_ref, part_ref, po, px, qo, qx, out_ref, w1_s, sem_p, sem_q):
+    first, second = weight_copies(lin_ref[0], masks_p, masks_q, po, px, qo, qx, w1_s, sem_p, sem_q)
+    for copy in first + second:
+        copy.wait()
+    out_ref[...] = nt(pp_ref[:, 128:], w1_s[:, 128:P_COLS]) + nt(pq_ref[...], w1_s[:, P_COLS:])
+    out_ref[...] += nt(pp_ref[:, :H], w1_s[:, :H])
     out_ref[HALO:, :] += part_ref[...]
 
 
-def normed_stage(proj_p, proj_q, w1, part):
-    return pl.pallas_call(
-        normed_kernel,
+def normed_stage(proj_p, proj_q, part, p, q):
+    (po, px, masks_p, lin), (qo, qx, masks_q, _) = p, q
+    return pl.pallas_call(
+        functools.partial(normed_kernel, masks_p, masks_q),
         out_shape=shape((proj_p.shape[0], D)),
-        in_specs=[VMEM] * 4,
+        in_specs=[SMEM] + [VMEM] * 3 + [ANY] * 4,
         out_specs=VMEM,
+        scratch_shapes=[pltpu.VMEM((D, W1_COLS), BF16), pltpu.SemaphoreType.DMA((len(masks_p),)), pltpu.SemaphoreType.DMA((len(masks_q),))],
         compiler_params=params(),
         cost_estimate=SMALL,
         name="normed_stage",
-    )(proj_p, proj_q, w1, part)
+    )(lin, proj_p, proj_q, part, po, px, qo, qx)
+
+
+def finish_kernel(normed_ref, rim_ref, tok_ref, g_ref, gain_ref, *outs):
+    rows = outs[0].shape[0]
+    for i, out_ref in enumerate(outs):
+        own = slice(HALO + i * rows, HALO + (i + 1) * rows)
+        u = tok_ref[own, :].astype(F32)
+        scale = lax.rsqrt(jnp.mean(u * u, axis=-1, keepdims=True) + EPS)
+        grad = normed_ref[own, :]
+        if i == len(outs) - 1:
+            grad = jnp.concatenate([grad[: rows - HALO], grad[rows - HALO :] + rim_ref[...]], axis=0)
+        unit, q = u * scale, grad * gain_ref[...]
+        out_ref[...] = (g_ref[i * rows : (i + 1) * rows, :].astype(F32) + scale * (q - unit * jnp.mean(q * unit, axis=-1, keepdims=True))).astype(BF16)
+
+
+def finish_stage(grad_normed, rim, ext_tok, g, gain_in, rows):
+    return pl.pallas_call(
+        finish_kernel,
+        out_shape=(shape((rows, D), BF16),) * MB,
+        in_specs=[VMEM] * 5,
+        out_specs=tuple([VMEM] * MB),
+        compiler_params=params(),
+        cost_estimate=SMALL,
+        name="finish_stage",
+    )(grad_normed, rim, ext_tok, g, gain_in)
 
 
 def body(tokens, scene_ids, valid_mask, norm_gain, w_in, conv_w, conv_b, dt_bias, a_log, d_skip, gate_gain, w_out, d_out):
@@ -886,16 +952,19 @@
         both = both.reshape(32, D // 32, both.shape[2])
         return both[:16], both[16:], np.arange(32), jnp.zeros((1,), jnp.int32)
 
-    w1_full, normed, conv_in, conv_pre, bc, x_part, dtx, hd, cumt, pay = first_stage(
-        (halo, *got), gain_in, meta, taps, hp, pieces(p, p_other, 0), pieces(q, q_other, 1), total
+    piece_p, piece_q = pieces(p, p_other, 0), pieces(q, q_other, 1)
+    normed, conv_in, conv_pre, bc, x_part, dtx, hd, cumt, pay = first_stage(
+        (halo, *got), gain_in, meta, taps, hp, piece_p, piece_q, total
     )
 
     def spans(k):
         return [d for d in range(n_s - k) if ((d + 1) * total - 1) // length == (d + k) * total // length]
 
     far = max(k for k in range(1, n_s) if spans(k))
+    reaches = [1 << b for b in range(far.bit_length())]
     pay, normed, dtx, cumt = tied(pay, normed, dtx, cumt)
-    before = [lax.ppermute(pay, "seq", [(d, d + k) for d in spans(k)]) for k in range(1, far + 1)]
+    forth = lambda v, k: lax.ppermute(v, "seq", [(d, d + k) for d in spans(k)])
+    before = [forth(pay, k) for k in range(1, far + 1)]
     normed_p, normed_q = turn_stage(tab_p, tab_q, normed)
     inside = pairs_stage(bc, dtx, cumt, id_col, id_row, total)
     g = jnp.concatenate(g)
@@ -905,7 +974,8 @@
         before, inside, bc, x_part, hd, ga, dga, gno, gain_out, skip_wide, pay, total
     )
 
-    adjoints = [None if k == 2 else lax.ppermute(pay_back, "seq", [(d + k, d) for d in spans(k)]) for k in range(1, far + 1)]
+    back = lambda v, k: lax.ppermute(v, "seq", [(d + k, d) for d in spans(k)])
+    adjoints = [back(pay_back, 1)]
 
     def sent(keep, send, which):
         if aligned:
@@ -919,18 +989,19 @@
     keep_g, send_g, keep_o, send_o = weights_stage(tab_q, normed_p, grad_gate, normed_out, g, total)
     gdtx, gb_pairs, gc_pairs = pairs_back_stage(bc, dtx, e, cumt, id_col, id_row, total)
     rg, ro = sent(keep_g, send_g, 0), sent(keep_o, send_o, 1)
-    (rg, ro), gdtx, gb_pairs, gc_pairs, normed_out, pay_back, near, *more = tied(
-        (rg, ro), gdtx, gb_pairs, gc_pairs, normed_out, pay_back, adjoints[0], *adjoints[2:]
-    )
-    adjoints = [near] + [lax.ppermute(pay_back, "seq", [(d + 2, d) for d in spans(2)])] + more
+    (rg, ro), gdtx, gb_pairs, gc_pairs, normed_out, pay_back, *adjoints = tied((rg, ro), gdtx, gb_pairs, gc_pairs, normed_out, pay_back, *adjoints)
+    held = pay_back
+    for k in reaches[1:]:
+        held = double_stage(held, adjoints[-1])
+        adjoints.append(back(held, k))
     block_out, part = rest_stage(normed_out, grad_gate, ext_tok, late, total)
-    rg, ro = cut(blocks(fold(rg, core)), y), cut(blocks(fold(ro, core)), x)
+    rg, ro = fold_cut([blocks(v) for v in rg], core, y), fold_cut([blocks(v) for v in ro], core, x)
     (rg, ro), gdtx, block_out, part, *adjoints = tied((rg, ro), gdtx, block_out, part, *adjoints)
 
     conv_refs = (conv_pre, conv_in, taps, meta)
     head_refs = (gdtx, e, x_part, dtx, bc, state_in, hd, skip_wide)
     keep_q, send_q, proj_q, gt_q, acc, few = back_stage(adjoints, head_refs, conv_refs, normed_q, (), total)
-    rg, ro = cut(fold(rg, y), x), cut(fold(ro, x), y)
+    rg, ro = fold_cut(rg, y, x), fold_cut(ro, x, y)
     thirds = lambda v: [v[i * rows : (i + 1) * rows] for i in range(MB)]
     block_out = home(thirds(block_out))
     rq = sent(keep_q, send_q, 1)
@@ -946,20 +1017,15 @@
     rp = sent(keep_p, send_p, 0)
     (both, rq, rp), proj_p, gt_p, few, block_out = tied((both, rq, rp), proj_p, gt_p, few, block_out)
 
-    grad_normed = normed_stage(proj_p, proj_q, w1_full, part)
+    grad_normed = normed_stage(proj_p, proj_q, part, piece_p, piece_q)
+    rp, rq = fold_cut([blocks(v) for v in rp], core, y), fold_cut([blocks(v) for v in rq], core, x)
+    rim = lax.ppermute(grad_normed[:HALO], "seq", [(d + 1, d) for d in range(n_s - 1)])
+    (rp, rq), grad_normed, rim = tied((rp, rq), grad_normed, rim)
     both = fold(both, z, F32)[0]
-    rp, rq = cut(blocks(fold(rp, core)), y), cut(blocks(fold(rq, core)), x)
-    (rp, rq), both, grad_normed = tied((rp, rq), both, grad_normed)
-    rim = lax.ppermute(grad_normed[:HALO], "seq", [(d + 1, d) for d in range(n_s - 1)])
-    rp, rq = cut(fold(rp, y), x), cut(fold(rq, x), y)
-    (rp, rq), rim, grad_normed = tied((rp, rq), rim, grad_normed)
-    own = grad_normed[HALO:]
-    own = jnp.concatenate([own[: total - HALO], own[total - HALO :] + rim])
-    u = ext_tok[HALO:].astype(F32)
-    in_scale = lax.rsqrt(jnp.mean(u * u, axis=-1, keepdims=True) + EPS)
-    unit, q_in = u * in_scale, own * gain_in
-    grad_in = (g.astype(F32) + in_scale * (q_in - unit * jnp.mean(q_in * unit, axis=-1, keepdims=True))).astype(BF16)
-    grad_in = home(thirds(grad_in))
+    rp, rq = fold_cut(rp, y, x), fold_cut(rq, x, y)
+    grad_in = finish_stage(grad_normed, rim, ext_tok, g, gain_in, rows)
+    (rp, rq), grad_in, both = tied((rp, rq), grad_in, both)
+    grad_in = home(grad_in)
     w1_grad = cut(jnp.concatenate([fold(rp, x), fold(rq, y)], axis=2), z)
     w1_grad, grad_in, block_out = tied(w1_grad, grad_in, block_out)
     w1_grad = fold(w1_grad, z, F32)[0]

time: 359 us -> 327 us (0.911)
  Pallas kernels: 100 us -> 83.8 us
  starting transfers between devices: 96.2 us -> 81.5 us
    pallas_call x2, Pallas kernels: 26.8 us -> 15.8 us  [back_stage(): pl.pallas_call(functools.partial(back_kernel, len(got), total, last, smal...]
    ppermute x6 -> x5, starting transfers between devices: 20.8 us -> 10.5 us  [the longest x3 7.7 us: body(): forth = lambda v, k: lax.ppermute(v, 'seq', [(d, d + k) for d in spans(k)])]
    convert_element_type x1 -> x8, other arithmetic: 0.5 us -> 9.92 us  [fold_cut(): made.append(total.astype(BF16))]
    convert_element_type x11 -> x3, other arithmetic: 8.88 us -> 0.34 us  [fold(): return total.astype(dtype)]
    pallas_call x1, Pallas kernels: 11.6 us -> 7.55 us  [output_stage(): pl.pallas_call(functools.partial(output_kernel, count, total), out_shape=...]
    ppermute x6, waiting for transfers between devices: 3.67 us -> 0.02 us  [home(): lax.ppermute(part, 'seq', [(d, k) for k, d in source(i)])]
    unnamed x132 -> x167, local copies, waits for them, and re-layouts: 15.5 us -> 18.2 us
  transfers between devices with their start and end apart: 48 -> 47, of which waited for: 17 -> 16; matrix products, arithmetic and copies ran while one was open for 5% -> 6% of each run, Pallas kernels for 25% -> 24%
where the time goes in v2:
time: 327 us; the launch traced here: 324 us
  waiting for transfers between devices  95.2 us (29%)
  Pallas kernels  83.8 us (26%)
  starting transfers between devices  81.5 us (25%)
  local copies, waits for them, and re-layouts  25.9 us (8%)
  other arithmetic  21.5 us (7%)
  between operations  16.1 us (5%)
    ppermute x27, waiting for transfers between devices, permute(): return lax.ppermute(block, BOTH, [(i, i ^ mask) for i in range(size)])  74.1 us
    ppermute x27, starting transfers between devices, permute(): return lax.ppermute(block, BOTH, [(i, i ^ mask) for i in range(size)])  34.7 us
    unnamed x167, local copies, waits for them, and re-layouts  18.2 us
    ppermute x6, starting transfers between devices, home(): lax.ppermute(part, 'seq', [(d, k) for k, d in source(i)])  18.1 us
    pallas_call x2, Pallas kernels, back_stage(): pl.pallas_call(functools.partial(back_kernel, len(got), total, last, smal...  15.8 us
    ppermute x3, waiting for transfers between devices, body(): got = [lax.ppermute(chosen(tokens, i), 'seq', source(i)) for i in range(MB)]  15.2 us
    pallas_call x1, Pallas kernels, first_stage(): pl.pallas_call(functools.partial(first_kernel, masks_p, masks_q, total),...  14.6 us
    convert_element_type x8, other arithmetic, fold_cut(): made.append(total.astype(BF16))  9.92 us
  transfers between devices with their start and end apart: 47, of which 16 were waited for; matrix products, arithmetic and copies ran while one was open for 6% of the time, Pallas kernels for 24%

profile of v2, /device:TPU:0, one launch (start us, length us, event | category | flops | bytes accessed | tf_op | source)
XLA Modules:
  0.0 324.1 jit_solution(14132855981339569193)
XLA Ops:
  12.6 5.1 %collective-permute-start.2 = (bf16[1,32,2432]{2,1,0:T(8,128)(2,1)S(1)}, bf16[1,32,2432]{2,1,0:T(8,128)(2,1)S(1)}, u32[]{:S(2)}, u32[]{:S(2)}) collective-permute-start(bf16[1,32,2432]{2,1,0:T(8,128)(2,1)S(1)} %bitcast.108), channel_id=1, source_target_pairs={{0,6},{1,7},{2,4},{3,5},{4,2},{5,3},{6,0},{7,1},{8,14},{9,15},{10,... | collective-permute-start | bytes 466952 | tf_op jit(solution)/shard_map/ppermute | solution.py:48
  23.3 7.6 %collective-permute-done.1 = bf16[1,32,2432]{2,1,0:T(8,128)(2,1)S(1)} collective-permute-done((bf16[1,32,2432]{2,1,0:T(8,128)(2,1)S(1)}, bf16[1,32,2432]{2,1,0:T(8,128)(2,1)S(1)}, u32[]{:S(2)}, u32[]{:S(2)}) %collective-permute-start.1) | collective-permute-done | bytes 155680 | tf_op jit(solution)/shard_map/ppermute | solution.py:48
  36.2 4.0 %collective-permute-start.7 = (bf16[128,1024]{1,0:T(8,128)(2,1)S(1)}, bf16[128,1024]{1,0:T(8,128)(2,1)S(1)}, u32[]{:S(2)}, u32[]{:S(2)}) collective-permute-start(bf16[128,1024]{1,0:T(8,128)(2,1)S(1)} %get-tuple-element.376), channel_id=1, source_target_pairs={{1,0},{4,1},{7,2},{2,3},{5,4},{0,5},{3,6},{6,7},{9,8},{12,9},{15,1... | collective-permute-start | bytes 786440 | tf_op jit(solution)/shard_map/ppermute | solution.py:923
  43.3 7.3 %collective-permute-done.7.t1_ref = bf16[128,1024]{1,0:T(8,128)(2,1)S(1)} collective-permute-done((bf16[128,1024]{1,0:T(8,128)(2,1)S(1)}, bf16[128,1024]{1,0:T(8,128)(2,1)S(1)}, u32[]{:S(2)}, u32[]{:S(2)}) %collective-permute-start.7) | collective-permute-done | bytes 262176 | tf_op jit(solution)/shard_map/ppermute | solution.py:923
  51.4 7.9 %collective-permute-done.8.t2_ref = bf16[128,1024]{1,0:T(8,128)(2,1)S(1)} collective-permute-done((bf16[128,1024]{1,0:T(8,128)(2,1)S(1)}, bf16[128,1024]{1,0:T(8,128)(2,1)S(1)}, u32[]{:S(2)}, u32[]{:S(2)}) %collective-permute-start.8) | collective-permute-done | bytes 262176 | tf_op jit(solution)/shard_map/ppermute | solution.py:923
  62.1 4.0 %collective-permute-start.12 = (bf16[128,1024]{1,0:T(8,128)(2,1)S(1)}, bf16[128,1024]{1,0:T(8,128)(2,1)S(1)}, u32[]{:S(2)}, u32[]{:S(2)}) collective-permute-start(bf16[128,1024]{1,0:T(8,128)(2,1)S(1)} %get-tuple-element.172), channel_id=1, source_target_pairs={{1,0},{4,1},{7,2},{2,3},{5,4},{0,5},{3,6},{6,7},{9,8},{12,9},{15,1... | collective-permute-start | bytes 786440 | tf_op jit(solution)/shard_map/ppermute | solution.py:926
  69.1 8.5 %collective-permute-done.9 = bf16[8,32,1152]{2,1,0:T(8,128)(2,1)S(1)} collective-permute-done((bf16[8,32,1152]{2,1,0:T(8,128)(2,1)S(1)}, bf16[8,32,1152]{2,1,0:T(8,128)(2,1)S(1)}, u32[]{:S(2)}, u32[]{:S(2)}) %collective-permute-start.9) | collective-permute-done | bytes 589856 | tf_op jit(solution)/shard_map/ppermute | solution.py:48
  77.8 8.8 %collective-permute-done.10 = bf16[8,32,1280]{2,1,0:T(8,128)(2,1)S(1)} collective-permute-done((bf16[8,32,1280]{2,1,0:T(8,128)(2,1)S(1)}, bf16[8,32,1280]{2,1,0:T(8,128)(2,1)S(1)}, u32[]{:S(2)}, u32[]{:S(2)}) %collective-permute-start.10) | collective-permute-done | bytes 655392 | tf_op jit(solution)/shard_map/ppermute | solution.py:48
  89.1 4.0 %collective-permute-done.14.px = bf16[16,32,1152]{2,1,0:T(8,128)(2,1)S(1)} collective-permute-done((bf16[16,32,1152]{2,1,0:T(8,128)(2,1)S(1)}, bf16[16,32,1152]{2,1,0:T(8,128)(2,1)S(1)}, u32[]{:S(2)}, u32[]{:S(2)}) %collective-permute-start.14) | collective-permute-done | bytes 1179680 | tf_op jit(solution)/shard_map/ppermute | solution.py:48
  95.7 14.6 %first_stage.1 = (bf16[400,1024]{1,0:T(8,128)(2,1)S(1)}, bf16[400,2304]{1,0:T(8,128)(2,1)S(1)}, bf16[384,2304]{1,0:T(8,128)(2,1)S(1)}, bf16[384,256]{1,0:T(8,128...) custom-call(s32[1]{0:T(128)} %bitcast.8.lin_ref, ...), custom_call_target="tpu_custom_call" | custom-call | flops 1 | bytes 1 | tf_op jit(solution)/shard_map/first_stage/pallas_call | solution.py:363
  113.9 3.7 %collective-permute-start.16 = (bf16[144,2048]{1,0:T(8,128)(2,1)}, bf16[144,2048]{1,0:T(8,128)(2,1)}, u32[]{:S(2)}, u32[]{:S(2)}) collective-permute-start(bf16[144,2048]{1,0:T(8,128)(2,1)} %get-tuple-element.198.refs_12_), channel_id=1, source_target_pairs={{0,1},{1,2},{2,3},{3,4},{4,5},{5,6},{6,7},{8,9},{9,10},{10,11},{11... | collective-permute-start | bytes 1769480 | tf_op jit(solution)/shard_map/ppermute | solution.py:966
  126.0 4.9 %pairs_stage.1.refs_3_ = f32[384,2048]{1,0:T(8,128)S(1)} custom-call(bf16[384,256]{1,0:T(8,128)(2,1)S(1)} %get-tuple-element.181.bc_ref.refs_4_.refs_6_, bf16[384,2048]{1,0:T(8,128)(2,1)S(1)} %get-tuple-element.186.dtx_ref.refs_5_, f32[32,384]{1,0:T(8,128)S(1)} %get-tuple-element.187.cumt_ref, f32[384,1]{1,0:T(8,128)S(1)} %get-tuple-element.188.id_col, ...), custom_call_target="tpu_custom_call" | custom-call | flops 1 | bytes 1 | tf_op jit(solution)/shard_map/pairs_stage/pallas_call | solution.py:456
  134.9 9.1 %gate_stage.1 = (bf16[384,2048]{1,0:T(8,128)(2,1)S(1)}, bf16[384,2048]{1,0:T(8,128)(2,1)S(1)}, bf16[384,2048]{1,0:T(8,128)(2,1)S(1)}) custom-call(bf16[400,1024]{1,0:T(8,128)(2,1)S(1)} %copy-done.25, bf16[384,1024]{1,0:T(8,128)(2,1)S(1)} %copy-done.9, bf16[32,2,32,2048]{3,2,1,0:T(8,128)(2,1)} %bitcast.98), custom_call_target="tpu_custom_call" | custom-call | flops 1 | bytes 1 | tf_op jit(solution)/shard_map/gate_stage/pallas_call | solution.py:417
  144.1 7.6 %output_stage.1 = (bf16[128,2048]{1,0:T(8,128)(2,1)S(1)}, bf16[384,2048]{1,0:T(8,128)(2,1)S(1)}, bf16[384,2048]{1,0:T(8,128)(2,1)S(1)}, bf16[384,2048]{1,0:T(8,1...) custom-call(bf16[144,2048]{1,0:T(8,128)(2,1)} %collective-permute-do, ...), custom_call_target="tpu_custom_call" | custom-call | flops 1 | bytes 1 | tf_op jit(solution)/shard_map/output_stage/pallas_call | solution.py:598
  153.2 8.0 %pairs_back_stage.1 = (f32[384,2048]{1,0:T(8,128)S(1)}, f32[384,128]{1,0:T(8,128)S(1)}, f32[384,128]{1,0:T(8,128)S(1)}) custom-call(bf16[384,256]{1,0:T(8,128)(2,1)S(1)} %get-tuple-element.181.bc_ref.refs_4_.refs_6_, bf16[384,2048]{1,0:T(8,128)(2,1)S(1)} %get-tuple-element.186.dtx_ref.refs_5_, bf16[384,2048]{1,0:T(8,128)(2,1)S(1)} %get-tuple-element.217.e_ref.refs_3_, ...), custom_call_target="tpu_custom_call" | custom-call | flops 1 | bytes 1 | tf_op jit(solution)/shard_map/pairs_back_stage/pallas_call | solution.py:504
  162.6 7.4 %weights_stage.1 = (bf16[512,2048]{1,0:T(8,128)(2,1)S(1)}, bf16[512,2048]{1,0:T(8,128)(2,1)}, bf16[1024,1024]{1,0:T(8,128)(2,1)S(1)}, bf16[1024,1024]{1,0:T(8,128)(2,1)}) custom-call(s32[32]{0:T(128)S(1)} %copy-done.63, bf16[1024,400]{1,0:T(8,128)(2,1)S(1)} %copy-done.21, bf16[384,2048]{1,0:T(8,128)(2,1)S(1)} %get-tuple-element.211.gg_ref, ...), custom_call_target="tpu_custom_call" | custom-call | flops 1 | bytes 1 | tf_op jit(solution)/shard_map/weights_stage/pallas_call | solution.py:650
  172.2 8.1 %rest_stage.1 = (bf16[384,1024]{1,0:T(8,128)(2,1)S(1)}, f32[384,1024]{1,0:T(8,128)S(1)}) custom-call(bf16[384,2048]{1,0:T(8,128)(2,1)S(1)} %get-tuple-element.227.no_ref, bf16[384,2048]{1,0:T(8,128)(2,1)S(1)} %get-tuple-element.211.gg_ref, bf16[400,1024]{1,0:T(8,128)(2,1)S(1)} %constant_dynamic-update-slice_fusion.3.tok_ref, bf16[32,2,32,2048]{3,2,1,0:T(8,128)(2,1)} %bitcast.99), custom_call_target="tpu_custom_call" | custom-call | flops 1 | bytes 1 | tf_op jit(solution)/shard_map/rest_stage/pallas_call | solution.py:679
  186.7 4.3 %collective-permute-done.22.refs_1_ = bf16[144,2048]{1,0:T(8,128)(2,1)S(1)} collective-permute-done((bf16[144,2048]{1,0:T(8,128)(2,1)S(1)}, bf16[144,2048]{1,0:T(8,128)(2,1)S(1)}, u32[]{:S(2)}, u32[]{:S(2)}) %collective-permute-start.22) | collective-permute-done | bytes 589856 | tf_op jit(solution)/shard_map/ppermute | solution.py:977
  193.2 5.2 %collective-permute-start.26 = (bf16[128,1024]{1,0:T(8,128)(2,1)S(1)}, bf16[128,1024]{1,0:T(8,128)(2,1)S(1)}, u32[]{:S(2)}, u32[]{:S(2)}) collective-permute-start(bf16[128,1024]{1,0:T(8,128)(2,1)S(1)} %get-tuple-element.372), channel_id=1, source_target_pairs={{0,1},{1,4},{2,7},{3,2},{4,5},{5,0},{6,3},{7,6},{8,9},{9,12},{10,1... | collective-permute-start | bytes 786440 | tf_op jit(solution)/shard_map/ppermute | solution.py:901
  198.4 4.7 %collective-permute-start.27 = (bf16[128,1024]{1,0:T(8,128)(2,1)S(1)}, bf16[128,1024]{1,0:T(8,128)(2,1)S(1)}, u32[]{:S(2)}, u32[]{:S(2)}) collective-permute-start(bf16[128,1024]{1,0:T(8,128)(2,1)S(1)} %get-tuple-element.371), channel_id=1, source_target_pairs={{0,2},{1,5},{2,0},{3,3},{4,6},{5,1},{6,4},{7,7},{8,10},{9,13},{10,... | collective-permute-start | bytes 786440 | tf_op jit(solution)/shard_map/ppermute | solution.py:901
  203.2 8.0 %back_first.1 = (bf16[512,1280]{1,0:T(8,128)(2,1)S(1)}, bf16[512,1280]{1,0:T(8,128)(2,1)S(1)}, bf16[400,1280]{1,0:T(8,128)(2,1)S(1)}, f32[8,1280]{1,0:T(8,128)S(...) custom-call(bf16[144,2048]{1,0:T(8,128)(2,1)S(1)} %collective-permute-done.19.next_ref.refs_0_, ...), custom_call_target="tpu_custom_call" | custom-call | flops 1 | bytes 1 | tf_op jit(solution)/shard_map/back_first/pallas_call | solution.py:816
  211.2 4.3 %collective-permute-done.23 = bf16[8,32,2048]{2,1,0:T(8,128)(2,1)S(1)} collective-permute-done((bf16[8,32,2048]{2,1,0:T(8,128)(2,1)S(1)}, bf16[8,32,2048]{2,1,0:T(8,128)(2,1)S(1)}, u32[]{:S(2)}, u32[]{:S(2)}) %collective-permute-start.23) | collective-permute-done | bytes 1048608 | tf_op jit(solution)/shard_map/ppermute | solution.py:48
  216.0 6.4 %collective-permute-done.24 = bf16[8,64,1024]{2,1,0:T(8,128)(2,1)S(1)} collective-permute-done((bf16[8,64,1024]{2,1,0:T(8,128)(2,1)S(1)}, bf16[8,64,1024]{2,1,0:T(8,128)(2,1)S(1)}, u32[]{:S(2)}, u32[]{:S(2)}) %collective-permute-start.24) | collective-permute-done | bytes 1048608 | tf_op jit(solution)/shard_map/ppermute | solution.py:48
  223.5 7.7 %back_last.1 = (bf16[512,1152]{1,0:T(8,128)(2,1)S(1)}, bf16[512,1152]{1,0:T(8,128)(2,1)S(1)}, bf16[400,1152]{1,0:T(8,128)(2,1)S(1)}, f32[8,1152]{1,0:T(8,128)}, ...) custom-call(bf16[144,2048]{1,0:T(8,128)(2,1)S(1)} %collective-permute-done.19.next_ref.refs_0_, ...), custom_call_target="tpu_custom_call" | custom-call | flops 1 | bytes 1 | tf_op jit(solution)/shard_map/back_last/pallas_call | solution.py:816
  231.2 3.8 %collective-permute-done.29 = bf16[4,64,1024]{2,1,0:T(8,128)(2,1)S(1)} collective-permute-done((bf16[4,64,1024]{2,1,0:T(8,128)(2,1)S(1)}, bf16[4,64,1024]{2,1,0:T(8,128)(2,1)S(1)}, u32[]{:S(2)}, u32[]{:S(2)}) %collective-permute-start.29) | collective-permute-done | bytes 524320 | tf_op jit(solution)/shard_map/ppermute | solution.py:48
  238.8 4.7 %normed_stage.1.normed_ref = f32[400,1024]{1,0:T(8,128)S(1)} custom-call(s32[1]{0:T(128)} %bitcast.8.lin_ref, bf16[400,1152]{1,0:T(8,128)(2,1)S(1)} %get-tuple-element.274.pp_ref, bf16[400,1280]{1,0:T(8,128)(2,1)S(1)} %get-tuple-element.275.pq_ref, f32[384,1024]{1,0:T(8,128)S(1)} %copy-done.27, bf16[16,32,1152]{2,1,0:T(8,128)(2,1)S(1)} %copy-done.5, ...), custom_call_target="tpu_custom_call" | custom-call | flops 1 | bytes 1 | tf_op jit(solution)/shard_map/normed_stage/pallas_call | solution.py:839
  244.8 5.9 %collective-permute-start.37 = (bf16[1,2,32,2048]{3,2,1,0:T(8,128)(2,1)}, bf16[1,2,32,2048]{3,2,1,0:T(8,128)(2,1)}, u32[]{:S(2)}, u32[]{:S(2)}) collective-permute-start(bf16[1,2,32,2048]{3,2,1,0:T(8,128)(2,1)} %get-tuple-element.289), channel_id=1, source_target_pairs={{0,6},{1,7},{2,4},{3,5},{4,2},{5,3},{6,0},{7,1},{8,14},{9,15},{10,... | collective-permute-start | bytes 786440 | tf_op jit(solution)/shard_map/ppermute | solution.py:48
  259.4 13.7 %collective-permute-done.36 = bf16[1,2,32,2048]{3,2,1,0:T(8,128)(2,1)} collective-permute-done((bf16[1,2,32,2048]{3,2,1,0:T(8,128)(2,1)}, bf16[1,2,32,2048]{3,2,1,0:T(8,128)(2,1)}, u32[]{:S(2)}, u32[]{:S(2)}) %collective-permute-start.36) | collective-permute-done | bytes 262176 | tf_op jit(solution)/shard_map/ppermute | solution.py:48
  282.4 3.4 %collective-permute-start.42 = (bf16[128,1024]{1,0:T(8,128)(2,1)S(1)}, bf16[128,1024]{1,0:T(8,128)(2,1)S(1)}, u32[]{:S(2)}, u32[]{:S(2)}) collective-permute-start(bf16[128,1024]{1,0:T(8,128)(2,1)S(1)} %get-tuple-element.296), channel_id=1, source_target_pairs={{0,2},{1,5},{2,0},{3,3},{4,6},{5,1},{6,4},{7,7},{8,10},{9,13},{10,... | collective-permute-start | bytes 786440 | tf_op jit(solution)/shard_map/ppermute | solution.py:901
  286.7 4.7 %collective-permute-done.38 = bf16[4,32,1152]{2,1,0:T(8,128)(2,1)S(1)} collective-permute-done((bf16[4,32,1152]{2,1,0:T(8,128)(2,1)S(1)}, bf16[4,32,1152]{2,1,0:T(8,128)(2,1)S(1)}, u32[]{:S(2)}, u32[]{:S(2)}) %collective-permute-start.38) | collective-permute-done | bytes 294944 | tf_op jit(solution)/shard_map/ppermute | solution.py:48
  291.6 8.8 %collective-permute-start.45 = (bf16[1,32,2432]{2,1,0:T(8,128)(2,1)S(1)}, bf16[1,32,2432]{2,1,0:T(8,128)(2,1)S(1)}, u32[]{:S(2)}, u32[]{:S(2)}) collective-permute-start(bf16[1,32,2432]{2,1,0:T(8,128)(2,1)S(1)} %get-tuple-element.310), channel_id=1, source_target_pairs={{0,6},{1,7},{2,4},{3,5},{4,2},{5,3},{6,0},{7,1},{8,14},{9,15},{10,... | collective-permute-start | bytes 466952 | tf_op jit(solution)/shard_map/ppermute | solution.py:48
  305.3 7.4 %collective-permute-done.44 = bf16[1,32,2432]{2,1,0:T(8,128)(2,1)S(1)} collective-permute-done((bf16[1,32,2432]{2,1,0:T(8,128)(2,1)S(1)}, bf16[1,32,2432]{2,1,0:T(8,128)(2,1)S(1)}, u32[]{:S(2)}, u32[]{:S(2)}) %collective-permute-start.44) | collective-permute-done | bytes 155680 | tf_op jit(solution)/shard_map/ppermute | solution.py:48
  (323 shorter events, 94.3 us)
Async XLA Ops:
  7.2 125.5 %all-gather.2.cloned.1.call-start = ((), (), s32[]{:S(2)}) async-start(), calls=%async_computation | async-start | bytes 8650752 | tf_op jit(solution)/shard_map/all_gather | solution.py:942
  17.7 13.2 %collective-permute-start.1 = (bf16[1,32,2432]{2,1,0:T(8,128)(2,1)S(1)}, bf16[1,32,2432]{2,1,0:T(8,128)(2,1)S(1)}, u32[]{:S(2)}, u32[]{:S(2)}) collective-permute-start(bf16[1,32,2432]{2,1,0:T(8,128)(2,1)S(1)} %bitcast.109), channel_id=1, source_target_pairs={{0,4},{1,5},{2,6},{3,7},{4,0},{5,1},{6,2},{7,3},{8,12},{9,13},{10,... | collective-permute-start | bytes 466952 | tf_op jit(solution)/shard_map/ppermute | solution.py:48
  17.7 13.2 %collective-permute-start = (bf16[1,32,2432]{2,1,0:T(8,128)(2,1)S(1)}, bf16[1,32,2432]{2,1,0:T(8,128)(2,1)S(1)}, u32[]{:S(2)}, u32[]{:S(2)}) collective-permute-start(bf16[1,32,2432]{2,1,0:T(8,128)(2,1)S(1)} %bitcast.110), channel_id=1, source_target_pairs={{0,2},{1,3},{2,0},{3,1},{4,6},{5,7},{6,4},{7,5},{8,10},{9,11},{10,... | collective-permute-start | bytes 466952 | tf_op jit(solution)/shard_map/ppermute | solution.py:48
  36.2 14.4 %collective-permute-start.7 = (bf16[128,1024]{1,0:T(8,128)(2,1)S(1)}, bf16[128,1024]{1,0:T(8,128)(2,1)S(1)}, u32[]{:S(2)}, u32[]{:S(2)}) collective-permute-start(bf16[128,1024]{1,0:T(8,128)(2,1)S(1)} %get-tuple-element.376), channel_id=1, source_target_pairs={{1,0},{4,1},{7,2},{2,3},{5,4},{0,5},{3,6},{6,7},{9,8},{12,9},{15,1... | collective-permute-start | bytes 786440 | tf_op jit(solution)/shard_map/ppermute | solution.py:923
  40.2 19.0 %collective-permute-start.8 = (bf16[128,1024]{1,0:T(8,128)(2,1)S(1)}, bf16[128,1024]{1,0:T(8,128)(2,1)S(1)}, u32[]{:S(2)}, u32[]{:S(2)}) collective-permute-start(bf16[128,1024]{1,0:T(8,128)(2,1)S(1)} %get-tuple-element.374), channel_id=1, source_target_pairs={{2,0},{5,1},{0,2},{3,3},{6,4},{1,5},{4,6},{7,7},{10,8},{13,9},{8,1... | collective-permute-start | bytes 786440 | tf_op jit(solution)/shard_map/ppermute | solution.py:923
  60.0 17.7 %collective-permute-start.9 = (bf16[8,32,1152]{2,1,0:T(8,128)(2,1)S(1)}, bf16[8,32,1152]{2,1,0:T(8,128)(2,1)S(1)}, u32[]{:S(2)}, u32[]{:S(2)}) collective-permute-start(bf16[8,32,1152]{2,1,0:T(8,128)(2,1)S(1)} %pad_maximum_fusion.4), channel_id=1, source_target_pairs={{0,16},{1,17},{2,18},{3,19},{4,20},{5,21},{6,22},{7,23},{8,24},{9,... | collective-permute-start | bytes 1769480 | tf_op jit(solution)/shard_map/ppermute | solution.py:48
  60.7 25.9 %collective-permute-start.10 = (bf16[8,32,1280]{2,1,0:T(8,128)(2,1)S(1)}, bf16[8,32,1280]{2,1,0:T(8,128)(2,1)S(1)}, u32[]{:S(2)}, u32[]{:S(2)}) collective-permute-start(bf16[8,32,1280]{2,1,0:T(8,128)(2,1)S(1)} %pad_maximum_fusion.2), channel_id=1, source_target_pairs={{0,1},{1,0},{2,3},{3,2},{4,5},{5,4},{6,7},{7,6},{8,9},{9,8},{10,11... | collective-permute-start | bytes 1966088 | tf_op jit(solution)/shard_map/ppermute | solution.py:48
  61.5 25.3 %collective-permute-start.11 = (bf16[128,1024]{1,0:T(8,128)(2,1)S(1)}, bf16[128,1024]{1,0:T(8,128)(2,1)S(1)}, u32[]{:S(2)}, u32[]{:S(2)}) collective-permute-start(bf16[128,1024]{1,0:T(8,128)(2,1)S(1)} %get-tuple-element.171), channel_id=1, source_target_pairs={{0,0},{3,1},{6,2},{1,3},{4,4},{7,5},{2,6},{5,7},{8,8},{11,9},{14,1... | collective-permute-start | bytes 786440 | tf_op jit(solution)/shard_map/ppermute | solution.py:926
  62.1 26.2 %collective-permute-start.12 = (bf16[128,1024]{1,0:T(8,128)(2,1)S(1)}, bf16[128,1024]{1,0:T(8,128)(2,1)S(1)}, u32[]{:S(2)}, u32[]{:S(2)}) collective-permute-start(bf16[128,1024]{1,0:T(8,128)(2,1)S(1)} %get-tuple-element.172), channel_id=1, source_target_pairs={{1,0},{4,1},{7,2},{2,3},{5,4},{0,5},{3,6},{6,7},{9,8},{12,9},{15,1... | collective-permute-start | bytes 786440 | tf_op jit(solution)/shard_map/ppermute | solution.py:926
  66.2 22.2 %collective-permute-start.13 = (bf16[128,1024]{1,0:T(8,128)(2,1)S(1)}, bf16[128,1024]{1,0:T(8,128)(2,1)S(1)}, u32[]{:S(2)}, u32[]{:S(2)}) collective-permute-start(bf16[128,1024]{1,0:T(8,128)(2,1)S(1)} %get-tuple-element.173), channel_id=1, source_target_pairs={{2,0},{5,1},{0,2},{3,3},{6,4},{1,5},{4,6},{7,7},{10,8},{13,9},{8,1... | collective-permute-start | bytes 786440 | tf_op jit(solution)/shard_map/ppermute | solution.py:926
  113.9 30.2 %collective-permute-start.16 = (bf16[144,2048]{1,0:T(8,128)(2,1)}, bf16[144,2048]{1,0:T(8,128)(2,1)}, u32[]{:S(2)}, u32[]{:S(2)}) collective-permute-start(bf16[144,2048]{1,0:T(8,128)(2,1)} %get-tuple-element.198.refs_12_), channel_id=1, source_target_pairs={{0,1},{1,2},{2,3},{3,4},{4,5},{5,6},{6,7},{8,9},{9,10},{10,11},{11... | collective-permute-start | bytes 1769480 | tf_op jit(solution)/shard_map/ppermute | solution.py:966
  117.6 26.5 %collective-permute-start.17 = (bf16[144,2048]{1,0:T(8,128)(2,1)}, bf16[144,2048]{1,0:T(8,128)(2,1)}, u32[]{:S(2)}, u32[]{:S(2)}) collective-permute-start(bf16[144,2048]{1,0:T(8,128)(2,1)} %get-tuple-element.198.refs_12_), channel_id=1, source_target_pairs={{0,2},{2,4},{3,5},{5,7},{8,10},{10,12},{11,13},{13,15},{16,18},{18... | collective-permute-start | bytes 1769480 | tf_op jit(solution)/shard_map/ppermute | solution.py:966
  119.7 24.4 %collective-permute-start.18 = (bf16[144,2048]{1,0:T(8,128)(2,1)}, bf16[144,2048]{1,0:T(8,128)(2,1)}, u32[]{:S(2)}, u32[]{:S(2)}) collective-permute-start(bf16[144,2048]{1,0:T(8,128)(2,1)} %get-tuple-element.198.refs_12_), channel_id=1, source_target_pairs={{2,5},{10,13},{18,21},{26,29}} | collective-permute-start | bytes 1769480 | tf_op jit(solution)/shard_map/ppermute | solution.py:966
  151.7 18.3 %collective-permute-start.19 = (bf16[144,2048]{1,0:T(8,128)(2,1)S(1)}, bf16[144,2048]{1,0:T(8,128)(2,1)S(1)}, u32[]{:S(2)}, u32[]{:S(2)}) collective-permute-start(bf16[144,2048]{1,0:T(8,128)(2,1)S(1)} %get-tuple-element.231.own_ref), channel_id=1, source_target_pairs={{1,0},{2,1},{3,2},{4,3},{5,4},{6,5},{7,6},{9,8},{10,9},{11,10},{12... | collective-permute-start | bytes 1769480 | tf_op jit(solution)/shard_map/ppermute | solution.py:977
  170.0 14.1 %collective-permute-start.20 = (bf16[16,32,2048]{2,1,0:T(8,128)(2,1)}, bf16[16,32,2048]{2,1,0:T(8,128)(2,1)}, u32[]{:S(2)}, u32[]{:S(2)}) collective-permute-start(bf16[16,32,2048]{2,1,0:T(8,128)(2,1)} %bitcast.19), channel_id=1, source_target_pairs={{0,8},{1,9},{2,10},{3,11},{4,12},{5,13},{6,14},{7,15},{8,0},{9,1},... | collective-permute-start | bytes 6291464 | tf_op jit(solution)/shard_map/ppermute | solution.py:48
  170.9 20.1 %collective-permute-start.22 = (bf16[144,2048]{1,0:T(8,128)(2,1)S(1)}, bf16[144,2048]{1,0:T(8,128)(2,1)S(1)}, u32[]{:S(2)}, u32[]{:S(2)}) collective-permute-start(bf16[144,2048]{1,0:T(8,128)(2,1)S(1)} %double_stage.1), channel_id=1, source_target_pairs={{2,0},{4,2},{5,3},{7,5},{10,8},{12,10},{13,11},{15,13},{18,16},{20... | collective-permute-start | bytes 1769480 | tf_op jit(solution)/shard_map/ppermute | solution.py:977
  191.0 24.6 %collective-permute-start.23 = (bf16[8,32,2048]{2,1,0:T(8,128)(2,1)S(1)}, bf16[8,32,2048]{2,1,0:T(8,128)(2,1)S(1)}, u32[]{:S(2)}, u32[]{:S(2)}) collective-permute-start(bf16[8,32,2048]{2,1,0:T(8,128)(2,1)S(1)} %get-tuple-element.233), channel_id=1, source_target_pairs={{0,16},{1,17},{2,18},{3,19},{4,20},{5,21},{6,22},{7,23},{8,24},{9,... | collective-permute-start | bytes 3145736 | tf_op jit(solution)/shard_map/ppermute | solution.py:48
  192.4 29.9 %collective-permute-start.24 = (bf16[8,64,1024]{2,1,0:T(8,128)(2,1)S(1)}, bf16[8,64,1024]{2,1,0:T(8,128)(2,1)S(1)}, u32[]{:S(2)}, u32[]{:S(2)}) collective-permute-start(bf16[8,64,1024]{2,1,0:T(8,128)(2,1)S(1)} %get-tuple-element.235), channel_id=1, source_target_pairs={{0,1},{1,0},{2,3},{3,2},{4,5},{5,4},{6,7},{7,6},{8,9},{9,8},{10,11... | collective-permute-start | bytes 3145736 | tf_op jit(solution)/shard_map/ppermute | solution.py:48
  192.5 30.3 %collective-permute-start.25 = (bf16[128,1024]{1,0:T(8,128)(2,1)S(1)}, bf16[128,1024]{1,0:T(8,128)(2,1)S(1)}, u32[]{:S(2)}, u32[]{:S(2)}) collective-permute-start(bf16[128,1024]{1,0:T(8,128)(2,1)S(1)} %get-tuple-element.373), channel_id=1, source_target_pairs={{0,0},{1,3},{2,6},{3,1},{4,4},{5,7},{6,2},{7,5},{8,8},{9,11},{10,1... | collective-permute-start | bytes 786440 | tf_op jit(solution)/shard_map/ppermute | solution.py:901
  193.2 29.6 %collective-permute-start.26 = (bf16[128,1024]{1,0:T(8,128)(2,1)S(1)}, bf16[128,1024]{1,0:T(8,128)(2,1)S(1)}, u32[]{:S(2)}, u32[]{:S(2)}) collective-permute-start(bf16[128,1024]{1,0:T(8,128)(2,1)S(1)} %get-tuple-element.372), channel_id=1, source_target_pairs={{0,1},{1,4},{2,7},{3,2},{4,5},{5,0},{6,3},{7,6},{8,9},{9,12},{10,1... | collective-permute-start | bytes 786440 | tf_op jit(solution)/shard_map/ppermute | solution.py:901
  198.4 24.4 %collective-permute-start.27 = (bf16[128,1024]{1,0:T(8,128)(2,1)S(1)}, bf16[128,1024]{1,0:T(8,128)(2,1)S(1)}, u32[]{:S(2)}, u32[]{:S(2)}) collective-permute-start(bf16[128,1024]{1,0:T(8,128)(2,1)S(1)} %get-tuple-element.371), channel_id=1, source_target_pairs={{0,2},{1,5},{2,0},{3,3},{4,6},{5,1},{6,4},{7,7},{8,10},{9,13},{10,... | collective-permute-start | bytes 786440 | tf_op jit(solution)/shard_map/ppermute | solution.py:901
  236.6 14.3 %collective-permute-start.30 = (bf16[16,32,1152]{2,1,0:T(8,128)(2,1)S(1)}, bf16[16,32,1152]{2,1,0:T(8,128)(2,1)S(1)}, u32[]{:S(2)}, u32[]{:S(2)}) collective-permute-start(bf16[16,32,1152]{2,1,0:T(8,128)(2,1)S(1)} %bitcast.97), channel_id=1, source_target_pairs={{0,8},{1,9},{2,10},{3,11},{4,12},{5,13},{6,14},{7,15},{8,0},{9,1},... | collective-permute-start | bytes 3538952 | tf_op jit(solution)/shard_map/ppermute | solution.py:48
  236.6 16.3 %collective-permute-start.31 = (bf16[16,32,1280]{2,1,0:T(8,128)(2,1)S(1)}, bf16[16,32,1280]{2,1,0:T(8,128)(2,1)S(1)}, u32[]{:S(2)}, u32[]{:S(2)}) collective-permute-start(bf16[16,32,1280]{2,1,0:T(8,128)(2,1)S(1)} %bitcast.96), channel_id=1, source_target_pairs={{0,8},{1,9},{2,10},{3,11},{4,12},{5,13},{6,14},{7,15},{8,0},{9,1},... | collective-permute-start | bytes 3932168 | tf_op jit(solution)/shard_map/ppermute | solution.py:48
  244.8 14.6 %collective-permute-start.37 = (bf16[1,2,32,2048]{3,2,1,0:T(8,128)(2,1)}, bf16[1,2,32,2048]{3,2,1,0:T(8,128)(2,1)}, u32[]{:S(2)}, u32[]{:S(2)}) collective-permute-start(bf16[1,2,32,2048]{3,2,1,0:T(8,128)(2,1)} %get-tuple-element.289), channel_id=1, source_target_pairs={{0,6},{1,7},{2,4},{3,5},{4,2},{5,3},{6,0},{7,1},{8,14},{9,15},{10,... | collective-permute-start | bytes 786440 | tf_op jit(solution)/shard_map/ppermute | solution.py:48
  250.8 22.4 %collective-permute-start.36 = (bf16[1,2,32,2048]{3,2,1,0:T(8,128)(2,1)}, bf16[1,2,32,2048]{3,2,1,0:T(8,128)(2,1)}, u32[]{:S(2)}, u32[]{:S(2)}) collective-permute-start(bf16[1,2,32,2048]{3,2,1,0:T(8,128)(2,1)} %get-tuple-element.288), channel_id=1, source_target_pairs={{0,4},{1,5},{2,6},{3,7},{4,0},{5,1},{6,2},{7,3},{8,12},{9,13},{10,... | collective-permute-start | bytes 786440 | tf_op jit(solution)/shard_map/ppermute | solution.py:48
  250.9 22.3 %collective-permute-start.35 = (bf16[1,2,32,2048]{3,2,1,0:T(8,128)(2,1)}, bf16[1,2,32,2048]{3,2,1,0:T(8,128)(2,1)}, u32[]{:S(2)}, u32[]{:S(2)}) collective-permute-start(bf16[1,2,32,2048]{3,2,1,0:T(8,128)(2,1)} %get-tuple-element.287), channel_id=1, source_target_pairs={{0,2},{1,3},{2,0},{3,1},{4,6},{5,7},{6,4},{7,5},{8,10},{9,11},{10,... | collective-permute-start | bytes 786440 | tf_op jit(solution)/shard_map/ppermute | solution.py:48
  254.4 20.9 %collective-permute-start.33 = (bf16[8,32,1152]{2,1,0:T(8,128)(2,1)}, bf16[8,32,1152]{2,1,0:T(8,128)(2,1)}, u32[]{:S(2)}, u32[]{:S(2)}) collective-permute-start(bf16[8,32,1152]{2,1,0:T(8,128)(2,1)} %get-tuple-element.278), channel_id=1, source_target_pairs={{0,16},{1,17},{2,18},{3,19},{4,20},{5,21},{6,22},{7,23},{8,24},{9,... | collective-permute-start | bytes 1769480 | tf_op jit(solution)/shard_map/ppermute | solution.py:48
  255.4 21.3 %collective-permute-start.34 = (bf16[8,32,1280]{2,1,0:T(8,128)(2,1)}, bf16[8,32,1280]{2,1,0:T(8,128)(2,1)S(1)}, u32[]{:S(2)}, u32[]{:S(2)}) collective-permute-start(bf16[8,32,1280]{2,1,0:T(8,128)(2,1)} %get-tuple-element.280), channel_id=1, source_target_pairs={{0,1},{1,0},{2,3},{3,2},{4,5},{5,4},{6,7},{7,6},{8,9},{9,8},{10,11... | collective-permute-start | bytes 1966088 | tf_op jit(solution)/shard_map/ppermute | solution.py:48
  276.9 14.5 %collective-permute-start.39 = (bf16[4,32,1280]{2,1,0:T(8,128)(2,1)S(1)}, bf16[4,32,1280]{2,1,0:T(8,128)(2,1)S(1)}, u32[]{:S(2)}, u32[]{:S(2)}) collective-permute-start(bf16[4,32,1280]{2,1,0:T(8,128)(2,1)S(1)} %get-tuple-element.293), channel_id=1, source_target_pairs={{0,16},{1,17},{2,18},{3,19},{4,20},{5,21},{6,22},{7,23},{8,24},{9,... | collective-permute-start | bytes 983048 | tf_op jit(solution)/shard_map/ppermute | solution.py:48
  278.4 13.0 %collective-permute-start.38 = (bf16[4,32,1152]{2,1,0:T(8,128)(2,1)S(1)}, bf16[4,32,1152]{2,1,0:T(8,128)(2,1)S(1)}, u32[]{:S(2)}, u32[]{:S(2)}) collective-permute-start(bf16[4,32,1152]{2,1,0:T(8,128)(2,1)S(1)} %get-tuple-element.291), channel_id=1, source_target_pairs={{0,1},{1,0},{2,3},{3,2},{4,5},{5,4},{6,7},{7,6},{8,9},{9,8},{10,11... | collective-permute-start | bytes 884744 | tf_op jit(solution)/shard_map/ppermute | solution.py:48
  278.4 13.2 %collective-permute-start.40 = (bf16[128,1024]{1,0:T(8,128)(2,1)S(1)}, bf16[128,1024]{1,0:T(8,128)(2,1)S(1)}, u32[]{:S(2)}, u32[]{:S(2)}) collective-permute-start(bf16[128,1024]{1,0:T(8,128)(2,1)S(1)} %get-tuple-element.294), channel_id=1, source_target_pairs={{0,0},{1,3},{2,6},{3,1},{4,4},{5,7},{6,2},{7,5},{8,8},{9,11},{10,1... | collective-permute-start | bytes 786440 | tf_op jit(solution)/shard_map/ppermute | solution.py:901
  291.6 13.7 %collective-permute-start.45 = (bf16[1,32,2432]{2,1,0:T(8,128)(2,1)S(1)}, bf16[1,32,2432]{2,1,0:T(8,128)(2,1)S(1)}, u32[]{:S(2)}, u32[]{:S(2)}) collective-permute-start(bf16[1,32,2432]{2,1,0:T(8,128)(2,1)S(1)} %get-tuple-element.310), channel_id=1, source_target_pairs={{0,6},{1,7},{2,4},{3,5},{4,2},{5,3},{6,0},{7,1},{8,14},{9,15},{10,... | collective-permute-start | bytes 466952 | tf_op jit(solution)/shard_map/ppermute | solution.py:48
  (95 other events, 950.6 us)
Sparse Core Ops, SparseCore 0:
  31.2 94.5 all-gather.1

commit v3 on v2

--- a/solution.py
+++ b/solution.py
@@ -916,19 +916,19 @@
 
     first = spread(w1[None], z)
     halo = lax.ppermute(chosen(tokens, -1)[rows - HALO :], "seq", source(-1))
-    first, halo, tokens, d_out, tables, late = tied(first, halo, tokens, d_out, tables, late)
+    first, halo, tokens, d_out, tables = tied(first, halo, tokens, d_out, tables)
     tab_small = tables[2]
     tab_p, tab_q = (tables[0], tables[1]) if aligned else (jnp.arange(32, dtype=jnp.int32),) * 2
     p, q = first[..., :P_COLS], first[..., P_COLS:]
     got = [lax.ppermute(chosen(tokens, i), "seq", source(i)) for i in range(MB)]
     picked = [chosen(d_out, i) for i in range(MB)]
-    p, q, picked, *got = tied(spread(p, x), spread(q, y), picked, *got)
-    g = [lax.ppermute(picked[i], "seq", source(i)) for i in range(MB)]
+    p, q, picked = tied(spread(p, x), spread(q, y), picked)
     ids = (scene_ids[:, 0] + 8 * jnp.arange(MB, dtype=jnp.int32)[:, None]).reshape(1, -1)
     lines = jnp.concatenate([jnp.pad(ids, ((0, 0), (HALO, 0)), constant_values=-1), jnp.pad(valid_mask[:, 0].reshape(1, -1), ((0, 0), (HALO, 0)))])
     lines = lax.dynamic_slice_in_dim(lines, s_rank * total, total + HALO, axis=1)
     lines = jnp.pad(lines.astype(F32), ((0, 6), (0, -(total + HALO) % 128)))
-    p, q, lines, *g = tied(spread(p, y), spread(q, x), lines, *g)
+    p, q, lines, picked, *got = tied(spread(p, y), spread(q, x), lines, picked, *got)
+    g = [lax.ppermute(picked[i], "seq", source(i)) for i in range(MB)]
     p_other, q_other = permute(p, n_s), permute(q, n_s)
     if aligned:
         small = jnp.concatenate([p[:, :, :128], p_other[:, :, :128]])
@@ -962,7 +962,7 @@
 
     far = max(k for k in range(1, n_s) if spans(k))
     reaches = [1 << b for b in range(far.bit_length())]
-    pay, normed, dtx, cumt = tied(pay, normed, dtx, cumt)
+    pay, normed, dtx, cumt, g = tied(pay, normed, dtx, cumt, g)
     forth = lambda v, k: lax.ppermute(v, "seq", [(d, d + k) for d in spans(k)])
     before = [forth(pay, k) for k in range(1, far + 1)]
     normed_p, normed_q = turn_stage(tab_p, tab_q, normed)
@@ -1024,10 +1024,10 @@
     both = fold(both, z, F32)[0]
     rp, rq = fold_cut(rp, y, x), fold_cut(rq, x, y)
     grad_in = finish_stage(grad_normed, rim, ext_tok, g, gain_in, rows)
-    (rp, rq), grad_in, both = tied((rp, rq), grad_in, both)
+    (rp, rq), grad_in = tied((rp, rq), grad_in)
     grad_in = home(grad_in)
     w1_grad = cut(jnp.concatenate([fold(rp, x), fold(rq, y)], axis=2), z)
-    w1_grad, grad_in, block_out = tied(w1_grad, grad_in, block_out)
+    w1_grad, both, block_out = tied(w1_grad, both, block_out)
     w1_grad = fold(w1_grad, z, F32)[0]
     if aligned:
         small = w1_grad[:8, H:128]

time: 327 us -> 315 us (0.963)
  local copies, waits for them, and re-layouts: 25.9 us -> 18.7 us
  waiting for transfers between devices: 95.2 us -> 91.2 us
    ppermute x3, waiting for transfers between devices: 15.2 us -> 2.02 us  [body(): got = [lax.ppermute(chosen(tokens, i), 'seq', source(i)) for i in range(MB)]]
    unnamed x167 -> x181, local copies, waits for them, and re-layouts: 18.2 us -> 12.5 us
    ppermute x27, starting transfers between devices: 34.7 us -> 29.9 us  [permute(): return lax.ppermute(block, BOTH, [(i, i ^ mask) for i in range(size)])]
    ppermute x3, waiting for transfers between devices: 1.59 us -> 5.94 us  [body(): g = [lax.ppermute(picked[i], 'seq', source(i)) for i in range(MB)]]
  transfers between devices with their start and end apart: 47 -> 47, of which waited for: 16 -> 20; matrix products, arithmetic and copies ran while one was open for 6% -> 6% of each run, Pallas kernels for 24% -> 24%
where the time goes in v3:
time: 315 us; the launch traced here: 311 us
  waiting for transfers between devices  91.2 us (29%)
  Pallas kernels  83 us (26%)
  starting transfers between devices  82.8 us (26%)
  other arithmetic  19.4 us (6%)
  local copies, waits for them, and re-layouts  18.7 us (6%)
  between operations  16.1 us (5%)
    ppermute x27, waiting for transfers between devices, permute(): return lax.ppermute(block, BOTH, [(i, i ^ mask) for i in range(size)])  76.8 us
    ppermute x27, starting transfers between devices, permute(): return lax.ppermute(block, BOTH, [(i, i ^ mask) for i in range(size)])  29.9 us
    ppermute x6, starting transfers between devices, home(): lax.ppermute(part, 'seq', [(d, k) for k, d in source(i)])  21.1 us
    pallas_call x2, Pallas kernels, back_stage(): pl.pallas_call(functools.partial(back_kernel, len(got), total, last, smal...  15.4 us
    pallas_call x1, Pallas kernels, first_stage(): pl.pallas_call(functools.partial(first_kernel, masks_p, masks_q, total),...  14.6 us
    unnamed x181, local copies, waits for them, and re-layouts  12.5 us
    convert_element_type x8, other arithmetic, fold_cut(): made.append(total.astype(BF16))  10.9 us
    ppermute x3, starting transfers between devices, body(): got = [lax.ppermute(chosen(tokens, i), 'seq', source(i)) for i in range(MB)]  9.52 us
  transfers between devices with their start and end apart: 47, of which 20 were waited for; matrix products, arithmetic and copies ran while one was open for 6% of the time, Pallas kernels for 24%

profile of v3, /device:TPU:0, one launch (start us, length us, event | category | flops | bytes accessed | tf_op | source)
XLA Modules:
  0.0 311.2 jit_solution(12225901216498580541)
XLA Ops:
  10.4 5.1 %collective-permute-start.2 = (bf16[1,32,2432]{2,1,0:T(8,128)(2,1)S(1)}, bf16[1,32,2432]{2,1,0:T(8,128)(2,1)S(1)}, u32[]{:S(2)}, u32[]{:S(2)}) collective-permute-start(bf16[1,32,2432]{2,1,0:T(8,128)(2,1)S(1)} %bitcast.108), channel_id=1, source_target_pairs={{0,6},{1,7},{2,4},{3,5},{4,2},{5,3},{6,0},{7,1},{8,14},{9,15},{10,... | collective-permute-start | bytes 466952 | tf_op jit(solution)/shard_map/ppermute | solution.py:48
  20.4 12.2 %collective-permute-done.1 = bf16[1,32,2432]{2,1,0:T(8,128)(2,1)S(1)} collective-permute-done((bf16[1,32,2432]{2,1,0:T(8,128)(2,1)S(1)}, bf16[1,32,2432]{2,1,0:T(8,128)(2,1)S(1)}, u32[]{:S(2)}, u32[]{:S(2)}) %collective-permute-start.1) | collective-permute-done | bytes 155680 | tf_op jit(solution)/shard_map/ppermute | solution.py:48
  40.5 4.8 %collective-permute-done.5 = bf16[4,32,1280]{2,1,0:T(8,128)(2,1)S(1)} collective-permute-done((bf16[4,32,1280]{2,1,0:T(8,128)(2,1)S(1)}, bf16[4,32,1280]{2,1,0:T(8,128)(2,1)S(1)}, u32[]{:S(2)}, u32[]{:S(2)}) %collective-permute-start.5) | collective-permute-done | bytes 327712 | tf_op jit(solution)/shard_map/ppermute | solution.py:48
  49.0 6.9 %collective-permute-start.9 = (bf16[128,1024]{1,0:T(8,128)(2,1)S(1)}, bf16[128,1024]{1,0:T(8,128)(2,1)S(1)}, u32[]{:S(2)}, u32[]{:S(2)}) collective-permute-start(bf16[128,1024]{1,0:T(8,128)(2,1)S(1)} %get-tuple-element.374), channel_id=1, source_target_pairs={{1,0},{4,1},{7,2},{2,3},{5,4},{0,5},{3,6},{6,7},{9,8},{12,9},{15,1... | collective-permute-start | bytes 786440 | tf_op jit(solution)/shard_map/ppermute | solution.py:923
  59.6 9.0 %collective-permute-done.7 = bf16[8,32,1280]{2,1,0:T(8,128)(2,1)S(1)} collective-permute-done((bf16[8,32,1280]{2,1,0:T(8,128)(2,1)S(1)}, bf16[8,32,1280]{2,1,0:T(8,128)(2,1)S(1)}, u32[]{:S(2)}, u32[]{:S(2)}) %collective-permute-start.7) | collective-permute-done | bytes 655392 | tf_op jit(solution)/shard_map/ppermute | solution.py:48
  72.0 3.9 %collective-permute-start.14 = (bf16[128,1024]{1,0:T(8,128)(2,1)S(1)}, bf16[128,1024]{1,0:T(8,128)(2,1)S(1)}, u32[]{:S(2)}, u32[]{:S(2)}) collective-permute-start(bf16[128,1024]{1,0:T(8,128)(2,1)S(1)} %copy-done.74), channel_id=1, source_target_pairs={{1,0},{4,1},{7,2},{2,3},{5,4},{0,5},{3,6},{6,7},{9,8},{12,9},{15,1... | collective-permute-start | bytes 786440 | tf_op jit(solution)/shard_map/ppermute | solution.py:931
  81.0 14.6 %first_stage.1 = (bf16[400,1024]{1,0:T(8,128)(2,1)S(1)}, bf16[400,2304]{1,0:T(8,128)(2,1)S(1)}, bf16[384,2304]{1,0:T(8,128)(2,1)S(1)}, bf16[384,256]{1,0:T(8,128...) custom-call(s32[1]{0:T(128)} %bitcast.8.lin_ref, ...), custom_call_target="tpu_custom_call" | custom-call | flops 1 | bytes 1 | tf_op jit(solution)/shard_map/first_stage/pallas_call | solution.py:363
  96.6 5.9 %collective-permute-done.15 = bf16[128,1024]{1,0:T(8,128)(2,1)S(1)} collective-permute-done((bf16[128,1024]{1,0:T(8,128)(2,1)S(1)}, bf16[128,1024]{1,0:T(8,128)(2,1)S(1)}, u32[]{:S(2)}, u32[]{:S(2)}) %collective-permute-start.15) | collective-permute-done | bytes 262176 | tf_op jit(solution)/shard_map/ppermute | solution.py:931
  102.6 5.0 %collective-permute-start.16 = (bf16[144,2048]{1,0:T(8,128)(2,1)}, bf16[144,2048]{1,0:T(8,128)(2,1)}, u32[]{:S(2)}, u32[]{:S(2)}) collective-permute-start(bf16[144,2048]{1,0:T(8,128)(2,1)} %get-tuple-element.199.refs_12_), channel_id=1, source_target_pairs={{0,1},{1,2},{2,3},{3,4},{4,5},{5,6},{6,7},{8,9},{9,10},{10,11},{11... | collective-permute-start | bytes 1769480 | tf_op jit(solution)/shard_map/ppermute | solution.py:966
  114.0 4.9 %pairs_stage.1.refs_3_ = f32[384,2048]{1,0:T(8,128)S(1)} custom-call(bf16[384,256]{1,0:T(8,128)(2,1)S(1)} %get-tuple-element.180.bc_ref.refs_4_.refs_6_, bf16[384,2048]{1,0:T(8,128)(2,1)S(1)} %get-tuple-element.188.dtx_ref.refs_5_, f32[32,384]{1,0:T(8,128)S(1)} %get-tuple-element.189.cumt_ref, f32[384,1]{1,0:T(8,128)S(1)} %get-tuple-element.190.id_col, ...), custom_call_target="tpu_custom_call" | custom-call | flops 1 | bytes 1 | tf_op jit(solution)/shard_map/pairs_stage/pallas_call | solution.py:456
  124.6 9.1 %gate_stage.1 = (bf16[384,2048]{1,0:T(8,128)(2,1)S(1)}, bf16[384,2048]{1,0:T(8,128)(2,1)S(1)}, bf16[384,2048]{1,0:T(8,128)(2,1)S(1)}) custom-call(bf16[400,1024]{1,0:T(8,128)(2,1)S(1)} %copy-done.25, bf16[384,1024]{1,0:T(8,128)(2,1)S(1)} %copy-done.9, bf16[32,2,32,2048]{3,2,1,0:T(8,128)(2,1)} %bitcast.98), custom_call_target="tpu_custom_call" | custom-call | flops 1 | bytes 1 | tf_op jit(solution)/shard_map/gate_stage/pallas_call | solution.py:417
  133.7 7.2 %output_stage.1 = (bf16[128,2048]{1,0:T(8,128)(2,1)S(1)}, bf16[384,2048]{1,0:T(8,128)(2,1)S(1)}, bf16[384,2048]{1,0:T(8,128)(2,1)S(1)}, bf16[384,2048]{1,0:T(8,1...) custom-call(bf16[144,2048]{1,0:T(8,128)(2,1)} %collective-permute-do, ...), custom_call_target="tpu_custom_call" | custom-call | flops 1 | bytes 1 | tf_op jit(solution)/shard_map/output_stage/pallas_call | solution.py:598
  142.5 7.9 %pairs_back_stage.1 = (f32[384,2048]{1,0:T(8,128)S(1)}, f32[384,128]{1,0:T(8,128)S(1)}, f32[384,128]{1,0:T(8,128)S(1)}) custom-call(bf16[384,256]{1,0:T(8,128)(2,1)S(1)} %get-tuple-element.180.bc_ref.refs_4_.refs_6_, bf16[384,2048]{1,0:T(8,128)(2,1)S(1)} %get-tuple-element.188.dtx_ref.refs_5_, bf16[384,2048]{1,0:T(8,128)(2,1)S(1)} %get-tuple-element.218.e_ref.refs_3_, ...), custom_call_target="tpu_custom_call" | custom-call | flops 1 | bytes 1 | tf_op jit(solution)/shard_map/pairs_back_stage/pallas_call | solution.py:504
  151.9 7.4 %weights_stage.1 = (bf16[512,2048]{1,0:T(8,128)(2,1)S(1)}, bf16[512,2048]{1,0:T(8,128)(2,1)}, bf16[1024,1024]{1,0:T(8,128)(2,1)S(1)}, bf16[1024,1024]{1,0:T(8,128)(2,1)}) custom-call(s32[32]{0:T(128)S(1)} %copy-done.60, bf16[1024,400]{1,0:T(8,128)(2,1)S(1)} %copy-done.21, bf16[384,2048]{1,0:T(8,128)(2,1)S(1)} %get-tuple-element.212.gg_ref, ...), custom_call_target="tpu_custom_call" | custom-call | flops 1 | bytes 1 | tf_op jit(solution)/shard_map/weights_stage/pallas_call | solution.py:650
  161.5 8.0 %rest_stage.1 = (bf16[384,1024]{1,0:T(8,128)(2,1)S(1)}, f32[384,1024]{1,0:T(8,128)S(1)}) custom-call(bf16[384,2048]{1,0:T(8,128)(2,1)S(1)} %get-tuple-element.228.no_ref, bf16[384,2048]{1,0:T(8,128)(2,1)S(1)} %get-tuple-element.212.gg_ref, bf16[400,1024]{1,0:T(8,128)(2,1)S(1)} %constant_dynamic-update-slice_fusion.3.tok_ref, bf16[32,2,32,2048]{3,2,1,0:T(8,128)(2,1)} %bitcast.99), custom_call_target="tpu_custom_call" | custom-call | flops 1 | bytes 1 | tf_op jit(solution)/shard_map/rest_stage/pallas_call | solution.py:679
  176.0 4.4 %collective-permute-done.22.refs_1_ = bf16[144,2048]{1,0:T(8,128)(2,1)S(1)} collective-permute-done((bf16[144,2048]{1,0:T(8,128)(2,1)S(1)}, bf16[144,2048]{1,0:T(8,128)(2,1)S(1)}, u32[]{:S(2)}, u32[]{:S(2)}) %collective-permute-start.22) | collective-permute-done | bytes 589856 | tf_op jit(solution)/shard_map/ppermute | solution.py:977
  181.2 4.9 %collective-permute-start.26 = (bf16[128,1024]{1,0:T(8,128)(2,1)S(1)}, bf16[128,1024]{1,0:T(8,128)(2,1)S(1)}, u32[]{:S(2)}, u32[]{:S(2)}) collective-permute-start(bf16[128,1024]{1,0:T(8,128)(2,1)S(1)} %get-tuple-element.370), channel_id=1, source_target_pairs={{0,1},{1,4},{2,7},{3,2},{4,5},{5,0},{6,3},{7,6},{8,9},{9,12},{10,1... | collective-permute-start | bytes 786440 | tf_op jit(solution)/shard_map/ppermute | solution.py:901
  186.2 4.6 %collective-permute-start.27 = (bf16[128,1024]{1,0:T(8,128)(2,1)S(1)}, bf16[128,1024]{1,0:T(8,128)(2,1)S(1)}, u32[]{:S(2)}, u32[]{:S(2)}) collective-permute-start(bf16[128,1024]{1,0:T(8,128)(2,1)S(1)} %get-tuple-element.369), channel_id=1, source_target_pairs={{0,2},{1,5},{2,0},{3,3},{4,6},{5,1},{6,4},{7,7},{8,10},{9,13},{10,... | collective-permute-start | bytes 786440 | tf_op jit(solution)/shard_map/ppermute | solution.py:901
  190.9 7.8 %back_first.1 = (bf16[512,1280]{1,0:T(8,128)(2,1)S(1)}, bf16[512,1280]{1,0:T(8,128)(2,1)S(1)}, bf16[400,1280]{1,0:T(8,128)(2,1)S(1)}, f32[8,1280]{1,0:T(8,128)S(...) custom-call(bf16[144,2048]{1,0:T(8,128)(2,1)S(1)} %collective-permute-done.19.next_ref.refs_0_, ...), custom_call_target="tpu_custom_call" | custom-call | flops 1 | bytes 1 | tf_op jit(solution)/shard_map/back_first/pallas_call | solution.py:816
  198.7 6.2 %collective-permute-done.23 = bf16[8,32,2048]{2,1,0:T(8,128)(2,1)S(1)} collective-permute-done((bf16[8,32,2048]{2,1,0:T(8,128)(2,1)S(1)}, bf16[8,32,2048]{2,1,0:T(8,128)(2,1)S(1)}, u32[]{:S(2)}, u32[]{:S(2)}) %collective-permute-start.23) | collective-permute-done | bytes 1048608 | tf_op jit(solution)/shard_map/ppermute | solution.py:48
  205.4 5.2 %collective-permute-done.24 = bf16[8,64,1024]{2,1,0:T(8,128)(2,1)S(1)} collective-permute-done((bf16[8,64,1024]{2,1,0:T(8,128)(2,1)S(1)}, bf16[8,64,1024]{2,1,0:T(8,128)(2,1)S(1)}, u32[]{:S(2)}, u32[]{:S(2)}) %collective-permute-start.24) | collective-permute-done | bytes 1048608 | tf_op jit(solution)/shard_map/ppermute | solution.py:48
  212.9 7.6 %back_last.1 = (bf16[512,1152]{1,0:T(8,128)(2,1)S(1)}, bf16[512,1152]{1,0:T(8,128)(2,1)S(1)}, bf16[400,1152]{1,0:T(8,128)(2,1)S(1)}, f32[8,1152]{1,0:T(8,128)}, ...) custom-call(bf16[144,2048]{1,0:T(8,128)(2,1)S(1)} %collective-permute-done.19.next_ref.refs_0_, ...), custom_call_target="tpu_custom_call" | custom-call | flops 1 | bytes 1 | tf_op jit(solution)/shard_map/back_last/pallas_call | solution.py:816
  220.5 3.0 collective-permute-done.29
  227.6 4.7 %normed_stage.1.normed_ref = f32[400,1024]{1,0:T(8,128)S(1)} custom-call(s32[1]{0:T(128)} %bitcast.8.lin_ref, bf16[400,1152]{1,0:T(8,128)(2,1)S(1)} %get-tuple-element.275.pp_ref, bf16[400,1280]{1,0:T(8,128)(2,1)S(1)} %get-tuple-element.276.pq_ref, f32[384,1024]{1,0:T(8,128)S(1)} %copy-done.27, bf16[16,32,1152]{2,1,0:T(8,128)(2,1)S(1)} %copy-done.5, ...), custom_call_target="tpu_custom_call" | custom-call | flops 1 | bytes 1 | tf_op jit(solution)/shard_map/normed_stage/pallas_call | solution.py:839
  240.5 3.2 %collective-permute-start.39 = (bf16[1,2,32,2048]{3,2,1,0:T(8,128)(2,1)}, bf16[1,2,32,2048]{3,2,1,0:T(8,128)(2,1)S(1)}, u32[]{:S(2)}, u32[]{:S(2)}) collective-permute-start(bf16[1,2,32,2048]{3,2,1,0:T(8,128)(2,1)} %get-tuple-element.294), channel_id=1, source_target_pairs={{0,6},{1,7},{2,4},{3,5},{4,2},{5,3},{6,0},{7,1},{8,14},{9,15},{10,... | collective-permute-start | bytes 786440 | tf_op jit(solution)/shard_map/ppermute | solution.py:48
  246.4 5.4 %collective-permute-done.33 = bf16[8,32,1152]{2,1,0:T(8,128)(2,1)} collective-permute-done((bf16[8,32,1152]{2,1,0:T(8,128)(2,1)}, bf16[8,32,1152]{2,1,0:T(8,128)(2,1)}, u32[]{:S(2)}, u32[]{:S(2)}) %collective-permute-start.33) | collective-permute-done | bytes 589856 | tf_op jit(solution)/shard_map/ppermute | solution.py:48
  255.4 5.3 %collective-permute-start.41 = (bf16[128,1024]{1,0:T(8,128)(2,1)S(1)}, bf16[128,1024]{1,0:T(8,128)(2,1)S(1)}, u32[]{:S(2)}, u32[]{:S(2)}) collective-permute-start(bf16[128,1024]{1,0:T(8,128)(2,1)S(1)} %get-tuple-element.302), channel_id=1, source_target_pairs={{0,1},{1,4},{2,7},{3,2},{4,5},{5,0},{6,3},{7,6},{8,9},{9,12},{10,1... | collective-permute-start | bytes 786440 | tf_op jit(solution)/shard_map/ppermute | solution.py:901
  260.7 4.9 %collective-permute-start.42 = (bf16[128,1024]{1,0:T(8,128)(2,1)S(1)}, bf16[128,1024]{1,0:T(8,128)(2,1)S(1)}, u32[]{:S(2)}, u32[]{:S(2)}) collective-permute-start(bf16[128,1024]{1,0:T(8,128)(2,1)S(1)} %get-tuple-element.303), channel_id=1, source_target_pairs={{0,2},{1,5},{2,0},{3,3},{4,6},{5,1},{6,4},{7,7},{8,10},{9,13},{10,... | collective-permute-start | bytes 786440 | tf_op jit(solution)/shard_map/ppermute | solution.py:901
  265.7 10.7 %collective-permute-done.38 = bf16[1,2,32,2048]{3,2,1,0:T(8,128)(2,1)S(1)} collective-permute-done((bf16[1,2,32,2048]{3,2,1,0:T(8,128)(2,1)}, bf16[1,2,32,2048]{3,2,1,0:T(8,128)(2,1)S(1)}, u32[]{:S(2)}, u32[]{:S(2)}) %collective-permute-start.38) | collective-permute-done | bytes 262176 | tf_op jit(solution)/shard_map/ppermute | solution.py:48
  279.0 7.6 %collective-permute-done.35 = bf16[4,32,1152]{2,1,0:T(8,128)(2,1)S(1)} collective-permute-done((bf16[4,32,1152]{2,1,0:T(8,128)(2,1)S(1)}, bf16[4,32,1152]{2,1,0:T(8,128)(2,1)S(1)}, u32[]{:S(2)}, u32[]{:S(2)}) %collective-permute-start.35) | collective-permute-done | bytes 294944 | tf_op jit(solution)/shard_map/ppermute | solution.py:48
  287.0 4.3 %collective-permute-start.43 = (bf16[1,32,2432]{2,1,0:T(8,128)(2,1)S(1)}, bf16[1,32,2432]{2,1,0:T(8,128)(2,1)S(1)}, u32[]{:S(2)}, u32[]{:S(2)}) collective-permute-start(bf16[1,32,2432]{2,1,0:T(8,128)(2,1)S(1)} %get-tuple-element.306), channel_id=1, source_target_pairs={{0,2},{1,3},{2,0},{3,1},{4,6},{5,7},{6,4},{7,5},{8,10},{9,11},{10,... | collective-permute-start | bytes 466952 | tf_op jit(solution)/shard_map/ppermute | solution.py:48
  295.8 4.1 %collective-permute-done.44 = bf16[1,32,2432]{2,1,0:T(8,128)(2,1)S(1)} collective-permute-done((bf16[1,32,2432]{2,1,0:T(8,128)(2,1)S(1)}, bf16[1,32,2432]{2,1,0:T(8,128)(2,1)S(1)}, u32[]{:S(2)}, u32[]{:S(2)}) %collective-permute-start.44) | collective-permute-done | bytes 155680 | tf_op jit(solution)/shard_map/ppermute | solution.py:48
  (339 shorter events, 89.1 us)
Async XLA Ops:
  7.3 115.0 %all-gather.2.cloned.1.call-start = ((), (), s32[]{:S(2)}) async-start(), calls=%async_computation | async-start | bytes 8650752 | tf_op jit(solution)/shard_map/all_gather | solution.py:942
  15.5 17.1 %collective-permute-start.1 = (bf16[1,32,2432]{2,1,0:T(8,128)(2,1)S(1)}, bf16[1,32,2432]{2,1,0:T(8,128)(2,1)S(1)}, u32[]{:S(2)}, u32[]{:S(2)}) collective-permute-start(bf16[1,32,2432]{2,1,0:T(8,128)(2,1)S(1)} %bitcast.109), channel_id=1, source_target_pairs={{0,4},{1,5},{2,6},{3,7},{4,0},{5,1},{6,2},{7,3},{8,12},{9,13},{10,... | collective-permute-start | bytes 466952 | tf_op jit(solution)/shard_map/ppermute | solution.py:48
  15.5 17.1 %collective-permute-start = (bf16[1,32,2432]{2,1,0:T(8,128)(2,1)S(1)}, bf16[1,32,2432]{2,1,0:T(8,128)(2,1)S(1)}, u32[]{:S(2)}, u32[]{:S(2)}) collective-permute-start(bf16[1,32,2432]{2,1,0:T(8,128)(2,1)S(1)} %bitcast.110), channel_id=1, source_target_pairs={{0,2},{1,3},{2,0},{3,1},{4,6},{5,7},{6,4},{7,5},{8,10},{9,11},{10,... | collective-permute-start | bytes 466952 | tf_op jit(solution)/shard_map/ppermute | solution.py:48
  16.2 16.5 %collective-permute-start.3 = (bf16[16,1024]{1,0:T(8,128)(2,1)S(1)}, bf16[16,1024]{1,0:T(8,128)(2,1)S(1)}, u32[]{:S(2)}, u32[]{:S(2)}) collective-permute-start(bf16[16,1024]{1,0:T(8,128)(2,1)S(1)} %fusion.15), channel_id=1, source_target_pairs={{7,0},{2,1},{5,2},{0,3},{3,4},{6,5},{1,6},{4,7},{15,8},{10,9},{13,... | collective-permute-start | bytes 98312 | tf_op jit(solution)/shard_map/ppermute | solution.py:918
  45.4 14.0 %collective-permute-start.6 = (bf16[8,32,1152]{2,1,0:T(8,128)(2,1)S(1)}, bf16[8,32,1152]{2,1,0:T(8,128)(2,1)S(1)}, u32[]{:S(2)}, u32[]{:S(2)}) collective-permute-start(bf16[8,32,1152]{2,1,0:T(8,128)(2,1)S(1)} %pad_maximum_fusion.4), channel_id=1, source_target_pairs={{0,16},{1,17},{2,18},{3,19},{4,20},{5,21},{6,22},{7,23},{8,24},{9,... | collective-permute-start | bytes 1769480 | tf_op jit(solution)/shard_map/ppermute | solution.py:48
  48.0 20.7 %collective-permute-start.7 = (bf16[8,32,1280]{2,1,0:T(8,128)(2,1)S(1)}, bf16[8,32,1280]{2,1,0:T(8,128)(2,1)S(1)}, u32[]{:S(2)}, u32[]{:S(2)}) collective-permute-start(bf16[8,32,1280]{2,1,0:T(8,128)(2,1)S(1)} %pad_maximum_fusion.2), channel_id=1, source_target_pairs={{0,1},{1,0},{2,3},{3,2},{4,5},{5,4},{6,7},{7,6},{8,9},{9,8},{10,11... | collective-permute-start | bytes 1966088 | tf_op jit(solution)/shard_map/ppermute | solution.py:48
  48.3 20.5 %collective-permute-start.8 = (bf16[128,1024]{1,0:T(8,128)(2,1)S(1)}, bf16[128,1024]{1,0:T(8,128)(2,1)S(1)}, u32[]{:S(2)}, u32[]{:S(2)}) collective-permute-start(bf16[128,1024]{1,0:T(8,128)(2,1)S(1)} %get-tuple-element.373), channel_id=1, source_target_pairs={{0,0},{3,1},{6,2},{1,3},{4,4},{7,5},{2,6},{5,7},{8,8},{11,9},{14,1... | collective-permute-start | bytes 786440 | tf_op jit(solution)/shard_map/ppermute | solution.py:923
  49.0 21.8 %collective-permute-start.9 = (bf16[128,1024]{1,0:T(8,128)(2,1)S(1)}, bf16[128,1024]{1,0:T(8,128)(2,1)S(1)}, u32[]{:S(2)}, u32[]{:S(2)}) collective-permute-start(bf16[128,1024]{1,0:T(8,128)(2,1)S(1)} %get-tuple-element.374), channel_id=1, source_target_pairs={{1,0},{4,1},{7,2},{2,3},{5,4},{0,5},{3,6},{6,7},{9,8},{12,9},{15,1... | collective-permute-start | bytes 786440 | tf_op jit(solution)/shard_map/ppermute | solution.py:923
  55.9 14.9 %collective-permute-start.10 = (bf16[128,1024]{1,0:T(8,128)(2,1)S(1)}, bf16[128,1024]{1,0:T(8,128)(2,1)S(1)}, u32[]{:S(2)}, u32[]{:S(2)}) collective-permute-start(bf16[128,1024]{1,0:T(8,128)(2,1)S(1)} %get-tuple-element.372), channel_id=1, source_target_pairs={{2,0},{5,1},{0,2},{3,3},{6,4},{1,5},{4,6},{7,7},{10,8},{13,9},{8,1... | collective-permute-start | bytes 786440 | tf_op jit(solution)/shard_map/ppermute | solution.py:923
  71.3 25.3 %collective-permute-start.13 = (bf16[128,1024]{1,0:T(8,128)(2,1)S(1)}, bf16[128,1024]{1,0:T(8,128)(2,1)S(1)}, u32[]{:S(2)}, u32[]{:S(2)}) collective-permute-start(bf16[128,1024]{1,0:T(8,128)(2,1)S(1)} %copy-done.75), channel_id=1, source_target_pairs={{0,0},{3,1},{6,2},{1,3},{4,4},{7,5},{2,6},{5,7},{8,8},{11,9},{14,1... | collective-permute-start | bytes 786440 | tf_op jit(solution)/shard_map/ppermute | solution.py:931
  72.0 24.6 %collective-permute-start.14 = (bf16[128,1024]{1,0:T(8,128)(2,1)S(1)}, bf16[128,1024]{1,0:T(8,128)(2,1)S(1)}, u32[]{:S(2)}, u32[]{:S(2)}) collective-permute-start(bf16[128,1024]{1,0:T(8,128)(2,1)S(1)} %copy-done.74), channel_id=1, source_target_pairs={{1,0},{4,1},{7,2},{2,3},{5,4},{0,5},{3,6},{6,7},{9,8},{12,9},{15,1... | collective-permute-start | bytes 786440 | tf_op jit(solution)/shard_map/ppermute | solution.py:931
  75.9 26.7 %collective-permute-start.15 = (bf16[128,1024]{1,0:T(8,128)(2,1)S(1)}, bf16[128,1024]{1,0:T(8,128)(2,1)S(1)}, u32[]{:S(2)}, u32[]{:S(2)}) collective-permute-start(bf16[128,1024]{1,0:T(8,128)(2,1)S(1)} %copy-done.73), channel_id=1, source_target_pairs={{2,0},{5,1},{0,2},{3,3},{6,4},{1,5},{4,6},{7,7},{10,8},{13,9},{8,1... | collective-permute-start | bytes 786440 | tf_op jit(solution)/shard_map/ppermute | solution.py:931
  102.6 31.1 %collective-permute-start.16 = (bf16[144,2048]{1,0:T(8,128)(2,1)}, bf16[144,2048]{1,0:T(8,128)(2,1)}, u32[]{:S(2)}, u32[]{:S(2)}) collective-permute-start(bf16[144,2048]{1,0:T(8,128)(2,1)} %get-tuple-element.199.refs_12_), channel_id=1, source_target_pairs={{0,1},{1,2},{2,3},{3,4},{4,5},{5,6},{6,7},{8,9},{9,10},{10,11},{11... | collective-permute-start | bytes 1769480 | tf_op jit(solution)/shard_map/ppermute | solution.py:966
  107.6 26.1 %collective-permute-start.17 = (bf16[144,2048]{1,0:T(8,128)(2,1)}, bf16[144,2048]{1,0:T(8,128)(2,1)}, u32[]{:S(2)}, u32[]{:S(2)}) collective-permute-start(bf16[144,2048]{1,0:T(8,128)(2,1)} %get-tuple-element.199.refs_12_), channel_id=1, source_target_pairs={{0,2},{2,4},{3,5},{5,7},{8,10},{10,12},{11,13},{13,15},{16,18},{18... | collective-permute-start | bytes 1769480 | tf_op jit(solution)/shard_map/ppermute | solution.py:966
  109.7 23.9 %collective-permute-start.18 = (bf16[144,2048]{1,0:T(8,128)(2,1)}, bf16[144,2048]{1,0:T(8,128)(2,1)}, u32[]{:S(2)}, u32[]{:S(2)}) collective-permute-start(bf16[144,2048]{1,0:T(8,128)(2,1)} %get-tuple-element.199.refs_12_), channel_id=1, source_target_pairs={{2,5},{10,13},{18,21},{26,29}} | collective-permute-start | bytes 1769480 | tf_op jit(solution)/shard_map/ppermute | solution.py:966
  141.0 18.3 %collective-permute-start.19 = (bf16[144,2048]{1,0:T(8,128)(2,1)S(1)}, bf16[144,2048]{1,0:T(8,128)(2,1)S(1)}, u32[]{:S(2)}, u32[]{:S(2)}) collective-permute-start(bf16[144,2048]{1,0:T(8,128)(2,1)S(1)} %get-tuple-element.232.own_ref), channel_id=1, source_target_pairs={{1,0},{2,1},{3,2},{4,3},{5,4},{6,5},{7,6},{9,8},{10,9},{11,10},{12... | collective-permute-start | bytes 1769480 | tf_op jit(solution)/shard_map/ppermute | solution.py:977
  159.3 14.1 %collective-permute-start.20 = (bf16[16,32,2048]{2,1,0:T(8,128)(2,1)}, bf16[16,32,2048]{2,1,0:T(8,128)(2,1)}, u32[]{:S(2)}, u32[]{:S(2)}) collective-permute-start(bf16[16,32,2048]{2,1,0:T(8,128)(2,1)} %bitcast.19), channel_id=1, source_target_pairs={{0,8},{1,9},{2,10},{3,11},{4,12},{5,13},{6,14},{7,15},{8,0},{9,1},... | collective-permute-start | bytes 6291464 | tf_op jit(solution)/shard_map/ppermute | solution.py:48
  160.2 20.2 %collective-permute-start.22 = (bf16[144,2048]{1,0:T(8,128)(2,1)S(1)}, bf16[144,2048]{1,0:T(8,128)(2,1)S(1)}, u32[]{:S(2)}, u32[]{:S(2)}) collective-permute-start(bf16[144,2048]{1,0:T(8,128)(2,1)S(1)} %double_stage.1), channel_id=1, source_target_pairs={{2,0},{4,2},{5,3},{7,5},{10,8},{12,10},{13,11},{15,13},{18,16},{20... | collective-permute-start | bytes 1769480 | tf_op jit(solution)/shard_map/ppermute | solution.py:977
  180.4 24.5 %collective-permute-start.23 = (bf16[8,32,2048]{2,1,0:T(8,128)(2,1)S(1)}, bf16[8,32,2048]{2,1,0:T(8,128)(2,1)S(1)}, u32[]{:S(2)}, u32[]{:S(2)}) collective-permute-start(bf16[8,32,2048]{2,1,0:T(8,128)(2,1)S(1)} %get-tuple-element.234), channel_id=1, source_target_pairs={{0,16},{1,17},{2,18},{3,19},{4,20},{5,21},{6,22},{7,23},{8,24},{9,... | collective-permute-start | bytes 3145736 | tf_op jit(solution)/shard_map/ppermute | solution.py:48
  180.4 30.2 %collective-permute-start.24 = (bf16[8,64,1024]{2,1,0:T(8,128)(2,1)S(1)}, bf16[8,64,1024]{2,1,0:T(8,128)(2,1)S(1)}, u32[]{:S(2)}, u32[]{:S(2)}) collective-permute-start(bf16[8,64,1024]{2,1,0:T(8,128)(2,1)S(1)} %get-tuple-element.236), channel_id=1, source_target_pairs={{0,1},{1,0},{2,3},{3,2},{4,5},{5,4},{6,7},{7,6},{8,9},{9,8},{10,11... | collective-permute-start | bytes 3145736 | tf_op jit(solution)/shard_map/ppermute | solution.py:48
  180.6 30.4 %collective-permute-start.25 = (bf16[128,1024]{1,0:T(8,128)(2,1)S(1)}, bf16[128,1024]{1,0:T(8,128)(2,1)S(1)}, u32[]{:S(2)}, u32[]{:S(2)}) collective-permute-start(bf16[128,1024]{1,0:T(8,128)(2,1)S(1)} %get-tuple-element.371), channel_id=1, source_target_pairs={{0,0},{1,3},{2,6},{3,1},{4,4},{5,7},{6,2},{7,5},{8,8},{9,11},{10,1... | collective-permute-start | bytes 786440 | tf_op jit(solution)/shard_map/ppermute | solution.py:901
  181.2 29.7 %collective-permute-start.26 = (bf16[128,1024]{1,0:T(8,128)(2,1)S(1)}, bf16[128,1024]{1,0:T(8,128)(2,1)S(1)}, u32[]{:S(2)}, u32[]{:S(2)}) collective-permute-start(bf16[128,1024]{1,0:T(8,128)(2,1)S(1)} %get-tuple-element.370), channel_id=1, source_target_pairs={{0,1},{1,4},{2,7},{3,2},{4,5},{5,0},{6,3},{7,6},{8,9},{9,12},{10,1... | collective-permute-start | bytes 786440 | tf_op jit(solution)/shard_map/ppermute | solution.py:901
  186.2 24.8 %collective-permute-start.27 = (bf16[128,1024]{1,0:T(8,128)(2,1)S(1)}, bf16[128,1024]{1,0:T(8,128)(2,1)S(1)}, u32[]{:S(2)}, u32[]{:S(2)}) collective-permute-start(bf16[128,1024]{1,0:T(8,128)(2,1)S(1)} %get-tuple-element.369), channel_id=1, source_target_pairs={{0,2},{1,5},{2,0},{3,3},{4,6},{5,1},{6,4},{7,7},{8,10},{9,13},{10,... | collective-permute-start | bytes 786440 | tf_op jit(solution)/shard_map/ppermute | solution.py:901
  238.5 13.3 %collective-permute-start.33 = (bf16[8,32,1152]{2,1,0:T(8,128)(2,1)}, bf16[8,32,1152]{2,1,0:T(8,128)(2,1)}, u32[]{:S(2)}, u32[]{:S(2)}) collective-permute-start(bf16[8,32,1152]{2,1,0:T(8,128)(2,1)} %get-tuple-element.279), channel_id=1, source_target_pairs={{0,16},{1,17},{2,18},{3,19},{4,20},{5,21},{6,22},{7,23},{8,24},{9,... | collective-permute-start | bytes 1769480 | tf_op jit(solution)/shard_map/ppermute | solution.py:48
  239.6 14.0 %collective-permute-start.34 = (bf16[8,32,1280]{2,1,0:T(8,128)(2,1)}, bf16[8,32,1280]{2,1,0:T(8,128)(2,1)}, u32[]{:S(2)}, u32[]{:S(2)}) collective-permute-start(bf16[8,32,1280]{2,1,0:T(8,128)(2,1)} %get-tuple-element.281), channel_id=1, source_target_pairs={{0,1},{1,0},{2,3},{3,2},{4,5},{5,4},{6,7},{7,6},{8,9},{9,8},{10,11... | collective-permute-start | bytes 1966088 | tf_op jit(solution)/shard_map/ppermute | solution.py:48
  240.5 20.2 %collective-permute-start.39 = (bf16[1,2,32,2048]{3,2,1,0:T(8,128)(2,1)}, bf16[1,2,32,2048]{3,2,1,0:T(8,128)(2,1)S(1)}, u32[]{:S(2)}, u32[]{:S(2)}) collective-permute-start(bf16[1,2,32,2048]{3,2,1,0:T(8,128)(2,1)} %get-tuple-element.294), channel_id=1, source_target_pairs={{0,6},{1,7},{2,4},{3,5},{4,2},{5,3},{6,0},{7,1},{8,14},{9,15},{10,... | collective-permute-start | bytes 786440 | tf_op jit(solution)/shard_map/ppermute | solution.py:48
  243.7 32.7 %collective-permute-start.38 = (bf16[1,2,32,2048]{3,2,1,0:T(8,128)(2,1)}, bf16[1,2,32,2048]{3,2,1,0:T(8,128)(2,1)S(1)}, u32[]{:S(2)}, u32[]{:S(2)}) collective-permute-start(bf16[1,2,32,2048]{3,2,1,0:T(8,128)(2,1)} %get-tuple-element.293), channel_id=1, source_target_pairs={{0,4},{1,5},{2,6},{3,7},{4,0},{5,1},{6,2},{7,3},{8,12},{9,13},{10,... | collective-permute-start | bytes 786440 | tf_op jit(solution)/shard_map/ppermute | solution.py:48
  245.1 31.3 %collective-permute-start.37 = (bf16[1,2,32,2048]{3,2,1,0:T(8,128)(2,1)}, bf16[1,2,32,2048]{3,2,1,0:T(8,128)(2,1)S(1)}, u32[]{:S(2)}, u32[]{:S(2)}) collective-permute-start(bf16[1,2,32,2048]{3,2,1,0:T(8,128)(2,1)} %get-tuple-element.292), channel_id=1, source_target_pairs={{0,2},{1,3},{2,0},{3,1},{4,6},{5,7},{6,4},{7,5},{8,10},{9,11},{10,... | collective-permute-start | bytes 786440 | tf_op jit(solution)/shard_map/ppermute | solution.py:48
  254.7 23.2 %collective-permute-start.40 = (bf16[128,1024]{1,0:T(8,128)(2,1)S(1)}, bf16[128,1024]{1,0:T(8,128)(2,1)S(1)}, u32[]{:S(2)}, u32[]{:S(2)}) collective-permute-start(bf16[128,1024]{1,0:T(8,128)(2,1)S(1)} %get-tuple-element.301), channel_id=1, source_target_pairs={{0,0},{1,3},{2,6},{3,1},{4,4},{5,7},{6,2},{7,5},{8,8},{9,11},{10,1... | collective-permute-start | bytes 786440 | tf_op jit(solution)/shard_map/ppermute | solution.py:901
  255.4 22.5 %collective-permute-start.41 = (bf16[128,1024]{1,0:T(8,128)(2,1)S(1)}, bf16[128,1024]{1,0:T(8,128)(2,1)S(1)}, u32[]{:S(2)}, u32[]{:S(2)}) collective-permute-start(bf16[128,1024]{1,0:T(8,128)(2,1)S(1)} %get-tuple-element.302), channel_id=1, source_target_pairs={{0,1},{1,4},{2,7},{3,2},{4,5},{5,0},{6,3},{7,6},{8,9},{9,12},{10,1... | collective-permute-start | bytes 786440 | tf_op jit(solution)/shard_map/ppermute | solution.py:901
  260.7 17.2 %collective-permute-start.42 = (bf16[128,1024]{1,0:T(8,128)(2,1)S(1)}, bf16[128,1024]{1,0:T(8,128)(2,1)S(1)}, u32[]{:S(2)}, u32[]{:S(2)}) collective-permute-start(bf16[128,1024]{1,0:T(8,128)(2,1)S(1)} %get-tuple-element.303), channel_id=1, source_target_pairs={{0,2},{1,5},{2,0},{3,3},{4,6},{5,1},{6,4},{7,7},{8,10},{9,13},{10,... | collective-permute-start | bytes 786440 | tf_op jit(solution)/shard_map/ppermute | solution.py:901
  287.0 12.9 %collective-permute-start.44 = (bf16[1,32,2432]{2,1,0:T(8,128)(2,1)S(1)}, bf16[1,32,2432]{2,1,0:T(8,128)(2,1)S(1)}, u32[]{:S(2)}, u32[]{:S(2)}) collective-permute-start(bf16[1,32,2432]{2,1,0:T(8,128)(2,1)S(1)} %get-tuple-element.307), channel_id=1, source_target_pairs={{0,4},{1,5},{2,6},{3,7},{4,0},{5,1},{6,2},{7,3},{8,12},{9,13},{10,... | collective-permute-start | bytes 466952 | tf_op jit(solution)/shard_map/ppermute | solution.py:48
  (104 other events, 1025.7 us)
Sparse Core Ops, SparseCore 0:
  11.1 100.6 all-gather.1
